TPU v7x, 768 devices: a whole 4x8x12 slice. The times are simulated.
768 devices in a mesh: ctx: 96 (over x, z, y_lo), tp: 8 (over y_hi, core).
Axes of the slice: x: 4, y: 8 (y_hi: 4, y_lo: 2; y = y_hi * 2 + y_lo), z: 12, core: 2. Of those that a mesh axis runs over, the one named last changes fastest.
Arguments:
- queries: bfloat16 [12288, 4096], P('ctx', 'tp'), may hold values from -6 to 6
- keys: bfloat16 [12288, 4096], P('ctx', 'tp'), may hold values from -6 to 6
- values: bfloat16 [12288, 4096], P('ctx', 'tp'), may hold values from -6 to 6
- state_retention_log: float32 [32, 12288], P('tp', 'ctx'), may hold values from -0.1 to 0, as said below
- boundary: int32 [12288], P('ctx'), may hold values 0 or 1
- gain: float32 [4096], P('tp'), may hold values from 0.25 to 1.75
- w_out: bfloat16 [4096, 6144], P('tp'), may hold values from -0.09375 to 0.09375
Outputs:
- attended: bfloat16 [12288, 6144], P('ctx', 'tp')
Inputs may be any that keep to these rules, and one draw needn't show every extreme that they name: `state_retention_log`: every entry is negative.
All inputs are finite; a program needn't handle non-finite values. No bound on the sum of `boundary` on one device may be relied on, other than what follows from the above.
Results may differ from a plain program's by a relative error of at most 0.0053.
Values sent between devices are 32-bit elements; how exact they have to be, the bound alone decides.
No kernel may reach another device: no remote copies, remote signals or barrier semaphores. Data moves between devices by JAX's collectives and lax.ppermute only.
A program may use at most 128 MiB of HBM per device.

v0:
```python
import math

import jax
import jax.numpy as jnp
from jax import lax
from jax.sharding import PartitionSpec as P

HEAD_DIM = 128


surge_log_factor = math.log(0.6)
highest = lax.Precision.HIGHEST


def prefix(value, axis, join, neutral, backward):
    count, mine = (lax.axis_size(axis), lax.axis_index(axis))
    pieces = jax.tree.map(lambda part: lax.all_gather(part, axis), value)
    if backward:
        pieces = jax.tree.map(lambda part: part[::-1], pieces)
        mine = count - 1 - mine
    subtotal = jax.tree.map(
        lambda part, zero: jnp.full_like(part, 0) + jnp.asarray(zero, part.dtype), value, neutral
    )

    def turn(position, subtotal):
        longer = join(subtotal, jax.tree.map(lambda part: part[position], pieces))
        return jax.tree.map(lambda new, old: jnp.where(position < mine, new, old), longer, subtotal)

    return lax.fori_loop(0, count - 1, turn, subtotal)


def combine_states(earlier, later):
    decay_before_block, state_early = earlier
    factor_late, state_late = later
    return (decay_before_block * factor_late, factor_late[:, None, None] * state_early + state_late)


def body(queries, keys, values, state_retention_log, boundary, gain, w_out):
    events = queries.shape[0]
    local_heads = queries.shape[1] // HEAD_DIM
    query_heads = queries.reshape(events, local_heads, HEAD_DIM)
    key_heads = keys.reshape(events, local_heads, HEAD_DIM)
    value_heads = values.reshape(events, local_heads, HEAD_DIM)
    retained_log_share = (
        state_retention_log + surge_log_factor * boundary.astype(jnp.float32)[None, :]
    )
    local_cum = jnp.cumsum(retained_log_share, axis=1)
    block_end = local_cum[:, -1]
    cum_rows = local_cum.T
    toward_end = jnp.exp(block_end[None, :] - cum_rows)[:, :, None]
    prefix_decay_factor = jnp.exp(cum_rows)[:, :, None]
    key_wide = key_heads.astype(jnp.float32)
    value_wide = value_heads.astype(jnp.float32)
    forward_term = jnp.einsum("bhd,bhe->hde", key_wide * toward_end, value_wide, precision=highest)
    backward_term = jnp.einsum(
        "bhd,bhe->hde", key_wide * prefix_decay_factor, value_wide, precision=highest
    )
    decay = jnp.exp(block_end)
    identity = (
        jnp.ones((local_heads,), jnp.float32),
        jnp.zeros((local_heads, HEAD_DIM, HEAD_DIM), jnp.float32),
    )
    state_fwd = prefix((decay, forward_term), "ctx", combine_states, identity, False)[1]
    state_bwd = prefix((decay, backward_term), "ctx", combine_states, identity, True)[1]
    attention_logits = jnp.einsum(
        "thd,shd->hts", query_heads, key_heads, preferred_element_type=jnp.float32
    )
    weight = jnp.exp(-jnp.abs(local_cum[:, :, None] - local_cum[:, None, :]))
    probs = (attention_logits * weight).astype(jnp.bfloat16)
    intra = jnp.einsum("hts,shd->thd", probs, value_heads, preferred_element_type=jnp.float32)
    query_wide = query_heads.astype(jnp.float32)
    inter = jnp.einsum(
        "thd,hde->the", query_wide * prefix_decay_factor, state_fwd, precision=highest
    )
    inter = inter + jnp.einsum(
        "thd,hde->the", query_wide * toward_end, state_bwd, precision=highest
    )
    total = intra + inter
    squared_average = jnp.mean(total * total, axis=2, keepdims=True)
    gain_heads = gain.reshape(local_heads, HEAD_DIM)
    normed = (total * lax.rsqrt(squared_average + 1e-06) * gain_heads[None, :, :]).astype(
        jnp.bfloat16
    )
    normed = normed.reshape(events, local_heads * HEAD_DIM)
    partial_out = jnp.dot(normed, w_out, preferred_element_type=jnp.float32)
    result = lax.psum_scatter(partial_out, "tp", scatter_dimension=1, tiled=True)
    return result.astype(jnp.bfloat16)


def solution(mesh):
    in_specs = (
        P("ctx", "tp"),
        P("ctx", "tp"),
        P("ctx", "tp"),
        P("tp", "ctx"),
        P("ctx"),
        P("tp"),
        P("tp", None),
    )
    out_specs = P("ctx", "tp")
    return jax.shard_map(body, mesh=mesh, in_specs=in_specs, out_specs=out_specs, check_vma=False)
```

profile of v0, /device:TPU:1, one launch (start us, length us, event | category | flops | bytes accessed | tf_op | source)
XLA Modules:
  0.0 1337.5 jit_solution(10794096833888266784)
XLA Ops:
  8.5 2.2 fusion.5
  10.7 2.2 fusion.6
  13.0 1.4 dynamic-slice
  15.3 213.0 %all-reduce = f32[384]{0:T(512)S(1)} all-reduce(f32[384]{0:T(512)S(1)} %dynamic-update-slice), channel_id=2, replica_groups=mesh['ctx'=96,'tp'=8] {'ctx'}, use_global_device_ids=true, to_apply=%add | all-reduce | flops 384 | bytes 3072
  228.4 1.3 convolution_bitcast_fusion
  229.7 357.6 %all-gather.6.cloned.1.call-done = f32[384,128,128]{2,1,0:T(8,128)} async-done(((f32[4,128,128]{2,1,0:T(8,128)}), f32[384,128,128]{2,1,0:T(8,128)}) %all-gather.6.cloned.1.call-update) | async-done | bytes 25165840 | tf_op jit(solution)/shard_map/all_gather | solution.py:17
  587.4 104.0 %while.28 = (s32[]{:T(128)}, f32[4,128,128]{2,1,0:T(8,128)S(1)}, s32[]{:T(128)}, f32[96,4]{1,0:T(8,128)S(1)}, f32[96,4,128,128]{3,2,1,0:T(8,128)}, /*index=5*/s32[]{:T(128)}, s32[]{:T(128)}) while((s32[]{:T(128)}, f32[4,128,128]{2,1,0:T(8,128)S(1)}, s32[]{:T(128)}, f32[96,4]{1,0:T(8,128)S(1)}, f32[96,4,128,128]{3,2,1,0:T(8,128)}, ...), condition=%wide.region_2.3_spmd.clone, body=%wide.region_1.2_spmd.clone.sunk | while | flops 262148 | bytes 786585 | solution.py:29
  618.0 1.1 fusion.56
  625.7 1.1 fusion.56
  627.9 1.1 fusion.56
  638.8 1.1 fusion.56
  642.1 1.1 fusion.56
  648.7 1.1 fusion.56
  649.8 1.1 fusion.56
  656.4 1.1 fusion.56
  660.8 1.1 fusion.56
  665.1 1.1 fusion.56
  675.0 1.1 fusion.56
  692.1 457.0 %all-gather.8.cloned.1.call-done = f32[384,128,128]{2,1,0:T(8,128)} async-done(((f32[4,128,128]{2,1,0:T(8,128)}), f32[384,128,128]{2,1,0:T(8,128)}) %all-gather.8.cloned.1.call-update) | async-done | bytes 25165840 | tf_op jit(solution)/shard_map/all_gather | solution.py:17
  1149.1 17.3 %rev.7 = f32[96,4,128,128]{3,2,1,0:T(8,128)} reverse(f32[96,4,128,128]{3,2,1,0:T(8,128)} %bitcast.104), dimensions={0} | reverse | bytes 50331648 | tf_op jit(solution)/shard_map/rev | solution.py:19
  1166.3 103.9 %while.29 = (s32[]{:T(128)}, f32[4,128,128]{2,1,0:T(8,128)S(1)}, s32[]{:T(128)}, f32[96,4]{1,0:T(8,128)S(1)}, f32[96,4,128,128]{3,2,1,0:T(8,128)}, /*index=5*/s32[]{:T(128)}, s32[]{:T(128)}) while((s32[]{:T(128)}, f32[4,128,128]{2,1,0:T(8,128)S(1)}, s32[]{:T(128)}, f32[96,4]{1,0:T(8,128)S(1)}, f32[96,4,128,128]{3,2,1,0:T(8,128)}, ...), condition=%wide.region_4.5_spmd.clone, body=%wide.region_3.4_spmd.clone.sunk | while | flops 262148 | bytes 786585 | solution.py:29
  1271.1 5.5 fusion.40
  1276.6 52.6 %reduce-scatter.2.cloned.1.call-done = f32[128,768]{1,0:T(8,128)} async-done(((f32[128,6144]{1,0:T(8,128)}), f32[128,768]{1,0:T(8,128)}) %reduce-scatter.2.cloned.1.call-update) | async-done | bytes 393232 | tf_op jit(solution)/shard_map/reduce_scatter | solution.py:86
  1329.2 1.7 convert_element_type.24
  (394 shorter events, 194.2 us)
Async XLA Ops:
  6.5 221.8 %copy-start = (bf16[128,512]{1,0:T(8,128)(2,1)S(1)}, bf16[128,512]{1,0:T(8,128)(2,1)}, u32[]{:S(2)}) copy-start(bf16[128,512]{1,0:T(8,128)(2,1)} %param.11) | copy-start | bytes 393220
  6.5 580.9 %all-gather.6.cloned.1.call-start = ((), (), s32[]{:S(2)}) async-start(), calls=%async_computation.2 | async-start | bytes 25427968 | tf_op jit(solution)/shard_map/all_gather | solution.py:17
  10.7 1138.4 %all-gather.8.cloned.1.call-start = ((), (), s32[]{:S(2)}) async-start(), calls=%async_computation.3 | async-start | bytes 25427968 | tf_op jit(solution)/shard_map/all_gather | solution.py:17
  12.9 1316.3 %reduce-scatter.2.cloned.1.call-start = ((), (), s32[]{:S(2)}) async-start(), calls=%async_computation.1 | async-start | bytes 3538944 | tf_op jit(solution)/shard_map/reduce_scatter | solution.py:86
  1149.1 121.9 %copy-start.1 = (f32[512]{0:T(512)S(1)}, f32[512]{0:T(512)}, u32[]{:S(2)}) copy-start(f32[512]{0:T(512)} %param.16) | copy-start | bytes 6148
Sparse Core Ops, SparseCore 0:
  10.8 576.5 all-gather.5
  589.8 559.2 all-gather.7
  1276.7 52.4 reduce-scatter.1
where the time goes:
time: 1350 us; the launch traced here: 1340 us
  waiting for transfers between devices  867 us (64%)
  blocking collectives  213 us (16%)
  other arithmetic  204 us (15%)
  local copies, waits for them, and re-layouts  21 us (2%)
  between operations  13.9 us (1%)
    all_gather x2, waiting for transfers between devices, prefix(): pieces = jax.tree.map(lambda part: lax.all_gather(part, axis), value)  815 us
    unnamed x1, blocking collectives  213 us
    select_n x190, other arithmetic, turn(): jnp.where(position < mine, new, old)  200 us
    reduce_scatter x1, waiting for transfers between devices, body(): lax.psum_scatter(partial_out, 'tp', scatter_dimension=1, tiled=True)  52.6 us
  transfers between devices with their start and end apart: 3, of which 3 were waited for; matrix products, arithmetic and copies ran while one was open for 8% of the time, Pallas kernels for 0%

commit v1 on v0

v1 whole, which is shorter than its diff:
```python
import functools
import math

import jax
import jax.numpy as jnp
import numpy as np
from jax import lax
from jax.experimental import pallas as pl
from jax.experimental.pallas import tpu as pltpu
from jax.sharding import PartitionSpec as P

HEAD_DIM = 128
EVENTS = 128
HEADS_DEV = 4
D = 6144
COLS = 768
PAIRS = 48
PIECES = PAIRS // HEADS_DEV
ROWS = 11
CHUNK = ROWS + 1
HEAD_ROWS = PIECES * CHUNK
PACKED = PAIRS * CHUNK
HALF = EVENTS // 2

surge_log_factor = math.log(0.6)
F32 = jnp.float32
BF16 = jnp.bfloat16
VMEM_LIMIT = 24 * 1024 * 1024

SIDE_GROUPS = [[2 * pair + side for pair in range(PAIRS)] for side in range(2)]
SIDE_SWAP = [(i, i ^ 1) for i in range(2 * PAIRS)]
CORE_SWAP = [(i, i ^ 1) for i in range(8)]
RING_UP = [(i, (i + 2) % 8) for i in range(8)]
RING_DOWN = [(i, (i - 2) % 8) for i in range(8)]


def piece_rows(piece):
    return min(ROWS, HEAD_DIM - ROWS * piece)


def call(kernel, outs, args, scalars=0, scratch=(), flops=0, moved=0):
    specs = [pl.BlockSpec(memory_space=pltpu.SMEM)] * scalars
    specs += [pl.BlockSpec(memory_space=pltpu.VMEM)] * (len(args) - scalars)
    return pl.pallas_call(
        kernel,
        out_shape=[jax.ShapeDtypeStruct(shape, dtype) for shape, dtype in outs],
        in_specs=specs,
        out_specs=[pl.BlockSpec(memory_space=pltpu.VMEM)] * len(outs),
        scratch_shapes=list(scratch),
        compiler_params=pltpu.CompilerParams(vmem_limit_bytes=VMEM_LIMIT),
        cost_estimate=pl.CostEstimate(flops=flops, bytes_accessed=moved, transcendentals=0),
    )(*args)


def event_sums(log_ref, boundary_ref):
    rate = log_ref[...] + surge_log_factor * boundary_ref[...].astype(F32)
    row = lax.broadcasted_iota(jnp.int32, (EVENTS, EVENTS), 0)
    column = lax.broadcasted_iota(jnp.int32, (EVENTS, EVENTS), 1)
    lower = (column <= row).astype(F32)
    upper = (row <= column).astype(F32)
    columns = lax.dot_general(
        lower, rate, (((1,), (1,)), ((), ())), precision=lax.Precision.HIGHEST, preferred_element_type=F32
    )
    return rate, columns, upper


def factors(side, columns):
    ends = columns[EVENTS - 1 : EVENTS, :]
    toward_end = jnp.exp(ends - columns)
    from_start = jnp.exp(columns)
    sent = jnp.where(side == 0, toward_end, from_start)
    kept = jnp.where(side == 0, from_start, toward_end)
    return ends, sent, kept


def halves(wide):
    high = wide.astype(BF16)
    low = (wide - high.astype(F32)).astype(BF16)
    return high, low


def terms_kernel(side_ref, key_ref, value_ref, log_ref, boundary_ref, sent_ref, kept_ref, decay_ref):
    _, columns, _ = event_sums(log_ref, boundary_ref)
    ends, sent, kept = factors(side_ref[0], columns)
    decay = jnp.exp(ends)
    sent_ref[...] = jnp.zeros_like(sent_ref)
    kept_ref[...] = jnp.zeros_like(kept_ref)
    for head in range(HEADS_DEV):
        lanes = slice(head * HEAD_DIM, (head + 1) * HEAD_DIM)
        value = value_ref[:, lanes].astype(F32)
        sides = halves(value * sent[:, head : head + 1]) + halves(value * kept[:, head : head + 1])
        product = lax.dot_general(
            key_ref[:, lanes],
            jnp.concatenate(sides, axis=1),
            (((0,), (0,)), ((), ())),
            preferred_element_type=F32,
        )
        sent_term = product[:, :128] + product[:, 128:256]
        kept_term = product[:, 256:384] + product[:, 384:]
        whole_row = jnp.broadcast_to(decay[:, head : head + 1], (1, HEAD_DIM))
        decay_ref[head : head + 1, :] = whole_row
        for piece in range(PIECES):
            count, first = piece_rows(piece), head * HEAD_ROWS + piece * CHUNK
            rows = slice(ROWS * piece, ROWS * piece + count)
            sent_ref[first : first + count, :] = sent_term[rows]
            kept_ref[first : first + count, :] = kept_term[rows]
            sent_ref[first + ROWS : first + CHUNK, :] = whole_row


def combine_kernel(kept_ref, got_ref, decay_ref, out_ref):
    for head in range(HEADS_DEV):
        rows = slice(head * HEAD_ROWS, (head + 1) * HEAD_ROWS)
        out_ref[rows, :] = kept_ref[rows, :] + decay_ref[head : head + 1, :] * got_ref[rows, :]


def scan_kernel(side_ref, term_ref, out_ref):
    def run(pairs):
        state = jnp.zeros((CHUNK, HEAD_DIM), F32)
        for pair in pairs:
            rows = slice(pair * CHUNK, (pair + 1) * CHUNK)
            out_ref[rows, :] = state
            term = term_ref[rows, :]
            state = term[ROWS:, :] * state + term

    @pl.when(side_ref[0] == 1)
    def _():
        run(range(PAIRS))

    @pl.when(side_ref[0] == 0)
    def _():
        run(range(PAIRS - 1, -1, -1))


def unpack(packed_ref, head):
    parts = []
    for piece in range(PIECES):
        first = head * HEAD_ROWS + piece * CHUNK
        parts.append(packed_ref[first : first + piece_rows(piece), :])
    return jnp.concatenate(parts, axis=0)


def times_state(query, state):
    product = jnp.dot(query, jnp.concatenate(halves(state), axis=1), preferred_element_type=F32)
    return product[:, :128] + product[:, 128:]


def inner_kernel(
    side_ref, query_ref, key_ref, value_ref, log_ref, boundary_ref, got_ref, own_ref, total_ref, factor_ref
):
    rate, columns, upper = event_sums(log_ref, boundary_ref)
    rows_cum = lax.dot_general(
        rate, upper, (((1,), (0,)), ((), ())), precision=lax.Precision.HIGHEST, preferred_element_type=F32
    )
    _, own, other = factors(side_ref[0], columns)
    for head in range(HEADS_DEV):
        lanes = slice(head * HEAD_DIM, (head + 1) * HEAD_DIM)
        query = query_ref[:, lanes]
        logits = lax.dot_general(
            query, key_ref[:, lanes], (((1,), (1,)), ((), ())), preferred_element_type=F32
        )
        weight = jnp.exp(-jnp.abs(columns[:, head : head + 1] - rows_cum[head : head + 1, :]))
        probs = (logits * weight).astype(BF16)
        intra = jnp.dot(probs, value_ref[:, lanes], preferred_element_type=F32)
        last = head * HEAD_ROWS + ROWS
        state = unpack(got_ref, head) + got_ref[last : last + 1, :] * unpack(own_ref, head)
        total_ref[:, lanes] = intra + own[:, head : head + 1] * times_state(query, state)
        factor_ref[:, lanes] = jnp.broadcast_to(other[:, head : head + 1], (EVENTS, HEAD_DIM))


def first_kernel(
    order_ref, query_ref, total_ref, factor_ref, other_ref, gain_ref, w_ref, normed_ref, send_ref, mine_ref
):
    step = pl.program_id(0)

    @pl.when(step == 0)
    def _():
        for head in range(HEADS_DEV):
            lanes = slice(head * HEAD_DIM, (head + 1) * HEAD_DIM)
            total = total_ref[:, lanes] + factor_ref[:, lanes] * times_state(
                query_ref[:, lanes], unpack(other_ref, head)
            )
            average = jnp.mean(total * total, axis=1, keepdims=True)
            scaled = total * lax.rsqrt(average + 1e-06) * gain_ref[:, lanes]
            normed_ref[:, lanes] = scaled.astype(BF16)
        send_ref[...] = jnp.dot(normed_ref[...], w_ref[...], preferred_element_type=F32)

    @pl.when(step == 1)
    def _():
        mine_ref[...] = jnp.dot(normed_ref[...], w_ref[...], preferred_element_type=F32)


def rest_kernel(order_ref, normed_ref, w_ref, send_ref, mine_ref):
    step = pl.program_id(0)
    product = jnp.dot(normed_ref[...], w_ref[...], preferred_element_type=F32)

    @pl.when(step < 3)
    def _():
        send_ref[0] = product

    @pl.when(step >= 3)
    def _():
        mine_ref[0] = product


def whole(shape):
    return pl.BlockSpec(shape, lambda step, order: (0,) * len(shape))


def project_first(order, query, total, factor, other, gain, w_out):
    spec = pltpu.PrefetchScalarGridSpec(
        num_scalar_prefetch=1,
        grid=(2,),
        in_specs=[
            whole(query.shape),
            whole(total.shape),
            whole(factor.shape),
            whole(other.shape),
            whole(gain.shape),
            pl.BlockSpec((w_out.shape[0], COLS), lambda step, order: (0, order[step])),
        ],
        out_specs=[whole((EVENTS, 512)), whole((EVENTS, COLS)), whole((EVENTS, COLS))],
    )
    return pl.pallas_call(
        first_kernel,
        grid_spec=spec,
        out_shape=[
            jax.ShapeDtypeStruct((EVENTS, 512), BF16),
            jax.ShapeDtypeStruct((EVENTS, COLS), F32),
            jax.ShapeDtypeStruct((EVENTS, COLS), F32),
        ],
        compiler_params=pltpu.CompilerParams(vmem_limit_bytes=VMEM_LIMIT),
        cost_estimate=pl.CostEstimate(flops=230_000_000, bytes_accessed=3_500_000, transcendentals=0),
    )(order, query, total, factor, other, gain, w_out)


def project_rest(order, normed, w_out):
    spec = pltpu.PrefetchScalarGridSpec(
        num_scalar_prefetch=1,
        grid=(6,),
        in_specs=[
            whole(normed.shape),
            pl.BlockSpec((w_out.shape[0], COLS), lambda step, order: (0, order[step])),
        ],
        out_specs=[
            pl.BlockSpec((1, EVENTS, COLS), lambda step, order: (jnp.minimum(step, 2), 0, 0)),
            pl.BlockSpec((1, EVENTS, COLS), lambda step, order: (jnp.maximum(step - 3, 0), 0, 0)),
        ],
    )
    return pl.pallas_call(
        rest_kernel,
        grid_spec=spec,
        out_shape=[
            jax.ShapeDtypeStruct((3, EVENTS, COLS), F32),
            jax.ShapeDtypeStruct((3, EVENTS, COLS), F32),
        ],
        compiler_params=pltpu.CompilerParams(vmem_limit_bytes=VMEM_LIMIT),
        cost_estimate=pl.CostEstimate(flops=604_000_000, bytes_accessed=7_500_000, transcendentals=0),
    )(order, normed, w_out)


def far_kernel(mine_ref, got_ref, top_ref, bottom_ref):
    top_ref[...] = mine_ref[:HALF] + got_ref[:HALF]
    bottom_ref[...] = mine_ref[HALF:] + got_ref[HALF:]


def near_kernel(mine_ref, got_ref, up_bottom_ref, down_top_ref, up_top_ref, down_bottom_ref, own_ref):
    up_bottom_ref[...] = mine_ref[0, HALF:] + got_ref[0, HALF:]
    down_top_ref[...] = mine_ref[1, :HALF] + got_ref[1, :HALF]
    up_top_ref[...] = mine_ref[0, :HALF] + got_ref[0, :HALF]
    down_bottom_ref[...] = mine_ref[1, HALF:] + got_ref[1, HALF:]
    own_ref[...] = mine_ref[2] + got_ref[2]


def relay_kernel(up_top_ref, from_below_ref, down_bottom_ref, from_above_ref, up_ref, down_ref):
    up_ref[...] = up_top_ref[...] + from_below_ref[...]
    down_ref[...] = down_bottom_ref[...] + from_above_ref[...]


def final_kernel(own_ref, top_a_ref, top_b_ref, bottom_a_ref, bottom_b_ref, out_ref):
    out_ref[:HALF] = (own_ref[:HALF] + (top_a_ref[...] + top_b_ref[...])).astype(BF16)
    out_ref[HALF:] = (own_ref[HALF:] + (bottom_a_ref[...] + bottom_b_ref[...])).astype(BF16)


def exchange_pieces(packed):
    pieces = packed.reshape(PAIRS, 3, 4, HEAD_DIM)
    pieces = lax.all_to_all(pieces, "ctx", 0, 0, axis_index_groups=SIDE_GROUPS)
    return pieces.reshape(PACKED, HEAD_DIM)


def body(queries, keys, values, state_retention_log, boundary, gain, w_out):
    side = (lax.axis_index("ctx") % 2).reshape(1)
    place = lax.axis_index("tp")
    ring, core = place // 2, place % 2
    blocks = [2 * ((ring + far) % 4) + c for far, c in ((2, 1 - core), (2, core))]
    first_order = jnp.stack(blocks).astype(jnp.int32)
    blocks = [2 * ((ring + far) % 4) + c for c in (1 - core, core) for far in (1, 3, 0)]
    rest_order = jnp.stack(blocks).astype(jnp.int32)
    boundary = boundary.reshape(1, EVENTS)
    gain = gain.reshape(1, 512)
    packed = ((PACKED, HEAD_DIM), F32)

    sent, kept, decay = call(
        terms_kernel,
        [packed, packed, ((HEADS_DEV, HEAD_DIM), F32)],
        (side, keys, values, state_retention_log, boundary),
        scalars=1,
        flops=70_000_000,
        moved=900_000,
    )
    got = lax.ppermute(sent, "ctx", SIDE_SWAP)
    (pair_terms,) = call(combine_kernel, [packed], (kept, got, decay), flops=200_000, moved=900_000)
    slices = exchange_pieces(pair_terms)
    (states,) = call(scan_kernel, [packed], (side, slices), scalars=1, flops=200_000, moved=600_000)
    own = exchange_pieces(states)
    other = lax.ppermute(own, "ctx", SIDE_SWAP)
    inner = ((EVENTS, 512), F32)
    total, factor = call(
        inner_kernel,
        [inner, inner],
        (side, queries, keys, values, state_retention_log, boundary, got, own),
        scalars=1,
        flops=100_000_000,
        moved=1_500_000,
    )
    normed, send, mine = project_first(first_order, queries, total, factor, other, gain, w_out)
    far_got = lax.ppermute(send, "tp", CORE_SWAP)
    near_send, near_mine = project_rest(rest_order, normed, w_out)
    half = ((HALF, COLS), F32)
    far_top, far_bottom = call(far_kernel, [half, half], (mine, far_got), moved=1_200_000)
    from_below = lax.ppermute(far_top, "tp", RING_UP)
    from_above = lax.ppermute(far_bottom, "tp", RING_DOWN)
    near_got = lax.ppermute(near_send, "tp", CORE_SWAP)
    up_bottom, down_top, up_top, down_bottom, own_sum = call(
        near_kernel, [half] * 4 + [((EVENTS, COLS), F32)], (near_mine, near_got), moved=3_600_000
    )
    bottom_a = lax.ppermute(up_bottom, "tp", RING_UP)
    top_a = lax.ppermute(down_top, "tp", RING_DOWN)
    up, down = call(
        relay_kernel, [half, half], (up_top, from_below, down_bottom, from_above), moved=1_200_000
    )
    top_b = lax.ppermute(up, "tp", RING_UP)
    bottom_b = lax.ppermute(down, "tp", RING_DOWN)
    (out,) = call(
        final_kernel,
        [((EVENTS, COLS), BF16)],
        (own_sum, top_a, top_b, bottom_a, bottom_b),
        moved=1_400_000,
    )
    return out


def solution(mesh):
    in_specs = (
        P("ctx", "tp"),
        P("ctx", "tp"),
        P("ctx", "tp"),
        P("tp", "ctx"),
        P("ctx"),
        P("tp"),
        P("tp", None),
    )
    out_specs = P("ctx", "tp")
    return jax.shard_map(body, mesh=mesh, in_specs=in_specs, out_specs=out_specs, check_vma=False)
```

time: 1350 us -> 143 us (0.11)
  the two profiles are of different devices: /device:TPU:1 before, /device:TPU:8 now
where the time goes in v1:
time: 143 us; the launch traced here: 142 us
  blocking collectives  52.6 us (37%)
  starting transfers between devices  43.5 us (30%)
  waiting for transfers between devices  31.8 us (22%)
  local copies, waits for them, and re-layouts  7.27 us (5%)
  Pallas kernels  6.68 us (5%)
    all_to_all x2, blocking collectives, exchange_pieces(): pieces = lax.all_to_all(pieces, 'ctx', 0, 0, axis_index_groups=SIDE_GROUPS)  52.6 us
    ppermute x1, starting transfers between devices, body(): got = lax.ppermute(sent, 'ctx', SIDE_SWAP)  11.4 us
    ppermute x1, starting transfers between devices, body(): top_b = lax.ppermute(up, 'tp', RING_UP)  8.85 us
    ppermute x1, waiting for transfers between devices, body(): from_below = lax.ppermute(far_top, 'tp', RING_UP)  7.27 us
    ppermute x1, waiting for transfers between devices, body(): bottom_b = lax.ppermute(down, 'tp', RING_DOWN)  7.25 us
    unnamed x24, local copies, waits for them, and re-layouts  7.19 us
    ppermute x1, waiting for transfers between devices, body(): top_a = lax.ppermute(down_top, 'tp', RING_DOWN)  5.9 us
    ppermute x1, waiting for transfers between devices, body(): other = lax.ppermute(own, 'ctx', SIDE_SWAP)  5.32 us
  transfers between devices with their start and end apart: 10, of which 7 were waited for; matrix products, arithmetic and copies ran while one was open for 0% of the time, Pallas kernels for 1%

profile of v1, /device:TPU:8, one launch (start us, length us, event | category | flops | bytes accessed | tf_op | source)
XLA Modules:
  0.0 142.2 jit_solution(9206487940461985902)
XLA Ops:
  0.0 0.9 copy-done.3
  0.9 0.9 copy-done.5
  3.8 11.4 %collective-permute-start = (f32[576,128]{1,0:T(8,128)S(1)}, f32[576,128]{1,0:T(8,128)S(1)}, u32[]{:S(2)}, u32[]{:S(2)}) collective-permute-start(f32[576,128]{1,0:T(8,128)S(1)} %get-tuple-element.24), channel_id=1, source_target_pairs={{0,8},{8,0},{16,24},{24,16},{32,40},{40,32},{48,56},{56,48},{64,72... | collective-permute-start | bytes 884744 | tf_op jit(solution)/shard_map/ppermute | solution.py:310
  15.2 4.7 %collective-permute-done.got_ref = f32[576,128]{1,0:T(8,128)S(1)} collective-permute-done((f32[576,128]{1,0:T(8,128)S(1)}, f32[576,128]{1,0:T(8,128)S(1)}, u32[]{:S(2)}, u32[]{:S(2)}) %collective-permute-start) | collective-permute-done | bytes 294944 | tf_op jit(solution)/shard_map/ppermute | solution.py:310
  20.0 30.5 %all_to_all.10 = f32[48,3,4,128]{3,2,1,0:T(4,128)S(1)} all-to-all(f32[48,3,4,128]{3,2,1,0:T(4,128)S(1)} %bitcast.17), channel_id=1, replica_groups={{0,16,32,48,64,80,96,112,128,144,160,176,192,208,224,240,256,272,288,30..., dimensions={0} | all-to-all | bytes 589824 | tf_op jit(solution)/shard_map/all_to_all | solution.py:286
  50.6 22.0 %all_to_all.11 = f32[48,3,4,128]{3,2,1,0:T(4,128)S(1)} all-to-all(f32[48,3,4,128]{3,2,1,0:T(4,128)S(1)} %bitcast.19), channel_id=1, replica_groups={{0,16,32,48,64,80,96,112,128,144,160,176,192,208,224,240,256,272,288,30..., dimensions={0} | all-to-all | bytes 589824 | tf_op jit(solution)/shard_map/all_to_all | solution.py:286
  72.7 2.3 %collective-permute-start.1 = (f32[576,128]{1,0:T(8,128)S(1)}, f32[576,128]{1,0:T(8,128)S(1)}, u32[]{:S(2)}, u32[]{:S(2)}) collective-permute-start(f32[576,128]{1,0:T(8,128)S(1)} %bitcast.15), channel_id=1, source_target_pairs={{0,8},{8,0},{16,24},{24,16},{32,40},{40,32},{48,56},{56,48},{64,72... | collective-permute-start | bytes 884744 | tf_op jit(solution)/shard_map/ppermute | solution.py:315
  75.9 5.3 %collective-permute-done.1.other_ref = f32[576,128]{1,0:T(8,128)S(1)} collective-permute-done((f32[576,128]{1,0:T(8,128)S(1)}, f32[576,128]{1,0:T(8,128)S(1)}, u32[]{:S(2)}, u32[]{:S(2)}) %collective-permute-start.1) | collective-permute-done | bytes 294944 | tf_op jit(solution)/shard_map/ppermute | solution.py:315
  81.3 2.8 %copy-done = bf16[512,6144]{1,0:T(8,128)(2,1)S(1)} copy-done((bf16[512,6144]{1,0:T(8,128)(2,1)S(1)}, bf16[512,6144]{1,0:T(8,128)(2,1)}, u32[]{:S(2)}) %copy-start) | copy-done | bytes 6291480
  84.1 1.6 %shard_map.77 = (bf16[128,512]{1,0:T(8,128)(2,1)S(1)}, f32[128,768]{1,0:T(8,128)S(1)}, f32[128,768]{1,0:T(8,128)S(1)}) custom-call(s32[2]{0:T(128)S(1)} %pad_add_fusion.order_ref, bf16[128,512]{1,0:T(8,128)(2,1)S(1)} %copy-done.2, f32[128,512]{1,0:T(8,128)S(1)} %get-tuple-element.27.total_ref, f32[128,512]{1,0:T(8,128)S(1)} %get-tuple-element.28.factor_ref, ...), custom_call_target="tpu_custom_call" | custom-call | flops 230000000 | bytes 3500000 | tf_op jit(solution)/shard_map/pallas_call | solution.py:223
  85.6 1.2 copy-done.1
  86.8 2.7 %shard_map.78 = (f32[3,128,768]{2,1,0:T(8,128)S(1)}, f32[3,128,768]{2,1,0:T(8,128)S(1)}) custom-call(s32[6]{0:T(128)S(1)} %stack.36.order_ref, bf16[128,512]{1,0:T(8,128)(2,1)S(1)} %get-tuple-element.29.normed_ref, bf16[512,6144]{1,0:T(8,128)(2,1)S(1)} %copy-done.1), custom_call_target="tpu_custom_call" | custom-call | flops 604000000 | bytes 7500000 | tf_op jit(solution)/shard_map/pallas_call | solution.py:249
  89.6 1.9 %collective-permute-start.2 = (f32[3,128,768]{2,1,0:T(8,128)S(1)}, f32[3,128,768]{2,1,0:T(8,128)S(1)}, u32[]{:S(2)}, u32[]{:S(2)}) collective-permute-start(f32[3,128,768]{2,1,0:T(8,128)S(1)} %get-tuple-element.31), channel_id=1, source_target_pairs={{0,1},{1,0},{2,3},{3,2},{4,5},{5,4},{6,7},{7,6},{8,9},{9,8},{10,11... | collective-permute-start | bytes 3538952 | tf_op jit(solution)/shard_map/ppermute | solution.py:332
  91.5 2.4 %collective-permute-start.4 = (f32[128,768]{1,0:T(8,128)S(1)}, f32[128,768]{1,0:T(8,128)S(1)}, u32[]{:S(2)}, u32[]{:S(2)}) collective-permute-start(f32[128,768]{1,0:T(8,128)S(1)} %get-tuple-element.36), channel_id=1, source_target_pairs={{0,1},{1,0},{2,3},{3,2},{4,5},{5,4},{6,7},{7,6},{8,9},{9,8},{10,11... | collective-permute-start | bytes 1179656 | tf_op jit(solution)/shard_map/ppermute | solution.py:326
  93.9 1.3 collective-permute-done.4.got_ref
  95.3 4.5 %collective-permute-start.5 = (f32[64,768]{1,0:T(8,128)S(1)}, f32[64,768]{1,0:T(8,128)S(1)}, u32[]{:S(2)}, u32[]{:S(2)}) collective-permute-start(f32[64,768]{1,0:T(8,128)S(1)} %get-tuple-element.37), channel_id=1, source_target_pairs={{0,2},{1,3},{2,4},{3,5},{4,6},{5,7},{6,0},{7,1},{8,10},{9,11},{10,... | collective-permute-start | bytes 589832 | tf_op jit(solution)/shard_map/ppermute | solution.py:330
  99.8 3.5 %collective-permute-start.6 = (f32[64,768]{1,0:T(8,128)S(1)}, f32[64,768]{1,0:T(8,128)S(1)}, u32[]{:S(2)}, u32[]{:S(2)}) collective-permute-start(f32[64,768]{1,0:T(8,128)S(1)} %get-tuple-element.39), channel_id=1, source_target_pairs={{0,6},{1,7},{2,0},{3,1},{4,2},{5,3},{6,4},{7,5},{8,14},{9,15},{10,... | collective-permute-start | bytes 589832 | tf_op jit(solution)/shard_map/ppermute | solution.py:331
  103.4 7.3 %collective-permute-done.5.from_below_ref = f32[64,768]{1,0:T(8,128)S(1)} collective-permute-done((f32[64,768]{1,0:T(8,128)S(1)}, f32[64,768]{1,0:T(8,128)S(1)}, u32[]{:S(2)}, u32[]{:S(2)}) %collective-permute-start.5) | collective-permute-done | bytes 196640 | tf_op jit(solution)/shard_map/ppermute | solution.py:330
  110.8 8.9 %collective-permute-start.7 = (f32[64,768]{1,0:T(8,128)S(1)}, f32[64,768]{1,0:T(8,128)S(1)}, u32[]{:S(2)}, u32[]{:S(2)}) collective-permute-start(f32[64,768]{1,0:T(8,128)S(1)} %get-tuple-element.40), channel_id=1, source_target_pairs={{0,2},{1,3},{2,4},{3,5},{4,6},{5,7},{6,0},{7,1},{8,10},{9,11},{10,... | collective-permute-start | bytes 589832 | tf_op jit(solution)/shard_map/ppermute | solution.py:341
  119.6 1.9 %collective-permute-start.9 = (f32[64,768]{1,0:T(8,128)S(1)}, f32[64,768]{1,0:T(8,128)S(1)}, u32[]{:S(2)}, u32[]{:S(2)}) collective-permute-start(f32[64,768]{1,0:T(8,128)S(1)} %get-tuple-element.42), channel_id=1, source_target_pairs={{0,6},{1,7},{2,0},{3,1},{4,2},{5,3},{6,4},{7,5},{8,14},{9,15},{10,... | collective-permute-start | bytes 589832 | tf_op jit(solution)/shard_map/ppermute | solution.py:342
  121.6 1.9 %collective-permute-start.3 = (f32[64,768]{1,0:T(8,128)S(1)}, f32[64,768]{1,0:T(8,128)S(1)}, u32[]{:S(2)}, u32[]{:S(2)}) collective-permute-start(f32[64,768]{1,0:T(8,128)S(1)} %get-tuple-element.33), channel_id=1, source_target_pairs={{0,6},{1,7},{2,0},{3,1},{4,2},{5,3},{6,4},{7,5},{8,14},{9,15},{10,... | collective-permute-start | bytes 589832 | tf_op jit(solution)/shard_map/ppermute | solution.py:337
  123.5 4.8 %collective-permute-start.8 = (f32[64,768]{1,0:T(8,128)S(1)}, f32[64,768]{1,0:T(8,128)S(1)}, u32[]{:S(2)}, u32[]{:S(2)}) collective-permute-start(f32[64,768]{1,0:T(8,128)S(1)} %get-tuple-element.41), channel_id=1, source_target_pairs={{0,2},{1,3},{2,4},{3,5},{4,6},{5,7},{6,0},{7,1},{8,10},{9,11},{10,... | collective-permute-start | bytes 589832 | tf_op jit(solution)/shard_map/ppermute | solution.py:336
  128.3 7.3 %collective-permute-done.9.bottom_b_ref = f32[64,768]{1,0:T(8,128)S(1)} collective-permute-done((f32[64,768]{1,0:T(8,128)S(1)}, f32[64,768]{1,0:T(8,128)S(1)}, u32[]{:S(2)}, u32[]{:S(2)}) %collective-permute-start.9) | collective-permute-done | bytes 196640 | tf_op jit(solution)/shard_map/ppermute | solution.py:342
  135.6 5.9 %collective-permute-done.3.top_a_ref = f32[64,768]{1,0:T(8,128)S(1)} collective-permute-done((f32[64,768]{1,0:T(8,128)S(1)}, f32[64,768]{1,0:T(8,128)S(1)}, u32[]{:S(2)}, u32[]{:S(2)}) %collective-permute-start.3) | collective-permute-done | bytes 196640 | tf_op jit(solution)/shard_map/ppermute | solution.py:337
  (34 shorter events, 4.0 us)
Async XLA Ops:
  0.0 0.9 copy-start.3
  0.9 0.9 copy-start.5
  1.8 0.7 copy-start.7
  2.5 0.7 copy-start.9
  3.8 16.1 %collective-permute-start = (f32[576,128]{1,0:T(8,128)S(1)}, f32[576,128]{1,0:T(8,128)S(1)}, u32[]{:S(2)}, u32[]{:S(2)}) collective-permute-start(f32[576,128]{1,0:T(8,128)S(1)} %get-tuple-element.24), channel_id=1, source_target_pairs={{0,8},{8,0},{16,24},{24,16},{32,40},{40,32},{48,56},{56,48},{64,72... | collective-permute-start | bytes 884744 | tf_op jit(solution)/shard_map/ppermute | solution.py:310
  19.9 55.3 %copy-start.2 = (bf16[128,512]{1,0:T(8,128)(2,1)S(1)}, bf16[128,512]{1,0:T(8,128)(2,1)}, u32[]{:S(2)}) copy-start(bf16[128,512]{1,0:T(8,128)(2,1)} %query_ref.3) | copy-start | bytes 393220
  19.9 55.3 %copy-start.4 = (bf16[128,512]{1,0:T(8,128)(2,1)S(1)}, bf16[128,512]{1,0:T(8,128)(2,1)}, u32[]{:S(2)}) copy-start(bf16[128,512]{1,0:T(8,128)(2,1)} %key_ref.3) | copy-start | bytes 393220
  19.9 55.3 %copy-start.6 = (bf16[128,512]{1,0:T(8,128)(2,1)S(1)}, bf16[128,512]{1,0:T(8,128)(2,1)}, u32[]{:S(2)}) copy-start(bf16[128,512]{1,0:T(8,128)(2,1)} %value_ref.3) | copy-start | bytes 393220
  20.0 55.3 %copy-start.8 = (f32[4,128]{1,0:T(4,128)S(1)}, f32[4,128]{1,0:T(4,128)}, u32[]{:S(2)}) copy-start(f32[4,128]{1,0:T(4,128)} %log_ref.3) | copy-start | bytes 6148
  20.0 55.3 %copy-start.10 = (s32[128]{0:T(128)S(1)}, s32[128]{0:T(128)}, u32[]{:S(2)}) copy-start(s32[128]{0:T(128)} %param.11) | copy-start | bytes 1540
  50.5 30.8 %copy-start.11 = (f32[512]{0:T(512)S(1)}, f32[512]{0:T(512)}, u32[]{:S(2)}) copy-start(f32[512]{0:T(512)} %param.12) | copy-start | bytes 6148
  72.7 8.6 %collective-permute-start.1 = (f32[576,128]{1,0:T(8,128)S(1)}, f32[576,128]{1,0:T(8,128)S(1)}, u32[]{:S(2)}, u32[]{:S(2)}) collective-permute-start(f32[576,128]{1,0:T(8,128)S(1)} %bitcast.15), channel_id=1, source_target_pairs={{0,8},{8,0},{16,24},{24,16},{32,40},{40,32},{48,56},{56,48},{64,72... | collective-permute-start | bytes 884744 | tf_op jit(solution)/shard_map/ppermute | solution.py:315
  81.3 2.8 %copy-start = (bf16[512,6144]{1,0:T(8,128)(2,1)S(1)}, bf16[512,6144]{1,0:T(8,128)(2,1)}, u32[]{:S(2)}) copy-start(bf16[512,6144]{1,0:T(8,128)(2,1)} %w_ref.3) | copy-start | bytes 18874372
  84.1 2.8 %copy-start.1 = (bf16[512,6144]{1,0:T(8,128)(2,1)S(1)}, bf16[512,6144]{1,0:T(8,128)(2,1)}, u32[]{:S(2)}) copy-start(bf16[512,6144]{1,0:T(8,128)(2,1)} %w_ref.3) | copy-start | bytes 18874372
  89.6 13.7 %collective-permute-start.2 = (f32[3,128,768]{2,1,0:T(8,128)S(1)}, f32[3,128,768]{2,1,0:T(8,128)S(1)}, u32[]{:S(2)}, u32[]{:S(2)}) collective-permute-start(f32[3,128,768]{2,1,0:T(8,128)S(1)} %get-tuple-element.31), channel_id=1, source_target_pairs={{0,1},{1,0},{2,3},{3,2},{4,5},{5,4},{6,7},{7,6},{8,9},{9,8},{10,11... | collective-permute-start | bytes 3538952 | tf_op jit(solution)/shard_map/ppermute | solution.py:332
  91.5 3.7 %collective-permute-start.4 = (f32[128,768]{1,0:T(8,128)S(1)}, f32[128,768]{1,0:T(8,128)S(1)}, u32[]{:S(2)}, u32[]{:S(2)}) collective-permute-start(f32[128,768]{1,0:T(8,128)S(1)} %get-tuple-element.36), channel_id=1, source_target_pairs={{0,1},{1,0},{2,3},{3,2},{4,5},{5,4},{6,7},{7,6},{8,9},{9,8},{10,11... | collective-permute-start | bytes 1179656 | tf_op jit(solution)/shard_map/ppermute | solution.py:326
  95.3 15.4 %collective-permute-start.5 = (f32[64,768]{1,0:T(8,128)S(1)}, f32[64,768]{1,0:T(8,128)S(1)}, u32[]{:S(2)}, u32[]{:S(2)}) collective-permute-start(f32[64,768]{1,0:T(8,128)S(1)} %get-tuple-element.37), channel_id=1, source_target_pairs={{0,2},{1,3},{2,4},{3,5},{4,6},{5,7},{6,0},{7,1},{8,10},{9,11},{10,... | collective-permute-start | bytes 589832 | tf_op jit(solution)/shard_map/ppermute | solution.py:330
  99.8 10.9 %collective-permute-start.6 = (f32[64,768]{1,0:T(8,128)S(1)}, f32[64,768]{1,0:T(8,128)S(1)}, u32[]{:S(2)}, u32[]{:S(2)}) collective-permute-start(f32[64,768]{1,0:T(8,128)S(1)} %get-tuple-element.39), channel_id=1, source_target_pairs={{0,6},{1,7},{2,0},{3,1},{4,2},{5,3},{6,4},{7,5},{8,14},{9,15},{10,... | collective-permute-start | bytes 589832 | tf_op jit(solution)/shard_map/ppermute | solution.py:331
  110.8 17.5 %collective-permute-start.7 = (f32[64,768]{1,0:T(8,128)S(1)}, f32[64,768]{1,0:T(8,128)S(1)}, u32[]{:S(2)}, u32[]{:S(2)}) collective-permute-start(f32[64,768]{1,0:T(8,128)S(1)} %get-tuple-element.40), channel_id=1, source_target_pairs={{0,2},{1,3},{2,4},{3,5},{4,6},{5,7},{6,0},{7,1},{8,10},{9,11},{10,... | collective-permute-start | bytes 589832 | tf_op jit(solution)/shard_map/ppermute | solution.py:341
  119.6 15.9 %collective-permute-start.9 = (f32[64,768]{1,0:T(8,128)S(1)}, f32[64,768]{1,0:T(8,128)S(1)}, u32[]{:S(2)}, u32[]{:S(2)}) collective-permute-start(f32[64,768]{1,0:T(8,128)S(1)} %get-tuple-element.42), channel_id=1, source_target_pairs={{0,6},{1,7},{2,0},{3,1},{4,2},{5,3},{6,4},{7,5},{8,14},{9,15},{10,... | collective-permute-start | bytes 589832 | tf_op jit(solution)/shard_map/ppermute | solution.py:342
  121.6 19.9 %collective-permute-start.3 = (f32[64,768]{1,0:T(8,128)S(1)}, f32[64,768]{1,0:T(8,128)S(1)}, u32[]{:S(2)}, u32[]{:S(2)}) collective-permute-start(f32[64,768]{1,0:T(8,128)S(1)} %get-tuple-element.33), channel_id=1, source_target_pairs={{0,6},{1,7},{2,0},{3,1},{4,2},{5,3},{6,4},{7,5},{8,14},{9,15},{10,... | collective-permute-start | bytes 589832 | tf_op jit(solution)/shard_map/ppermute | solution.py:337
  123.5 18.0 %collective-permute-start.8 = (f32[64,768]{1,0:T(8,128)S(1)}, f32[64,768]{1,0:T(8,128)S(1)}, u32[]{:S(2)}, u32[]{:S(2)}) collective-permute-start(f32[64,768]{1,0:T(8,128)S(1)} %get-tuple-element.41), channel_id=1, source_target_pairs={{0,2},{1,3},{2,4},{3,5},{4,6},{5,7},{6,0},{7,1},{8,10},{9,11},{10,... | collective-permute-start | bytes 589832 | tf_op jit(solution)/shard_map/ppermute | solution.py:336

commit v2 on v1

v2 whole, which is shorter than its diff:
```python
import math

import jax
import jax.numpy as jnp
from jax import lax
from jax.experimental import pallas as pl
from jax.experimental.pallas import tpu as pltpu
from jax.sharding import PartitionSpec as P

HEAD_DIM = 128
EVENTS = 128
HEADS_DEV = 4
D = 6144
COLS = 768
PAIRS = 48
PIECES = PAIRS // HEADS_DEV
ROWS = 11
CHUNK = ROWS + 1
HEAD_ROWS = PIECES * CHUNK
PACKED = PAIRS * CHUNK

surge_log_factor = math.log(0.6)
F32 = jnp.float32
BF16 = jnp.bfloat16
VMEM_LIMIT = 24 * 1024 * 1024
TERMS_LIMIT = 60_000_000
STAGE_LIMIT = 46 * 1024 * 1024

SIDE_GROUPS = [[2 * pair + side for pair in range(PAIRS)] for side in range(2)]
SIDE_SWAP = [(i, i ^ 1) for i in range(2 * PAIRS)]
CORE_SWAP = [(i, i ^ 1) for i in range(8)]
ONWARD = [(i, (i + (2 if i % 2 == 0 else 6)) % 8) for i in range(8)]
BACK = [(i, (i + (6 if i % 2 == 0 else 2)) % 8) for i in range(8)]


def piece_rows(piece):
    return min(ROWS, HEAD_DIM - ROWS * piece)


def call(kernel, outs, args, scalars=0, scratch=(), flops=0, moved=0, space=pltpu.VMEM, limit=VMEM_LIMIT):
    specs = [pl.BlockSpec(memory_space=pltpu.SMEM)] * scalars
    specs += [pl.BlockSpec(memory_space=space)] * (len(args) - scalars)
    return pl.pallas_call(
        kernel,
        out_shape=[jax.ShapeDtypeStruct(shape, dtype) for shape, dtype in outs],
        in_specs=specs,
        out_specs=[pl.BlockSpec(memory_space=pltpu.VMEM)] * len(outs),
        scratch_shapes=list(scratch),
        compiler_params=pltpu.CompilerParams(vmem_limit_bytes=limit),
        cost_estimate=pl.CostEstimate(flops=flops, bytes_accessed=moved, transcendentals=0),
    )(*args)


def event_sums(log_ref, boundary_ref):
    rate = log_ref[...] + surge_log_factor * boundary_ref[...].astype(F32)
    row = lax.broadcasted_iota(jnp.int32, (EVENTS, EVENTS), 0)
    column = lax.broadcasted_iota(jnp.int32, (EVENTS, EVENTS), 1)
    lower = (column <= row).astype(F32)
    upper = (row <= column).astype(F32)
    columns = lax.dot_general(
        lower, rate, (((1,), (1,)), ((), ())), precision=lax.Precision.HIGHEST, preferred_element_type=F32
    )
    return rate, columns, upper


def factors(side, columns):
    ends = columns[EVENTS - 1 : EVENTS, :]
    toward_end = jnp.exp(ends - columns)
    from_start = jnp.exp(columns)
    sent = jnp.where(side == 0, toward_end, from_start)
    kept = jnp.where(side == 0, from_start, toward_end)
    return ends, sent, kept


def halves(wide):
    high = wide.astype(BF16)
    low = (wide - high.astype(F32)).astype(BF16)
    return high, low


def terms_kernel(
    side_ref,
    key_hbm,
    value_hbm,
    log_hbm,
    boundary_hbm,
    sent_ref,
    kept_ref,
    decay_ref,
    key_ref,
    value_ref,
    log_ref,
    boundary_ref,
    sems,
):
    copies = [
        pltpu.make_async_copy(log_hbm, log_ref, sems.at[0]),
        pltpu.make_async_copy(boundary_hbm, boundary_ref, sems.at[1]),
        pltpu.make_async_copy(key_hbm, key_ref, sems.at[2]),
        pltpu.make_async_copy(value_hbm, value_ref, sems.at[3]),
    ]
    for copy in copies:
        copy.start()
    for copy in copies:
        copy.wait()
    _, columns, _ = event_sums(log_ref, boundary_ref)
    ends, sent, kept = factors(side_ref[0], columns)
    decay = jnp.exp(ends)
    sent_ref[...] = jnp.zeros_like(sent_ref)
    kept_ref[...] = jnp.zeros_like(kept_ref)
    for head in range(HEADS_DEV):
        lanes = slice(head * HEAD_DIM, (head + 1) * HEAD_DIM)
        value = value_ref[:, lanes].astype(F32)
        sides = halves(value * sent[:, head : head + 1]) + halves(value * kept[:, head : head + 1])
        product = lax.dot_general(
            key_ref[:, lanes],
            jnp.concatenate(sides, axis=1),
            (((0,), (0,)), ((), ())),
            preferred_element_type=F32,
        )
        sent_term = product[:, :128] + product[:, 128:256]
        kept_term = product[:, 256:384] + product[:, 384:]
        whole_row = jnp.broadcast_to(decay[:, head : head + 1], (1, HEAD_DIM))
        decay_ref[head : head + 1, :] = whole_row
        for piece in range(PIECES):
            count, first = piece_rows(piece), head * HEAD_ROWS + piece * CHUNK
            rows = slice(ROWS * piece, ROWS * piece + count)
            sent_ref[first : first + count, :] = sent_term[rows]
            kept_ref[first : first + count, :] = kept_term[rows]
            sent_ref[first + ROWS : first + CHUNK, :] = whole_row


def combine_kernel(kept_ref, got_ref, decay_ref, out_ref):
    for head in range(HEADS_DEV):
        rows = slice(head * HEAD_ROWS, (head + 1) * HEAD_ROWS)
        out_ref[rows, :] = kept_ref[rows, :] + decay_ref[head : head + 1, :] * got_ref[rows, :]


def scan_kernel(side_ref, term_ref, out_ref):
    def run(pairs):
        state = jnp.zeros((CHUNK, HEAD_DIM), F32)
        for pair in pairs:
            rows = slice(pair * CHUNK, (pair + 1) * CHUNK)
            out_ref[rows, :] = state
            term = term_ref[rows, :]
            state = term[ROWS:, :] * state + term

    @pl.when(side_ref[0] == 1)
    def _():
        run(range(PAIRS))

    @pl.when(side_ref[0] == 0)
    def _():
        run(range(PAIRS - 1, -1, -1))


def unpack(packed_ref, head):
    parts = []
    for piece in range(PIECES):
        first = head * HEAD_ROWS + piece * CHUNK
        parts.append(packed_ref[first : first + piece_rows(piece), :])
    return jnp.concatenate(parts, axis=0)


def times_state(query, state):
    product = jnp.dot(query, jnp.concatenate(halves(state), axis=1), preferred_element_type=F32)
    return product[:, :128] + product[:, 128:]


def inner_kernel(
    side_ref, query_ref, key_ref, value_ref, log_ref, boundary_ref, got_ref, own_ref, total_ref, factor_ref
):
    rate, columns, upper = event_sums(log_ref, boundary_ref)
    rows_cum = lax.dot_general(
        rate, upper, (((1,), (0,)), ((), ())), precision=lax.Precision.HIGHEST, preferred_element_type=F32
    )
    _, own, other = factors(side_ref[0], columns)
    for head in range(HEADS_DEV):
        lanes = slice(head * HEAD_DIM, (head + 1) * HEAD_DIM)
        query = query_ref[:, lanes]
        logits = lax.dot_general(
            query, key_ref[:, lanes], (((1,), (1,)), ((), ())), preferred_element_type=F32
        )
        weight = jnp.exp(-jnp.abs(columns[:, head : head + 1] - rows_cum[head : head + 1, :]))
        probs = (logits * weight).astype(BF16)
        intra = jnp.dot(probs, value_ref[:, lanes], preferred_element_type=F32)
        last = head * HEAD_ROWS + ROWS
        state = unpack(got_ref, head) + got_ref[last : last + 1, :] * unpack(own_ref, head)
        total_ref[:, lanes] = intra + own[:, head : head + 1] * times_state(query, state)
        factor_ref[:, lanes] = jnp.broadcast_to(other[:, head : head + 1], (EVENTS, HEAD_DIM))


def stage_kernel(w_hbm, staged_ref, sems):
    copies = [
        pltpu.make_async_copy(w_hbm.at[:, pl.ds(block * COLS, COLS)], staged_ref.at[block], sems.at[block])
        for block in range(D // COLS)
    ]
    for copy in copies:
        copy.start()
    for copy in copies:
        copy.wait()


def block_of(place, far, core):
    return 2 * (((place >> 1) + far) & 3) + core


def first_kernel(
    place_ref, query_ref, total_ref, factor_ref, other_ref, gain_ref, w_ref, normed_ref, send_ref, mine_ref
):
    for head in range(HEADS_DEV):
        lanes = slice(head * HEAD_DIM, (head + 1) * HEAD_DIM)
        total = total_ref[:, lanes] + factor_ref[:, lanes] * times_state(
            query_ref[:, lanes], unpack(other_ref, head)
        )
        average = jnp.mean(total * total, axis=1, keepdims=True)
        scaled = total * lax.rsqrt(average + 1e-06) * gain_ref[:, lanes]
        normed_ref[:, lanes] = scaled.astype(BF16)
    place = place_ref[0]
    core = place & 1
    normed = normed_ref[...]
    send_ref[...] = jnp.dot(normed, w_ref[block_of(place, 2, 1 - core)], preferred_element_type=F32)
    mine_ref[...] = jnp.dot(normed, w_ref[block_of(place, 2, core)], preferred_element_type=F32)


def rest_kernel(place_ref, normed_ref, w_ref, send_ref, mine_ref):
    place = place_ref[0]
    core = place & 1
    normed = normed_ref[...]
    for target_ref, whose in ((send_ref, 1 - core), (mine_ref, core)):
        for slot, far in enumerate((3 - 2 * whose, 1 + 2 * whose, 0)):
            target_ref[slot] = jnp.dot(
                normed, w_ref[block_of(place, far, whose)], preferred_element_type=F32
            )


def far_kernel(mine_ref, got_ref, out_ref):
    out_ref[...] = mine_ref[...] + got_ref[...]


def near_kernel(mine_ref, got_ref, behind_ref, ahead_ref, own_ref):
    behind_ref[...] = mine_ref[0] + got_ref[0]
    ahead_ref[...] = mine_ref[1] + got_ref[1]
    own_ref[...] = mine_ref[2] + got_ref[2]


def final_kernel(one_ref, two_ref, out_ref):
    out_ref[...] = (one_ref[...] + two_ref[...]).astype(BF16)


def exchange_pieces(packed):
    pieces = packed.reshape(PAIRS, 3, 4, HEAD_DIM)
    pieces = lax.all_to_all(pieces, "ctx", 0, 0, axis_index_groups=SIDE_GROUPS)
    return pieces.reshape(PACKED, HEAD_DIM)


def body(queries, keys, values, state_retention_log, boundary, gain, w_out):
    side = (lax.axis_index("ctx") & 1).reshape(1)
    place = lax.axis_index("tp").reshape(1)
    boundary = boundary.reshape(1, EVENTS)
    gain = gain.reshape(1, 512)
    packed = ((PACKED, HEAD_DIM), F32)

    sent, kept, decay = call(
        terms_kernel,
        [packed, packed, ((HEADS_DEV, HEAD_DIM), F32)],
        (side, keys, values, state_retention_log, boundary),
        scalars=1,
        scratch=[
            pltpu.VMEM((EVENTS, 512), BF16),
            pltpu.VMEM((EVENTS, 512), BF16),
            pltpu.VMEM((HEADS_DEV, EVENTS), F32),
            pltpu.VMEM((1, EVENTS), jnp.int32),
            pltpu.SemaphoreType.DMA((4,)),
        ],
        flops=70_000_000,
        moved=900_000,
        space=pltpu.HBM,
        limit=TERMS_LIMIT,
    )
    sent, w_out = lax.optimization_barrier((sent, w_out))
    got = lax.ppermute(sent, "ctx", SIDE_SWAP)
    (staged,) = call(
        stage_kernel,
        [((D // COLS, 512, COLS), BF16)],
        (w_out,),
        scratch=[pltpu.SemaphoreType.DMA((D // COLS,))],
        moved=12_600_000,
        space=pltpu.HBM,
        limit=STAGE_LIMIT,
    )
    got, staged = lax.optimization_barrier((got, staged))
    (pair_terms,) = call(combine_kernel, [packed], (kept, got, decay), flops=200_000, moved=900_000)
    slices = exchange_pieces(pair_terms)
    (states,) = call(scan_kernel, [packed], (side, slices), scalars=1, flops=200_000, moved=600_000)
    own = exchange_pieces(states)
    other = lax.ppermute(own, "ctx", SIDE_SWAP)
    inner = ((EVENTS, 512), F32)
    total, factor = call(
        inner_kernel,
        [inner, inner],
        (side, queries, keys, values, state_retention_log, boundary, got, own),
        scalars=1,
        flops=100_000_000,
        moved=1_500_000,
    )
    block = ((EVENTS, COLS), F32)
    three = ((3, EVENTS, COLS), F32)
    normed, send, mine = call(
        first_kernel,
        [((EVENTS, 512), BF16), block, block],
        (place, queries, total, factor, other, gain, staged),
        scalars=1,
        flops=230_000_000,
        moved=3_500_000,
    )
    far_got = lax.ppermute(send, "tp", CORE_SWAP)
    (far,) = call(far_kernel, [block], (mine, far_got), moved=1_200_000)
    near_send, near_mine = call(
        rest_kernel, [three, three], (place, normed, staged), scalars=1, flops=604_000_000, moved=7_500_000
    )
    far, near_send = lax.optimization_barrier((far, near_send))
    ahead_got = lax.ppermute(far, "tp", ONWARD)
    near_got = lax.ppermute(near_send, "tp", CORE_SWAP)
    behind, ahead, own_sum = call(near_kernel, [block] * 3, (near_mine, near_got), moved=3_600_000)
    one = lax.ppermute(behind, "tp", BACK)
    (passed,) = call(far_kernel, [block], (ahead, ahead_got), moved=1_200_000)
    two = lax.ppermute(passed, "tp", ONWARD)
    (own_and_one,) = call(far_kernel, [block], (own_sum, one), moved=1_200_000)
    (out,) = call(final_kernel, [((EVENTS, COLS), BF16)], (own_and_one, two), moved=1_000_000)
    return out


def solution(mesh):
    in_specs = (
        P("ctx", "tp"),
        P("ctx", "tp"),
        P("ctx", "tp"),
        P("tp", "ctx"),
        P("ctx"),
        P("tp"),
        P("tp", None),
    )
    out_specs = P("ctx", "tp")
    return jax.shard_map(body, mesh=mesh, in_specs=in_specs, out_specs=out_specs, check_vma=False)
```

time: 143 us -> 126 us (0.88)
  the two profiles are of different devices: /device:TPU:8 before, /device:TPU:1 now
where the time goes in v2:
time: 126 us; the launch traced here: 125 us
  blocking collectives  56.3 us (45%)
  starting transfers between devices  31.5 us (25%)
  waiting for transfers between devices  22.9 us (18%)
  Pallas kernels  8.51 us (7%)
  local copies, waits for them, and re-layouts  5.48 us (4%)
    all_to_all x2, blocking collectives, exchange_pieces(): pieces = lax.all_to_all(pieces, 'ctx', 0, 0, axis_index_groups=SIDE_GROUPS)  56.3 us
    ppermute x1, waiting for transfers between devices, body(): ahead_got = lax.ppermute(far, 'tp', ONWARD)  13.3 us
    pallas_call x12, Pallas kernels, call(): pl.pallas_call(kernel, out_shape=[jax.ShapeDtypeStruct(shape, dtype) for...  8.51 us
    ppermute x1, starting transfers between devices, body(): far_got = lax.ppermute(send, 'tp', CORE_SWAP)  7.73 us
    ppermute x1, starting transfers between devices, body(): two = lax.ppermute(passed, 'tp', ONWARD)  6.36 us
    ppermute x1, starting transfers between devices, body(): ahead_got = lax.ppermute(far, 'tp', ONWARD)  5.88 us
    ppermute x1, waiting for transfers between devices, body(): two = lax.ppermute(passed, 'tp', ONWARD)  5.53 us
    unnamed x22, local copies, waits for them, and re-layouts  5.48 us
  transfers between devices with their start and end apart: 7, of which 4 were waited for; matrix products, arithmetic and copies ran while one was open for 0% of the time, Pallas kernels for 4%

profile of v2, /device:TPU:1, one launch (start us, length us, event | category | flops | bytes accessed | tf_op | source)
XLA Modules:
  0.0 125.1 jit_solution(7066435907572142058)
XLA Ops:
  0.0 2.5 %shard_map.73 = (f32[576,128]{1,0:T(8,128)}, f32[576,128]{1,0:T(8,128)}, f32[4,128]{1,0:T(4,128)}) custom-call(s32[1]{0:T(128)} %bitcast.1.side_ref, bf16[128,512]{1,0:T(8,128)(2,1)} %key_ref.1, bf16[128,512]{1,0:T(8,128)(2,1)} %value_ref.1, f32[4,128]{1,0:T(4,128)} %log_ref.1, s32[1,128]{1,0:T(1,128)} %bitcast.13), custom_call_target="tpu_custom_call" | custom-call | flops 70000000 | bytes 900000 | tf_op jit(solution)/shard_map/pallas_call | solution.py:43
  2.5 0.0 copy-start.8
  2.5 4.2 %collective-permute-start = (f32[576,128]{1,0:T(8,128)}, f32[576,128]{1,0:T(8,128)S(1)}, u32[]{:S(2)}, u32[]{:S(2)}) collective-permute-start(f32[576,128]{1,0:T(8,128)} %get-tuple-element.25), channel_id=1, source_target_pairs={{0,8},{8,0},{16,24},{24,16},{32,40},{40,32},{48,56},{56,48},{64,72... | collective-permute-start | bytes 884744 | tf_op jit(solution)/shard_map/ppermute | solution.py:282
  6.7 2.9 %shard_map.74.w_ref = bf16[8,512,768]{2,1,0:T(8,128)(2,1)S(1)} custom-call(bf16[512,6144]{1,0:T(8,128)(2,1)} %w_hbm), custom_call_target="tpu_custom_call" | custom-call | bytes 12600000 | tf_op jit(solution)/shard_map/pallas_call | solution.py:43
  9.6 2.6 %copy-done = bf16[8,512,768]{2,1,0:T(8,128)(2,1)} copy-done((bf16[8,512,768]{2,1,0:T(8,128)(2,1)}, bf16[8,512,768]{2,1,0:T(8,128)(2,1)S(1)}, u32[]{:S(2)}) %copy-start) | copy-done | bytes 6291480
  12.3 34.2 %all_to_all.10 = f32[48,3,4,128]{3,2,1,0:T(4,128)S(1)} all-to-all(f32[48,3,4,128]{3,2,1,0:T(4,128)S(1)} %bitcast.10), channel_id=1, replica_groups={{0,16,32,48,64,80,96,112,128,144,160,176,192,208,224,240,256,272,288,30..., dimensions={0} | all-to-all | bytes 589824 | tf_op jit(solution)/shard_map/all_to_all | solution.py:253
  46.5 0.1 shard_map.76
  46.6 22.2 %all_to_all.11 = f32[48,3,4,128]{3,2,1,0:T(4,128)S(1)} all-to-all(f32[48,3,4,128]{3,2,1,0:T(4,128)S(1)} %bitcast.12), channel_id=1, replica_groups={{0,16,32,48,64,80,96,112,128,144,160,176,192,208,224,240,256,272,288,30..., dimensions={0} | all-to-all | bytes 589824 | tf_op jit(solution)/shard_map/all_to_all | solution.py:253
  68.8 3.2 %collective-permute-start.1 = (f32[576,128]{1,0:T(8,128)S(1)}, f32[576,128]{1,0:T(8,128)S(1)}, u32[]{:S(2)}, u32[]{:S(2)}) collective-permute-start(f32[576,128]{1,0:T(8,128)S(1)} %bitcast.8), channel_id=1, source_target_pairs={{0,8},{8,0},{16,24},{24,16},{32,40},{40,32},{48,56},{56,48},{64,72... | collective-permute-start | bytes 884744 | tf_op jit(solution)/shard_map/ppermute | solution.py:297
  72.0 0.7 shard_map.77
  72.7 3.5 %collective-permute-done.1.other_ref = f32[576,128]{1,0:T(8,128)S(1)} collective-permute-done((f32[576,128]{1,0:T(8,128)S(1)}, f32[576,128]{1,0:T(8,128)S(1)}, u32[]{:S(2)}, u32[]{:S(2)}) %collective-permute-start.1) | collective-permute-done | bytes 294944 | tf_op jit(solution)/shard_map/ppermute | solution.py:297
  76.2 2.8 %copy-done.1 = bf16[8,512,768]{2,1,0:T(8,128)(2,1)S(1)} copy-done((bf16[8,512,768]{2,1,0:T(8,128)(2,1)S(1)}, bf16[8,512,768]{2,1,0:T(8,128)(2,1)}, u32[]{:S(2)}) %copy-start.1) | copy-done | bytes 6291480
  79.0 0.6 shard_map.78
  79.6 7.7 %collective-permute-start.2 = (f32[128,768]{1,0:T(8,128)S(1)}, f32[128,768]{1,0:T(8,128)S(1)}, u32[]{:S(2)}, u32[]{:S(2)}) collective-permute-start(f32[128,768]{1,0:T(8,128)S(1)} %get-tuple-element.36), channel_id=1, source_target_pairs={{0,1},{1,0},{2,3},{3,2},{4,5},{5,4},{6,7},{7,6},{8,9},{9,8},{10,11... | collective-permute-start | bytes 1179656 | tf_op jit(solution)/shard_map/ppermute | solution.py:317
  87.4 0.8 shard_map.79
  88.2 0.5 collective-permute-done.2.got_ref
  88.7 2.3 %collective-permute-start.3 = (f32[3,128,768]{2,1,0:T(8,128)S(1)}, f32[3,128,768]{2,1,0:T(8,128)S(1)}, u32[]{:S(2)}, u32[]{:S(2)}) collective-permute-start(f32[3,128,768]{2,1,0:T(8,128)S(1)} %get-tuple-element.38), channel_id=1, source_target_pairs={{0,1},{1,0},{2,3},{3,2},{4,5},{5,4},{6,7},{7,6},{8,9},{9,8},{10,11... | collective-permute-start | bytes 3538952 | tf_op jit(solution)/shard_map/ppermute | solution.py:324
  91.0 5.9 %collective-permute-start.5 = (f32[128,768]{1,0:T(8,128)S(1)}, f32[128,768]{1,0:T(8,128)S(1)}, u32[]{:S(2)}, u32[]{:S(2)}) collective-permute-start(f32[128,768]{1,0:T(8,128)S(1)} %shard_map.80), channel_id=1, source_target_pairs={{0,2},{1,7},{2,4},{3,1},{4,6},{5,3},{6,0},{7,5},{8,10},{9,15},{10,... | collective-permute-start | bytes 1179656 | tf_op jit(solution)/shard_map/ppermute | solution.py:323
  96.9 0.1 shard_map.81
  97.1 1.9 %collective-permute-start.4 = (f32[128,768]{1,0:T(8,128)S(1)}, f32[128,768]{1,0:T(8,128)S(1)}, u32[]{:S(2)}, u32[]{:S(2)}) collective-permute-start(f32[128,768]{1,0:T(8,128)S(1)} %get-tuple-element.40), channel_id=1, source_target_pairs={{0,6},{1,3},{2,0},{3,5},{4,2},{5,7},{6,4},{7,1},{8,14},{9,11},{10,... | collective-permute-start | bytes 1179656 | tf_op jit(solution)/shard_map/ppermute | solution.py:326
  99.0 13.3 %collective-permute-done.5.got_ref = f32[128,768]{1,0:T(8,128)S(1)} collective-permute-done((f32[128,768]{1,0:T(8,128)S(1)}, f32[128,768]{1,0:T(8,128)S(1)}, u32[]{:S(2)}, u32[]{:S(2)}) %collective-permute-start.5) | collective-permute-done | bytes 393248 | tf_op jit(solution)/shard_map/ppermute | solution.py:323
  112.4 6.4 %collective-permute-start.6 = (f32[128,768]{1,0:T(8,128)S(1)}, f32[128,768]{1,0:T(8,128)S(1)}, u32[]{:S(2)}, u32[]{:S(2)}) collective-permute-start(f32[128,768]{1,0:T(8,128)S(1)} %shard_map.83), channel_id=1, source_target_pairs={{0,2},{1,7},{2,4},{3,1},{4,6},{5,3},{6,0},{7,5},{8,10},{9,15},{10,... | collective-permute-start | bytes 1179656 | tf_op jit(solution)/shard_map/ppermute | solution.py:328
  118.8 5.5 %collective-permute-done.6.two_ref = f32[128,768]{1,0:T(8,128)S(1)} collective-permute-done((f32[128,768]{1,0:T(8,128)S(1)}, f32[128,768]{1,0:T(8,128)S(1)}, u32[]{:S(2)}, u32[]{:S(2)}) %collective-permute-start.6) | collective-permute-done | bytes 393248 | tf_op jit(solution)/shard_map/ppermute | solution.py:328
  124.3 0.7 shard_map.84
  (26 shorter events, 0.2 us)
Async XLA Ops:
  2.5 9.8 %copy-start.6 = (f32[576,128]{1,0:T(8,128)S(1)}, f32[576,128]{1,0:T(8,128)}, u32[]{:S(2)}) copy-start(f32[576,128]{1,0:T(8,128)} %get-tuple-element.28.kept_ref) | copy-start | bytes 884740
  2.5 9.7 %copy-start.8 = (f32[4,128]{1,0:T(4,128)S(1)}, f32[4,128]{1,0:T(4,128)}, u32[]{:S(2)}) copy-start(f32[4,128]{1,0:T(4,128)} %get-tuple-element.29.decay_ref) | copy-start | bytes 6148
  2.5 9.7 %collective-permute-start = (f32[576,128]{1,0:T(8,128)}, f32[576,128]{1,0:T(8,128)S(1)}, u32[]{:S(2)}, u32[]{:S(2)}) collective-permute-start(f32[576,128]{1,0:T(8,128)} %get-tuple-element.25), channel_id=1, source_target_pairs={{0,8},{8,0},{16,24},{24,16},{32,40},{40,32},{48,56},{56,48},{64,72... | collective-permute-start | bytes 884744 | tf_op jit(solution)/shard_map/ppermute | solution.py:282
  9.6 2.7 %copy-start = (bf16[8,512,768]{2,1,0:T(8,128)(2,1)}, bf16[8,512,768]{2,1,0:T(8,128)(2,1)S(1)}, u32[]{:S(2)}) copy-start(bf16[8,512,768]{2,1,0:T(8,128)(2,1)S(1)} %shard_map.74.w_ref) | copy-start | bytes 18874372
  12.2 59.7 %copy-start.3 = (bf16[128,512]{1,0:T(8,128)(2,1)S(1)}, bf16[128,512]{1,0:T(8,128)(2,1)}, u32[]{:S(2)}) copy-start(bf16[128,512]{1,0:T(8,128)(2,1)} %query_ref.3) | copy-start | bytes 393220
  12.3 59.7 %copy-start.4 = (bf16[128,512]{1,0:T(8,128)(2,1)S(1)}, bf16[128,512]{1,0:T(8,128)(2,1)}, u32[]{:S(2)}) copy-start(bf16[128,512]{1,0:T(8,128)(2,1)} %key_ref.1) | copy-start | bytes 393220
  12.3 59.7 %copy-start.5 = (bf16[128,512]{1,0:T(8,128)(2,1)S(1)}, bf16[128,512]{1,0:T(8,128)(2,1)}, u32[]{:S(2)}) copy-start(bf16[128,512]{1,0:T(8,128)(2,1)} %value_ref.1) | copy-start | bytes 393220
  12.3 59.7 %copy-start.7 = (f32[4,128]{1,0:T(4,128)S(1)}, f32[4,128]{1,0:T(4,128)}, u32[]{:S(2)}) copy-start(f32[4,128]{1,0:T(4,128)} %log_ref.1) | copy-start | bytes 6148
  12.3 59.7 %copy-start.9 = (s32[128]{0:T(128)S(1)}, s32[128]{0:T(128)}, u32[]{:S(2)}) copy-start(s32[128]{0:T(128)} %param.11) | copy-start | bytes 1540
  46.5 29.7 %copy-start.10 = (f32[512]{0:T(512)S(1)}, f32[512]{0:T(512)}, u32[]{:S(2)}) copy-start(f32[512]{0:T(512)} %param.12) | copy-start | bytes 6148
  68.8 7.5 %collective-permute-start.1 = (f32[576,128]{1,0:T(8,128)S(1)}, f32[576,128]{1,0:T(8,128)S(1)}, u32[]{:S(2)}, u32[]{:S(2)}) collective-permute-start(f32[576,128]{1,0:T(8,128)S(1)} %bitcast.8), channel_id=1, source_target_pairs={{0,8},{8,0},{16,24},{24,16},{32,40},{40,32},{48,56},{56,48},{64,72... | collective-permute-start | bytes 884744 | tf_op jit(solution)/shard_map/ppermute | solution.py:297
  76.2 2.8 %copy-start.1 = (bf16[8,512,768]{2,1,0:T(8,128)(2,1)S(1)}, bf16[8,512,768]{2,1,0:T(8,128)(2,1)}, u32[]{:S(2)}) copy-start(bf16[8,512,768]{2,1,0:T(8,128)(2,1)} %copy-done) | copy-start | bytes 18874372
  79.0 8.4 %copy-start.2 = (bf16[8,512,768]{2,1,0:T(8,128)(2,1)S(1)}, bf16[8,512,768]{2,1,0:T(8,128)(2,1)}, u32[]{:S(2)}) copy-start(bf16[8,512,768]{2,1,0:T(8,128)(2,1)} %copy-done) | copy-start | bytes 18874372
  79.6 9.1 %collective-permute-start.2 = (f32[128,768]{1,0:T(8,128)S(1)}, f32[128,768]{1,0:T(8,128)S(1)}, u32[]{:S(2)}, u32[]{:S(2)}) collective-permute-start(f32[128,768]{1,0:T(8,128)S(1)} %get-tuple-element.36), channel_id=1, source_target_pairs={{0,1},{1,0},{2,3},{3,2},{4,5},{5,4},{6,7},{7,6},{8,9},{9,8},{10,11... | collective-permute-start | bytes 1179656 | tf_op jit(solution)/shard_map/ppermute | solution.py:317
  88.7 8.2 %collective-permute-start.3 = (f32[3,128,768]{2,1,0:T(8,128)S(1)}, f32[3,128,768]{2,1,0:T(8,128)S(1)}, u32[]{:S(2)}, u32[]{:S(2)}) collective-permute-start(f32[3,128,768]{2,1,0:T(8,128)S(1)} %get-tuple-element.38), channel_id=1, source_target_pairs={{0,1},{1,0},{2,3},{3,2},{4,5},{5,4},{6,7},{7,6},{8,9},{9,8},{10,11... | collective-permute-start | bytes 3538952 | tf_op jit(solution)/shard_map/ppermute | solution.py:324
  91.0 21.3 %collective-permute-start.5 = (f32[128,768]{1,0:T(8,128)S(1)}, f32[128,768]{1,0:T(8,128)S(1)}, u32[]{:S(2)}, u32[]{:S(2)}) collective-permute-start(f32[128,768]{1,0:T(8,128)S(1)} %shard_map.80), channel_id=1, source_target_pairs={{0,2},{1,7},{2,4},{3,1},{4,6},{5,3},{6,0},{7,5},{8,10},{9,15},{10,... | collective-permute-start | bytes 1179656 | tf_op jit(solution)/shard_map/ppermute | solution.py:323
  97.1 21.7 %collective-permute-start.4 = (f32[128,768]{1,0:T(8,128)S(1)}, f32[128,768]{1,0:T(8,128)S(1)}, u32[]{:S(2)}, u32[]{:S(2)}) collective-permute-start(f32[128,768]{1,0:T(8,128)S(1)} %get-tuple-element.40), channel_id=1, source_target_pairs={{0,6},{1,3},{2,0},{3,5},{4,2},{5,7},{6,4},{7,1},{8,14},{9,11},{10,... | collective-permute-start | bytes 1179656 | tf_op jit(solution)/shard_map/ppermute | solution.py:326
  112.4 12.0 %collective-permute-start.6 = (f32[128,768]{1,0:T(8,128)S(1)}, f32[128,768]{1,0:T(8,128)S(1)}, u32[]{:S(2)}, u32[]{:S(2)}) collective-permute-start(f32[128,768]{1,0:T(8,128)S(1)} %shard_map.83), channel_id=1, source_target_pairs={{0,2},{1,7},{2,4},{3,1},{4,6},{5,3},{6,0},{7,5},{8,10},{9,15},{10,... | collective-permute-start | bytes 1179656 | tf_op jit(solution)/shard_map/ppermute | solution.py:328

commit v3 on v2

--- a/solution.py
+++ b/solution.py
@@ -18,17 +18,17 @@
 CHUNK = ROWS + 1
 HEAD_ROWS = PIECES * CHUNK
 PACKED = PAIRS * CHUNK
+RING = 4
 
 surge_log_factor = math.log(0.6)
 F32 = jnp.float32
 BF16 = jnp.bfloat16
 VMEM_LIMIT = 24 * 1024 * 1024
-TERMS_LIMIT = 60_000_000
-STAGE_LIMIT = 46 * 1024 * 1024
 
 SIDE_GROUPS = [[2 * pair + side for pair in range(PAIRS)] for side in range(2)]
 SIDE_SWAP = [(i, i ^ 1) for i in range(2 * PAIRS)]
 CORE_SWAP = [(i, i ^ 1) for i in range(8)]
+CORE_PAIRS = [[i, i + 1] for i in range(0, 8, 2)]
 ONWARD = [(i, (i + (2 if i % 2 == 0 else 6)) % 8) for i in range(8)]
 BACK = [(i, (i + (6 if i % 2 == 0 else 2)) % 8) for i in range(8)]
 
@@ -37,16 +37,19 @@
     return min(ROWS, HEAD_DIM - ROWS * piece)
 
 
-def call(kernel, outs, args, scalars=0, scratch=(), flops=0, moved=0, space=pltpu.VMEM, limit=VMEM_LIMIT):
+def call(kernel, outs, args, scalars=0, scratch=(), flops=0, moved=0, space=pltpu.VMEM, out_space=None):
     specs = [pl.BlockSpec(memory_space=pltpu.SMEM)] * scalars
     specs += [pl.BlockSpec(memory_space=space)] * (len(args) - scalars)
+    if space is pltpu.HBM:
+        args = args[:scalars] + tuple(pltpu.with_memory_space_constraint(x, space) for x in args[scalars:])
+    shapes = [jax.ShapeDtypeStruct(shape, dtype) if out_space is None else out_space(shape, dtype) for shape, dtype in outs]
     return pl.pallas_call(
         kernel,
-        out_shape=[jax.ShapeDtypeStruct(shape, dtype) for shape, dtype in outs],
+        out_shape=shapes,
         in_specs=specs,
-        out_specs=[pl.BlockSpec(memory_space=pltpu.VMEM)] * len(outs),
+        out_specs=[pl.BlockSpec(memory_space=out_space or pltpu.VMEM)] * len(outs),
         scratch_shapes=list(scratch),
-        compiler_params=pltpu.CompilerParams(vmem_limit_bytes=limit),
+        compiler_params=pltpu.CompilerParams(vmem_limit_bytes=VMEM_LIMIT),
         cost_estimate=pl.CostEstimate(flops=flops, bytes_accessed=moved, transcendentals=0),
     )(*args)
 
@@ -190,24 +193,49 @@
         factor_ref[:, lanes] = jnp.broadcast_to(other[:, head : head + 1], (EVENTS, HEAD_DIM))
 
 
-def stage_kernel(w_hbm, staged_ref, sems):
-    copies = [
-        pltpu.make_async_copy(w_hbm.at[:, pl.ds(block * COLS, COLS)], staged_ref.at[block], sems.at[block])
-        for block in range(D // COLS)
-    ]
-    for copy in copies:
+def widen_kernel(place_ref, w_ref, wide_ref):
+    wide_ref[0] = w_ref[...].astype(F32)
+
+
+def widen_partner_columns(place, w_out):
+    rows = w_out.shape[0] // 2
+    spec = pltpu.PrefetchScalarGridSpec(
+        num_scalar_prefetch=1,
+        grid=(RING, 2),
+        in_specs=[pl.BlockSpec((rows, COLS), lambda t, r, place: (r, 2 * t + 1 - (place[0] & 1)))],
+        out_specs=pl.BlockSpec((1, rows, COLS), lambda t, r, place: (t, r, 0)),
+    )
+    return pl.pallas_call(
+        widen_kernel,
+        grid_spec=spec,
+        out_shape=pltpu.HBM((RING, w_out.shape[0], COLS), F32),
+        compiler_params=pltpu.CompilerParams(vmem_limit_bytes=VMEM_LIMIT),
+        cost_estimate=pl.CostEstimate(flops=0, bytes_accessed=9_500_000, transcendentals=0),
+    )(place, pltpu.with_memory_space_constraint(w_out, pltpu.HBM))
+
+
+def stage_kernel(place_ref, w_hbm, wide_hbm, staged_ref, wide_ref, sems):
+    rows = w_hbm.shape[0]
+    core = place_ref[0] & 1
+    arriving, owned = [], []
+    for t in range(RING):
+        arriving.append(pltpu.make_async_copy(wide_hbm.at[1 - core, t], wide_ref.at[t], sems.at[t]))
+        columns = pl.ds(pl.multiple_of((2 * t + core) * COLS, COLS), COLS)
+        owned.append(
+            pltpu.make_async_copy(
+                w_hbm.at[:, columns], staged_ref.at[t, pl.ds(0, rows)], sems.at[RING + t]
+            )
+        )
+    for copy in arriving + owned:
         copy.start()
-    for copy in copies:
+    for t in range(RING):
+        arriving[t].wait()
+        staged_ref[t, rows:, :] = wide_ref[t].astype(BF16)
+    for copy in owned:
         copy.wait()
 
 
-def block_of(place, far, core):
-    return 2 * (((place >> 1) + far) & 3) + core
-
-
-def first_kernel(
-    place_ref, query_ref, total_ref, factor_ref, other_ref, gain_ref, w_ref, normed_ref, send_ref, mine_ref
-):
+def normed_kernel(query_ref, total_ref, factor_ref, other_ref, gain_ref, normed_ref):
     for head in range(HEADS_DEV):
         lanes = slice(head * HEAD_DIM, (head + 1) * HEAD_DIM)
         total = total_ref[:, lanes] + factor_ref[:, lanes] * times_state(
@@ -215,33 +243,30 @@
         )
         average = jnp.mean(total * total, axis=1, keepdims=True)
         scaled = total * lax.rsqrt(average + 1e-06) * gain_ref[:, lanes]
-        normed_ref[:, lanes] = scaled.astype(BF16)
+        normed_ref[:, lanes] = scaled.astype(BF16).astype(F32)
+
+
+def project(place_ref, own_ref, got_ref, w_ref, out_refs, fars):
     place = place_ref[0]
-    core = place & 1
-    normed = normed_ref[...]
-    send_ref[...] = jnp.dot(normed, w_ref[block_of(place, 2, 1 - core)], preferred_element_type=F32)
-    mine_ref[...] = jnp.dot(normed, w_ref[block_of(place, 2, core)], preferred_element_type=F32)
-
-
-def rest_kernel(place_ref, normed_ref, w_ref, send_ref, mine_ref):
-    place = place_ref[0]
-    core = place & 1
-    normed = normed_ref[...]
-    for target_ref, whose in ((send_ref, 1 - core), (mine_ref, core)):
-        for slot, far in enumerate((3 - 2 * whose, 1 + 2 * whose, 0)):
-            target_ref[slot] = jnp.dot(
-                normed, w_ref[block_of(place, far, whose)], preferred_element_type=F32
-            )
+    normed = jnp.concatenate([own_ref[...].astype(BF16), got_ref[...].astype(BF16)], axis=1)
+    for out_ref, far in zip(out_refs, fars):
+        block = ((place >> 1) + far) & 3
+        out_ref[...] = jnp.dot(normed, w_ref[block], preferred_element_type=F32)
+
+
+def opposite_kernel(place_ref, own_ref, got_ref, w_ref, out_ref):
+    project(place_ref, own_ref, got_ref, w_ref, [out_ref], [2])
+
+
+def rest_kernel(place_ref, own_ref, got_ref, w_ref, behind_ref, ahead_ref, mine_ref):
+    core = place_ref[0] & 1
+    project(
+        place_ref, own_ref, got_ref, w_ref, [behind_ref, ahead_ref, mine_ref], [3 - 2 * core, 1 + 2 * core, 0]
+    )
 
 
 def far_kernel(mine_ref, got_ref, out_ref):
     out_ref[...] = mine_ref[...] + got_ref[...]
-
-
-def near_kernel(mine_ref, got_ref, behind_ref, ahead_ref, own_ref):
-    behind_ref[...] = mine_ref[0] + got_ref[0]
-    ahead_ref[...] = mine_ref[1] + got_ref[1]
-    own_ref[...] = mine_ref[2] + got_ref[2]
 
 
 def final_kernel(one_ref, two_ref, out_ref):
@@ -276,25 +301,33 @@
         flops=70_000_000,
         moved=900_000,
         space=pltpu.HBM,
-        limit=TERMS_LIMIT,
-    )
-    sent, w_out = lax.optimization_barrier((sent, w_out))
+        out_space=pltpu.VMEM,
+    )
+    sent, w_late = lax.optimization_barrier((sent, w_out))
     got = lax.ppermute(sent, "ctx", SIDE_SWAP)
-    (staged,) = call(
-        stage_kernel,
-        [((D // COLS, 512, COLS), BF16)],
-        (w_out,),
-        scratch=[pltpu.SemaphoreType.DMA((D // COLS,))],
-        moved=12_600_000,
-        space=pltpu.HBM,
-        limit=STAGE_LIMIT,
-    )
-    got, staged = lax.optimization_barrier((got, staged))
+    wide = widen_partner_columns(place, w_late)
+    got, wide = lax.optimization_barrier((got, wide))
+    wide_both = lax.all_gather(wide, "tp", axis_index_groups=CORE_PAIRS)
     (pair_terms,) = call(combine_kernel, [packed], (kept, got, decay), flops=200_000, moved=900_000)
     slices = exchange_pieces(pair_terms)
     (states,) = call(scan_kernel, [packed], (side, slices), scalars=1, flops=200_000, moved=600_000)
     own = exchange_pieces(states)
+    own, w_late = lax.optimization_barrier((own, w_late))
     other = lax.ppermute(own, "ctx", SIDE_SWAP)
+    (staged,) = call(
+        stage_kernel,
+        [((RING, 1024, COLS), BF16)],
+        (place, w_late, wide_both),
+        scalars=1,
+        scratch=[
+            pltpu.VMEM((RING, 512, COLS), F32),
+            pltpu.SemaphoreType.DMA((2 * RING,)),
+        ],
+        moved=16_000_000,
+        space=pltpu.HBM,
+        out_space=pltpu.VMEM,
+    )
+    other, staged = lax.optimization_barrier((other, staged))
     inner = ((EVENTS, 512), F32)
     total, factor = call(
         inner_kernel,
@@ -305,24 +338,31 @@
         moved=1_500_000,
     )
     block = ((EVENTS, COLS), F32)
-    three = ((3, EVENTS, COLS), F32)
-    normed, send, mine = call(
-        first_kernel,
-        [((EVENTS, 512), BF16), block, block],
-        (place, queries, total, factor, other, gain, staged),
-        scalars=1,
-        flops=230_000_000,
-        moved=3_500_000,
-    )
-    far_got = lax.ppermute(send, "tp", CORE_SWAP)
-    (far,) = call(far_kernel, [block], (mine, far_got), moved=1_200_000)
-    near_send, near_mine = call(
-        rest_kernel, [three, three], (place, normed, staged), scalars=1, flops=604_000_000, moved=7_500_000
-    )
-    far, near_send = lax.optimization_barrier((far, near_send))
-    ahead_got = lax.ppermute(far, "tp", ONWARD)
-    near_got = lax.ppermute(near_send, "tp", CORE_SWAP)
-    behind, ahead, own_sum = call(near_kernel, [block] * 3, (near_mine, near_got), moved=3_600_000)
+    (normed,) = call(
+        normed_kernel,
+        [inner],
+        (queries, total, factor, other, gain),
+        flops=70_000_000,
+        moved=1_300_000,
+    )
+    normed_got = lax.ppermute(normed, "tp", CORE_SWAP)
+    (opposite,) = call(
+        opposite_kernel,
+        [block],
+        (place, normed, normed_got, staged),
+        scalars=1,
+        flops=200_000_000,
+        moved=2_500_000,
+    )
+    ahead_got = lax.ppermute(opposite, "tp", ONWARD)
+    behind, ahead, own_sum = call(
+        rest_kernel,
+        [block] * 3,
+        (place, normed, normed_got, staged),
+        scalars=1,
+        flops=600_000_000,
+        moved=6_000_000,
+    )
     one = lax.ppermute(behind, "tp", BACK)
     (passed,) = call(far_kernel, [block], (ahead, ahead_got), moved=1_200_000)
     two = lax.ppermute(passed, "tp", ONWARD)

time: 126 us -> 133 us (1.056)
  between operations: 0.26 us -> 13.6 us
  Pallas kernels: 8.51 us -> 15.3 us
  local copies, waits for them, and re-layouts: 5.48 us -> 0.03 us
  waiting for transfers between devices: 22.9 us -> 18.8 us
  starting transfers between devices: 31.5 us -> 28.4 us
    pallas_call x12, Pallas kernels: 8.51 us -> 15.3 us  [the longest x11 8.56 us: call(): pl.pallas_call(kernel, out_shape=shapes, in_specs=specs, out_specs=[pl.Bl...]
    unnamed x22 -> x12, local copies, waits for them, and re-layouts: 5.48 us -> 0.03 us
    ppermute x1, waiting for transfers between devices: 3.53 us -> 0.03 us  [body(): other = lax.ppermute(own, 'ctx', SIDE_SWAP)]
    ppermute x3 -> x2, starting transfers between devices: 15.9 us -> 13 us  [the longest x1 7.67 us: body(): normed_got = lax.ppermute(normed, 'tp', CORE_SWAP)]
    ppermute x3 -> x2, waiting for transfers between devices: 13.9 us -> 13.1 us  [the longest x1 12 us: body(): ahead_got = lax.ppermute(opposite, 'tp', ONWARD)]
  transfers between devices with their start and end apart: 7 -> 7, of which waited for: 4 -> 3; matrix products, arithmetic and copies ran while one was open for 0% -> 0% of each run, Pallas kernels for 4% -> 9%
where the time goes in v3:
time: 133 us; the launch traced here: 131 us
  blocking collectives  55.1 us (41%)
  starting transfers between devices  28.4 us (21%)
  waiting for transfers between devices  18.8 us (14%)
  Pallas kernels  15.3 us (12%)
  between operations  13.6 us (10%)
    all_to_all x2, blocking collectives, exchange_pieces(): pieces = lax.all_to_all(pieces, 'ctx', 0, 0, axis_index_groups=SIDE_GROUPS)  55.1 us
    ppermute x1, waiting for transfers between devices, body(): ahead_got = lax.ppermute(opposite, 'tp', ONWARD)  12 us
    pallas_call x11, Pallas kernels, call(): pl.pallas_call(kernel, out_shape=shapes, in_specs=specs, out_specs=[pl.Bl...  8.56 us
    ppermute x1, starting transfers between devices, body(): normed_got = lax.ppermute(normed, 'tp', CORE_SWAP)  7.67 us
    pallas_call x1, Pallas kernels, widen_partner_columns(): pl.pallas_call(widen_kernel, grid_spec=spec, out_shape=pltpu.HBM((RING, w...  6.7 us
    ppermute x1, starting transfers between devices, body(): two = lax.ppermute(passed, 'tp', ONWARD)  6.5 us
    ppermute x1, waiting for transfers between devices, body(): two = lax.ppermute(passed, 'tp', ONWARD)  5.6 us
    ppermute x1, starting transfers between devices, body(): ahead_got = lax.ppermute(opposite, 'tp', ONWARD)  5.36 us
  transfers between devices with their start and end apart: 7, of which 3 were waited for; matrix products, arithmetic and copies ran while one was open for 0% of the time, Pallas kernels for 9%

profile of v3, /device:TPU:1, one launch (start us, length us, event | category | flops | bytes accessed | tf_op | source)
XLA Modules:
  0.0 131.2 jit_solution(15294973372682975500)
XLA Ops:
  6.5 1.7 %shard_map.73 = (f32[576,128]{1,0:T(8,128)S(1)}, f32[576,128]{1,0:T(8,128)S(1)}, f32[4,128]{1,0:T(4,128)S(1)}) custom-call(s32[1]{0:T(128)} %bitcast.1.side_ref, bf16[128,512]{1,0:T(8,128)(2,1)} %key_ref.1, bf16[128,512]{1,0:T(8,128)(2,1)} %value_ref.1, f32[4,128]{1,0:T(4,128)} %log_ref.1, s32[1,128]{1,0:T(1,128)} %bitcast.15), custom_call_target="tpu_custom_call" | custom-call | flops 70000000 | bytes 900000 | tf_op jit(solution)/shard_map/pallas_call | solution.py:46
  8.2 4.0 %collective-permute-start = (f32[576,128]{1,0:T(8,128)S(1)}, f32[576,128]{1,0:T(8,128)S(1)}, u32[]{:S(2)}, u32[]{:S(2)}) collective-permute-start(f32[576,128]{1,0:T(8,128)S(1)} %get-tuple-element.22), channel_id=1, source_target_pairs={{0,8},{8,0},{16,24},{24,16},{32,40},{40,32},{48,56},{56,48},{64,72... | collective-permute-start | bytes 884744 | tf_op jit(solution)/shard_map/ppermute | solution.py:307
  12.3 6.7 %shard_map.74 = f32[4,512,768]{2,1,0:T(8,128)} custom-call(s32[1]{0:T(128)} %bitcast.place_ref, bf16[512,6144]{1,0:T(8,128)(2,1)} %w_hbm), custom_call_target="tpu_custom_call" | custom-call | bytes 9500000 | tf_op jit(solution)/shard_map/pallas_call | solution.py:208
  19.0 0.0 all-gather.3.cloned.1.call-update
  19.1 33.4 %all_to_all.10 = f32[48,3,4,128]{3,2,1,0:T(4,128)S(1)} all-to-all(f32[48,3,4,128]{3,2,1,0:T(4,128)S(1)} %bitcast.11), channel_id=1, replica_groups={{0,16,32,48,64,80,96,112,128,144,160,176,192,208,224,240,256,272,288,30..., dimensions={0} | all-to-all | bytes 589824 | tf_op jit(solution)/shard_map/all_to_all | solution.py:278
  52.5 0.1 shard_map.76
  52.6 21.8 %all_to_all.11 = f32[48,3,4,128]{3,2,1,0:T(4,128)S(1)} all-to-all(f32[48,3,4,128]{3,2,1,0:T(4,128)S(1)} %bitcast.13), channel_id=1, replica_groups={{0,16,32,48,64,80,96,112,128,144,160,176,192,208,224,240,256,272,288,30..., dimensions={0} | all-to-all | bytes 589824 | tf_op jit(solution)/shard_map/all_to_all | solution.py:278
  74.3 2.9 %collective-permute-start.1 = (f32[576,128]{1,0:T(8,128)S(1)}, f32[576,128]{1,0:T(8,128)S(1)}, u32[]{:S(2)}, u32[]{:S(2)}) collective-permute-start(f32[576,128]{1,0:T(8,128)S(1)} %bitcast.9), channel_id=1, source_target_pairs={{0,8},{8,0},{16,24},{24,16},{32,40},{40,32},{48,56},{56,48},{64,72... | collective-permute-start | bytes 884744 | tf_op jit(solution)/shard_map/ppermute | solution.py:316
  77.3 0.7 shard_map.77
  77.9 0.0 all-gather.3.cloned.1.call-done
  78.0 0.0 copy-start.4
  78.0 3.8 %shard_map.78.w_ref = bf16[4,1024,768]{2,1,0:T(8,128)(2,1)S(1)} custom-call(s32[1]{0:T(128)} %bitcast.place_ref, bf16[512,6144]{1,0:T(8,128)(2,1)} %w_hbm, f32[2,4,512,768]{3,2,1,0:T(8,128)} %bitcast.17), custom_call_target="tpu_custom_call" | custom-call | bytes 16000000 | tf_op jit(solution)/shard_map/pallas_call | solution.py:46
  81.8 0.0 collective-permute-done.1.other_ref
  81.8 0.3 shard_map.79.own_ref
  82.1 7.7 %collective-permute-start.2 = (f32[128,512]{1,0:T(8,128)S(1)}, f32[128,512]{1,0:T(8,128)S(1)}, u32[]{:S(2)}, u32[]{:S(2)}) collective-permute-start(f32[128,512]{1,0:T(8,128)S(1)} %shard_map.79.own_ref), channel_id=1, source_target_pairs={{0,1},{1,0},{2,3},{3,2},{4,5},{5,4},{6,7},{7,6},{8,9},{9,8},{10,11... | collective-permute-start | bytes 786440 | tf_op jit(solution)/shard_map/ppermute | solution.py:348
  89.8 1.1 collective-permute-done.2.got_ref
  90.9 0.4 shard_map.82
  91.3 5.4 %collective-permute-start.4 = (f32[128,768]{1,0:T(8,128)S(1)}, f32[128,768]{1,0:T(8,128)S(1)}, u32[]{:S(2)}, u32[]{:S(2)}) collective-permute-start(f32[128,768]{1,0:T(8,128)S(1)} %shard_map.82), channel_id=1, source_target_pairs={{0,2},{1,7},{2,4},{3,1},{4,6},{5,3},{6,0},{7,5},{8,10},{9,15},{10,... | collective-permute-start | bytes 1179656 | tf_op jit(solution)/shard_map/ppermute | solution.py:357
  96.7 0.8 shard_map.80
  97.5 1.9 %collective-permute-start.3 = (f32[128,768]{1,0:T(8,128)S(1)}, f32[128,768]{1,0:T(8,128)S(1)}, u32[]{:S(2)}, u32[]{:S(2)}) collective-permute-start(f32[128,768]{1,0:T(8,128)S(1)} %get-tuple-element.35), channel_id=1, source_target_pairs={{0,6},{1,3},{2,0},{3,5},{4,2},{5,7},{6,4},{7,1},{8,14},{9,11},{10,... | collective-permute-start | bytes 1179656 | tf_op jit(solution)/shard_map/ppermute | solution.py:366
  99.4 12.0 %collective-permute-done.4.got_ref = f32[128,768]{1,0:T(8,128)S(1)} collective-permute-done((f32[128,768]{1,0:T(8,128)S(1)}, f32[128,768]{1,0:T(8,128)S(1)}, u32[]{:S(2)}, u32[]{:S(2)}) %collective-permute-start.4) | collective-permute-done | bytes 393248 | tf_op jit(solution)/shard_map/ppermute | solution.py:357
  111.5 6.5 %collective-permute-start.5 = (f32[128,768]{1,0:T(8,128)S(1)}, f32[128,768]{1,0:T(8,128)S(1)}, u32[]{:S(2)}, u32[]{:S(2)}) collective-permute-start(f32[128,768]{1,0:T(8,128)S(1)} %shard_map.83), channel_id=1, source_target_pairs={{0,2},{1,7},{2,4},{3,1},{4,6},{5,3},{6,0},{7,5},{8,10},{9,15},{10,... | collective-permute-start | bytes 1179656 | tf_op jit(solution)/shard_map/ppermute | solution.py:368
  118.0 5.6 %collective-permute-done.5.two_ref = f32[128,768]{1,0:T(8,128)S(1)} collective-permute-done((f32[128,768]{1,0:T(8,128)S(1)}, f32[128,768]{1,0:T(8,128)S(1)}, u32[]{:S(2)}, u32[]{:S(2)}) %collective-permute-start.5) | collective-permute-done | bytes 393248 | tf_op jit(solution)/shard_map/ppermute | solution.py:368
  123.6 0.7 shard_map.84
  (17 shorter events, 0.1 us)
Async XLA Ops:
  6.5 71.4 %all-gather.3.cloned.1.call-start = ((), (), s32[]{:S(2)}) async-start(), calls=%async_computation.2 | async-start | bytes 18874368 | tf_op jit(solution)/shard_map/all_gather | solution.py:310
  8.2 10.8 %collective-permute-start = (f32[576,128]{1,0:T(8,128)S(1)}, f32[576,128]{1,0:T(8,128)S(1)}, u32[]{:S(2)}, u32[]{:S(2)}) collective-permute-start(f32[576,128]{1,0:T(8,128)S(1)} %get-tuple-element.22), channel_id=1, source_target_pairs={{0,8},{8,0},{16,24},{24,16},{32,40},{40,32},{48,56},{56,48},{64,72... | collective-permute-start | bytes 884744 | tf_op jit(solution)/shard_map/ppermute | solution.py:307
  19.0 58.2 %copy-start = (bf16[128,512]{1,0:T(8,128)(2,1)S(1)}, bf16[128,512]{1,0:T(8,128)(2,1)}, u32[]{:S(2)}) copy-start(bf16[128,512]{1,0:T(8,128)(2,1)} %query_ref.3) | copy-start | bytes 393220
  19.0 58.2 %copy-start.1 = (bf16[128,512]{1,0:T(8,128)(2,1)S(1)}, bf16[128,512]{1,0:T(8,128)(2,1)}, u32[]{:S(2)}) copy-start(bf16[128,512]{1,0:T(8,128)(2,1)} %key_ref.1) | copy-start | bytes 393220
  19.0 58.3 %copy-start.2 = (bf16[128,512]{1,0:T(8,128)(2,1)S(1)}, bf16[128,512]{1,0:T(8,128)(2,1)}, u32[]{:S(2)}) copy-start(bf16[128,512]{1,0:T(8,128)(2,1)} %value_ref.1) | copy-start | bytes 393220
  19.0 58.3 %copy-start.3 = (f32[4,128]{1,0:T(4,128)S(1)}, f32[4,128]{1,0:T(4,128)}, u32[]{:S(2)}) copy-start(f32[4,128]{1,0:T(4,128)} %log_ref.1) | copy-start | bytes 6148
  19.0 58.3 %copy-start.5 = (s32[128]{0:T(128)S(1)}, s32[128]{0:T(128)}, u32[]{:S(2)}) copy-start(s32[128]{0:T(128)} %param.11) | copy-start | bytes 1540
  74.3 7.5 %collective-permute-start.1 = (f32[576,128]{1,0:T(8,128)S(1)}, f32[576,128]{1,0:T(8,128)S(1)}, u32[]{:S(2)}, u32[]{:S(2)}) collective-permute-start(f32[576,128]{1,0:T(8,128)S(1)} %bitcast.9), channel_id=1, source_target_pairs={{0,8},{8,0},{16,24},{24,16},{32,40},{40,32},{48,56},{56,48},{64,72... | collective-permute-start | bytes 884744 | tf_op jit(solution)/shard_map/ppermute | solution.py:316
  78.0 3.8 %copy-start.4 = (f32[512]{0:T(512)S(1)}, f32[512]{0:T(512)}, u32[]{:S(2)}) copy-start(f32[512]{0:T(512)} %param.12) | copy-start | bytes 6148
  82.1 8.8 %collective-permute-start.2 = (f32[128,512]{1,0:T(8,128)S(1)}, f32[128,512]{1,0:T(8,128)S(1)}, u32[]{:S(2)}, u32[]{:S(2)}) collective-permute-start(f32[128,512]{1,0:T(8,128)S(1)} %shard_map.79.own_ref), channel_id=1, source_target_pairs={{0,1},{1,0},{2,3},{3,2},{4,5},{5,4},{6,7},{7,6},{8,9},{9,8},{10,11... | collective-permute-start | bytes 786440 | tf_op jit(solution)/shard_map/ppermute | solution.py:348
  91.3 20.1 %collective-permute-start.4 = (f32[128,768]{1,0:T(8,128)S(1)}, f32[128,768]{1,0:T(8,128)S(1)}, u32[]{:S(2)}, u32[]{:S(2)}) collective-permute-start(f32[128,768]{1,0:T(8,128)S(1)} %shard_map.82), channel_id=1, source_target_pairs={{0,2},{1,7},{2,4},{3,1},{4,6},{5,3},{6,0},{7,5},{8,10},{9,15},{10,... | collective-permute-start | bytes 1179656 | tf_op jit(solution)/shard_map/ppermute | solution.py:357
  97.5 20.5 %collective-permute-start.3 = (f32[128,768]{1,0:T(8,128)S(1)}, f32[128,768]{1,0:T(8,128)S(1)}, u32[]{:S(2)}, u32[]{:S(2)}) collective-permute-start(f32[128,768]{1,0:T(8,128)S(1)} %get-tuple-element.35), channel_id=1, source_target_pairs={{0,6},{1,3},{2,0},{3,5},{4,2},{5,7},{6,4},{7,1},{8,14},{9,11},{10,... | collective-permute-start | bytes 1179656 | tf_op jit(solution)/shard_map/ppermute | solution.py:366
  111.5 12.2 %collective-permute-start.5 = (f32[128,768]{1,0:T(8,128)S(1)}, f32[128,768]{1,0:T(8,128)S(1)}, u32[]{:S(2)}, u32[]{:S(2)}) collective-permute-start(f32[128,768]{1,0:T(8,128)S(1)} %shard_map.83), channel_id=1, source_target_pairs={{0,2},{1,7},{2,4},{3,1},{4,6},{5,3},{6,0},{7,5},{8,10},{9,15},{10,... | collective-permute-start | bytes 1179656 | tf_op jit(solution)/shard_map/ppermute | solution.py:368
Sparse Core Ops, SparseCore 0:
  19.2 45.3 all-gather.2

commit v4 on v2

--- a/solution.py
+++ b/solution.py
@@ -23,12 +23,12 @@
 F32 = jnp.float32
 BF16 = jnp.bfloat16
 VMEM_LIMIT = 24 * 1024 * 1024
-TERMS_LIMIT = 60_000_000
-STAGE_LIMIT = 46 * 1024 * 1024
 
 SIDE_GROUPS = [[2 * pair + side for pair in range(PAIRS)] for side in range(2)]
 SIDE_SWAP = [(i, i ^ 1) for i in range(2 * PAIRS)]
+SIDE_PAIRS = [[i, i + 1] for i in range(0, 2 * PAIRS, 2)]
 CORE_SWAP = [(i, i ^ 1) for i in range(8)]
+CORE_PAIRS = [[i, i + 1] for i in range(0, 8, 2)]
 ONWARD = [(i, (i + (2 if i % 2 == 0 else 6)) % 8) for i in range(8)]
 BACK = [(i, (i + (6 if i % 2 == 0 else 2)) % 8) for i in range(8)]
 
@@ -37,16 +37,19 @@
     return min(ROWS, HEAD_DIM - ROWS * piece)
 
 
-def call(kernel, outs, args, scalars=0, scratch=(), flops=0, moved=0, space=pltpu.VMEM, limit=VMEM_LIMIT):
+def call(kernel, outs, args, scalars=0, scratch=(), flops=0, moved=0, space=pltpu.VMEM, out_space=None):
     specs = [pl.BlockSpec(memory_space=pltpu.SMEM)] * scalars
     specs += [pl.BlockSpec(memory_space=space)] * (len(args) - scalars)
+    if space is pltpu.HBM:
+        args = args[:scalars] + tuple(pltpu.with_memory_space_constraint(x, space) for x in args[scalars:])
+    shapes = [(out_space or jax.ShapeDtypeStruct)(shape, dtype) for shape, dtype in outs]
     return pl.pallas_call(
         kernel,
-        out_shape=[jax.ShapeDtypeStruct(shape, dtype) for shape, dtype in outs],
+        out_shape=shapes,
         in_specs=specs,
-        out_specs=[pl.BlockSpec(memory_space=pltpu.VMEM)] * len(outs),
+        out_specs=[pl.BlockSpec(memory_space=out_space or pltpu.VMEM)] * len(outs),
         scratch_shapes=list(scratch),
-        compiler_params=pltpu.CompilerParams(vmem_limit_bytes=limit),
+        compiler_params=pltpu.CompilerParams(vmem_limit_bytes=VMEM_LIMIT),
         cost_estimate=pl.CostEstimate(flops=flops, bytes_accessed=moved, transcendentals=0),
     )(*args)
 
@@ -130,7 +133,8 @@
             sent_ref[first + ROWS : first + CHUNK, :] = whole_row
 
 
-def combine_kernel(kept_ref, got_ref, decay_ref, out_ref):
+def combine_kernel(side_ref, kept_ref, both_ref, decay_ref, out_ref, got_ref):
+    got_ref[...] = both_ref[1 - side_ref[0]]
     for head in range(HEADS_DEV):
         rows = slice(head * HEAD_ROWS, (head + 1) * HEAD_ROWS)
         out_ref[rows, :] = kept_ref[rows, :] + decay_ref[head : head + 1, :] * got_ref[rows, :]
@@ -206,7 +210,18 @@
 
 
 def first_kernel(
-    place_ref, query_ref, total_ref, factor_ref, other_ref, gain_ref, w_ref, normed_ref, send_ref, mine_ref
+    place_ref,
+    query_ref,
+    total_ref,
+    factor_ref,
+    other_ref,
+    gain_ref,
+    w_ref,
+    normed_ref,
+    opposite_send_ref,
+    opposite_ref,
+    behind_send_ref,
+    behind_ref,
 ):
     for head in range(HEADS_DEV):
         lanes = slice(head * HEAD_DIM, (head + 1) * HEAD_DIM)
@@ -219,29 +234,34 @@
     place = place_ref[0]
     core = place & 1
     normed = normed_ref[...]
-    send_ref[...] = jnp.dot(normed, w_ref[block_of(place, 2, 1 - core)], preferred_element_type=F32)
-    mine_ref[...] = jnp.dot(normed, w_ref[block_of(place, 2, core)], preferred_element_type=F32)
-
-
-def rest_kernel(place_ref, normed_ref, w_ref, send_ref, mine_ref):
+    for out_ref, far, whose in (
+        (opposite_send_ref, 2, 1 - core),
+        (opposite_ref, 2, core),
+        (behind_send_ref, 1 + 2 * core, 1 - core),
+        (behind_ref, 3 - 2 * core, core),
+    ):
+        out_ref[...] = jnp.dot(normed, w_ref[block_of(place, far, whose)], preferred_element_type=F32)
+
+
+def rest_kernel(place_ref, normed_ref, w_ref, ahead_send_ref, ahead_ref, own_send_ref, own_ref):
     place = place_ref[0]
     core = place & 1
     normed = normed_ref[...]
-    for target_ref, whose in ((send_ref, 1 - core), (mine_ref, core)):
-        for slot, far in enumerate((3 - 2 * whose, 1 + 2 * whose, 0)):
-            target_ref[slot] = jnp.dot(
-                normed, w_ref[block_of(place, far, whose)], preferred_element_type=F32
-            )
-
-
-def far_kernel(mine_ref, got_ref, out_ref):
-    out_ref[...] = mine_ref[...] + got_ref[...]
-
-
-def near_kernel(mine_ref, got_ref, behind_ref, ahead_ref, own_ref):
-    behind_ref[...] = mine_ref[0] + got_ref[0]
-    ahead_ref[...] = mine_ref[1] + got_ref[1]
-    own_ref[...] = mine_ref[2] + got_ref[2]
+    for out_ref, far, whose in (
+        (ahead_send_ref, 3 - 2 * core, 1 - core),
+        (ahead_ref, 1 + 2 * core, core),
+        (own_send_ref, 0, 1 - core),
+        (own_ref, 0, core),
+    ):
+        out_ref[...] = jnp.dot(normed, w_ref[block_of(place, far, whose)], preferred_element_type=F32)
+
+
+def core_sum_kernel(place_ref, mine_ref, both_ref, out_ref):
+    out_ref[...] = mine_ref[...] + both_ref[1 - (place_ref[0] & 1)]
+
+
+def three_kernel(place_ref, mine_ref, both_ref, more_ref, out_ref):
+    out_ref[...] = mine_ref[...] + both_ref[1 - (place_ref[0] & 1)] + more_ref[...]
 
 
 def final_kernel(one_ref, two_ref, out_ref):
@@ -276,25 +296,27 @@
         flops=70_000_000,
         moved=900_000,
         space=pltpu.HBM,
-        limit=TERMS_LIMIT,
-    )
-    sent, w_out = lax.optimization_barrier((sent, w_out))
-    got = lax.ppermute(sent, "ctx", SIDE_SWAP)
+        out_space=pltpu.VMEM,
+    )
+    both = lax.all_gather(sent, "ctx", axis_index_groups=SIDE_PAIRS)
+    pair_terms, got = call(
+        combine_kernel, [packed, packed], (side, kept, both, decay), scalars=1, flops=200_000, moved=1_500_000
+    )
+    slices = exchange_pieces(pair_terms)
+    (states,) = call(scan_kernel, [packed], (side, slices), scalars=1, flops=200_000, moved=600_000)
+    own = exchange_pieces(states)
+    own, w_late = lax.optimization_barrier((own, w_out))
+    other = lax.ppermute(own, "ctx", SIDE_SWAP)
     (staged,) = call(
         stage_kernel,
         [((D // COLS, 512, COLS), BF16)],
-        (w_out,),
+        (w_late,),
         scratch=[pltpu.SemaphoreType.DMA((D // COLS,))],
         moved=12_600_000,
         space=pltpu.HBM,
-        limit=STAGE_LIMIT,
-    )
-    got, staged = lax.optimization_barrier((got, staged))
-    (pair_terms,) = call(combine_kernel, [packed], (kept, got, decay), flops=200_000, moved=900_000)
-    slices = exchange_pieces(pair_terms)
-    (states,) = call(scan_kernel, [packed], (side, slices), scalars=1, flops=200_000, moved=600_000)
-    own = exchange_pieces(states)
-    other = lax.ppermute(own, "ctx", SIDE_SWAP)
+        out_space=pltpu.VMEM,
+    )
+    other, staged = lax.optimization_barrier((other, staged))
     inner = ((EVENTS, 512), F32)
     total, factor = call(
         inner_kernel,
@@ -305,28 +327,35 @@
         moved=1_500_000,
     )
     block = ((EVENTS, COLS), F32)
-    three = ((3, EVENTS, COLS), F32)
-    normed, send, mine = call(
+    two_blocks = ((2, EVENTS, COLS), F32)
+    normed, opposite_send, opposite_mine, behind_send, behind_mine = call(
         first_kernel,
-        [((EVENTS, 512), BF16), block, block],
+        [((EVENTS, 512), BF16)] + [block] * 4,
         (place, queries, total, factor, other, gain, staged),
         scalars=1,
-        flops=230_000_000,
-        moved=3_500_000,
-    )
-    far_got = lax.ppermute(send, "tp", CORE_SWAP)
-    (far,) = call(far_kernel, [block], (mine, far_got), moved=1_200_000)
-    near_send, near_mine = call(
-        rest_kernel, [three, three], (place, normed, staged), scalars=1, flops=604_000_000, moved=7_500_000
-    )
-    far, near_send = lax.optimization_barrier((far, near_send))
-    ahead_got = lax.ppermute(far, "tp", ONWARD)
-    near_got = lax.ppermute(near_send, "tp", CORE_SWAP)
-    behind, ahead, own_sum = call(near_kernel, [block] * 3, (near_mine, near_got), moved=3_600_000)
+        flops=430_000_000,
+        moved=6_000_000,
+    )
+
+    def core_sum(mine, both):
+        return call(core_sum_kernel, [block], (place, mine, both), scalars=1)[0]
+
+    opposite_both = lax.all_gather(opposite_send, "tp", axis_index_groups=CORE_PAIRS)
+    opposite = core_sum(opposite_mine, opposite_both)
+    opposite, behind_send = lax.optimization_barrier((opposite, behind_send))
+    ahead_got = lax.ppermute(opposite, "tp", ONWARD)
+    behind_both = lax.all_gather(behind_send, "tp", axis_index_groups=CORE_PAIRS)
+    behind_both, normed = lax.optimization_barrier((behind_both, normed))
+    behind = core_sum(behind_mine, behind_both)
     one = lax.ppermute(behind, "tp", BACK)
-    (passed,) = call(far_kernel, [block], (ahead, ahead_got), moved=1_200_000)
+    ahead_send, ahead_mine, own_send, own_mine = call(
+        rest_kernel, [block] * 4, (place, normed, staged), scalars=1, flops=400_000_000, moved=5_000_000
+    )
+    ahead_both = lax.all_gather(ahead_send, "tp", axis_index_groups=CORE_PAIRS)
+    own_both = lax.all_gather(own_send, "tp", axis_index_groups=CORE_PAIRS)
+    (passed,) = call(three_kernel, [block], (place, ahead_mine, ahead_both, ahead_got), scalars=1)
     two = lax.ppermute(passed, "tp", ONWARD)
-    (own_and_one,) = call(far_kernel, [block], (own_sum, one), moved=1_200_000)
+    (own_and_one,) = call(three_kernel, [block], (place, own_mine, own_both, one), scalars=1, moved=1_600_000)
     (out,) = call(final_kernel, [((EVENTS, COLS), BF16)], (own_and_one, two), moved=1_000_000)
     return out
 

time: 126 us -> 118 us (0.937); the launches traced: 125 us -> 115 us
  blocking collectives: 56.3 us -> 81.6 us
  waiting for transfers between devices: 22.9 us -> 5.48 us
  starting transfers between devices: 31.5 us -> 20.3 us
  local copies, waits for them, and re-layouts: 5.48 us -> 0.04 us
    all_gather x0 -> x5, blocking collectives: none -> 24.1 us  [the longest x1 7.55 us: body(): lax.all_gather(opposite_send, 'tp', axis_index_groups=CORE_PAIRS)]
    ppermute x4 -> x1, starting transfers between devices: 20.1 us -> 5.88 us  [body(): ahead_got = lax.ppermute(opposite, 'tp', ONWARD)]
    ppermute x4 -> x1, waiting for transfers between devices: 13.9 us -> 0.02 us  [body(): ahead_got = lax.ppermute(opposite, 'tp', ONWARD)]
    unnamed x22 -> x12, local copies, waits for them, and re-layouts: 5.48 us -> 0.04 us
    ppermute x1, waiting for transfers between devices: 3.53 us -> 0.45 us  [body(): other = lax.ppermute(own, 'ctx', SIDE_SWAP)]
    ppermute x1, starting transfers between devices: 1.92 us -> 4.05 us  [body(): one = lax.ppermute(behind, 'tp', BACK)]
  transfers between devices with their start and end apart: 7 -> 4, of which waited for: 4 -> 2; matrix products, arithmetic and copies ran while one was open for 0% -> 0% of each run, Pallas kernels for 4% -> 4%
where the time goes in v4:
time: 118 us; the launch traced here: 115 us
  blocking collectives  81.6 us (69%)
  starting transfers between devices  20.3 us (17%)
  Pallas kernels  7.83 us (7%)
  waiting for transfers between devices  5.48 us (5%)
    all_to_all x2, blocking collectives, exchange_pieces(): pieces = lax.all_to_all(pieces, 'ctx', 0, 0, axis_index_groups=SIDE_GROUPS)  57.5 us
    pallas_call x12, Pallas kernels, call(): pl.pallas_call(kernel, out_shape=shapes, in_specs=specs, out_specs=[pl.Bl...  7.83 us
    all_gather x1, blocking collectives, body(): lax.all_gather(opposite_send, 'tp', axis_index_groups=CORE_PAIRS)  7.55 us
    ppermute x1, starting transfers between devices, body(): two = lax.ppermute(passed, 'tp', ONWARD)  7.16 us
    all_gather x1, blocking collectives, body(): both = lax.all_gather(sent, 'ctx', axis_index_groups=SIDE_PAIRS)  6.91 us
    ppermute x1, starting transfers between devices, body(): ahead_got = lax.ppermute(opposite, 'tp', ONWARD)  5.88 us
    ppermute x1, waiting for transfers between devices, body(): two = lax.ppermute(passed, 'tp', ONWARD)  5 us
    all_gather x1, blocking collectives, body(): own_both = lax.all_gather(own_send, 'tp', axis_index_groups=CORE_PAIRS)  4.93 us
  transfers between devices with their start and end apart: 4, of which 2 were waited for; matrix products, arithmetic and copies ran while one was open for 0% of the time, Pallas kernels for 4%

profile of v4, /device:TPU:1, one launch (start us, length us, event | category | flops | bytes accessed | tf_op | source)
XLA Modules:
  0.0 115.4 jit_solution(14835433267491912330)
XLA Ops:
  0.0 1.7 %shard_map.73 = (f32[576,128]{1,0:T(8,128)S(1)}, f32[576,128]{1,0:T(8,128)S(1)}, f32[4,128]{1,0:T(4,128)S(1)}) custom-call(s32[1]{0:T(128)} %bitcast.1.side_ref, bf16[128,512]{1,0:T(8,128)(2,1)} %key_ref.1, bf16[128,512]{1,0:T(8,128)(2,1)} %value_ref.1, f32[4,128]{1,0:T(4,128)} %log_ref.1, s32[1,128]{1,0:T(1,128)} %bitcast.23), custom_call_target="tpu_custom_call" | custom-call | flops 70000000 | bytes 900000 | tf_op jit(solution)/shard_map/pallas_call | solution.py:46
  1.7 6.9 %all-gather = f32[1152,128]{1,0:T(8,128)S(1)} all-gather(f32[576,128]{1,0:T(8,128)S(1)} %get-tuple-element.30), channel_id=2, replica_groups={{0,8},{16,24},{32,40},{48,56},{64,72},{80,88},{96,104},{112,120},{128,1..., dimensions={0}, use_global_device_ids=true | all-gather | bytes 884736 | tf_op jit(solution)/shard_map/all_gather | solution.py:301
  8.6 0.1 shard_map.74
  8.7 35.3 %all_to_all.10 = f32[48,3,4,128]{3,2,1,0:T(4,128)S(1)} all-to-all(f32[48,3,4,128]{3,2,1,0:T(4,128)S(1)} %bitcast.22), channel_id=1, replica_groups={{0,16,32,48,64,80,96,112,128,144,160,176,192,208,224,240,256,272,288,30..., dimensions={0} | all-to-all | bytes 589824 | tf_op jit(solution)/shard_map/all_to_all | solution.py:273
  44.0 0.1 shard_map.75
  44.1 22.2 %all_to_all.11 = f32[48,3,4,128]{3,2,1,0:T(4,128)S(1)} all-to-all(f32[48,3,4,128]{3,2,1,0:T(4,128)S(1)} %bitcast.21), channel_id=1, replica_groups={{0,16,32,48,64,80,96,112,128,144,160,176,192,208,224,240,256,272,288,30..., dimensions={0} | all-to-all | bytes 589824 | tf_op jit(solution)/shard_map/all_to_all | solution.py:273
  66.3 3.2 %collective-permute-start = (f32[576,128]{1,0:T(8,128)S(1)}, f32[576,128]{1,0:T(8,128)S(1)}, u32[]{:S(2)}, u32[]{:S(2)}) collective-permute-start(f32[576,128]{1,0:T(8,128)S(1)} %bitcast.18), channel_id=1, source_target_pairs={{0,8},{8,0},{16,24},{24,16},{32,40},{40,32},{48,56},{56,48},{64,72... | collective-permute-start | bytes 884744 | tf_op jit(solution)/shard_map/ppermute | solution.py:309
  69.5 3.0 %shard_map.77.w_ref = bf16[8,512,768]{2,1,0:T(8,128)(2,1)S(1)} custom-call(bf16[512,6144]{1,0:T(8,128)(2,1)} %w_hbm), custom_call_target="tpu_custom_call" | custom-call | bytes 12600000 | tf_op jit(solution)/shard_map/pallas_call | solution.py:46
  72.6 0.7 shard_map.76
  73.3 0.5 collective-permute-done.other_ref
  73.7 0.8 shard_map.78
  74.5 7.6 %all-gather.1 = f32[256,768]{1,0:T(8,128)S(1)} all-gather(f32[128,768]{1,0:T(8,128)S(1)} %get-tuple-element.41), channel_id=3, replica_groups={{0,1},{2,3},{4,5},{6,7},{8,9},{10,11},{12,13},{14,15},{16,17},{18,19},{..., dimensions={0}, use_global_device_ids=true | all-gather | bytes 1179648 | tf_op jit(solution)/shard_map/all_gather | solution.py:343
  82.1 5.9 %collective-permute-start.2 = (f32[128,768]{1,0:T(8,128)S(1)}, f32[128,768]{1,0:T(8,128)S(1)}, u32[]{:S(2)}, u32[]{:S(2)}) collective-permute-start(f32[128,768]{1,0:T(8,128)S(1)} %shard_map.79), channel_id=1, source_target_pairs={{0,2},{1,7},{2,4},{3,1},{4,6},{5,3},{6,0},{7,5},{8,10},{9,15},{10,... | collective-permute-start | bytes 1179656 | tf_op jit(solution)/shard_map/ppermute | solution.py:346
  88.0 2.4 %all-gather.2 = f32[256,768]{1,0:T(8,128)S(1)} all-gather(f32[128,768]{1,0:T(8,128)S(1)} %get-tuple-element.43), channel_id=4, replica_groups={{0,1},{2,3},{4,5},{6,7},{8,9},{10,11},{12,13},{14,15},{16,17},{18,19},{..., dimensions={0}, use_global_device_ids=true | all-gather | bytes 1179648 | tf_op jit(solution)/shard_map/all_gather | solution.py:347
  90.4 4.0 %collective-permute-start.1 = (f32[128,768]{1,0:T(8,128)S(1)}, f32[128,768]{1,0:T(8,128)S(1)}, u32[]{:S(2)}, u32[]{:S(2)}) collective-permute-start(f32[128,768]{1,0:T(8,128)S(1)} %shard_map.81), channel_id=1, source_target_pairs={{0,6},{1,3},{2,0},{3,5},{4,2},{5,7},{6,4},{7,1},{8,14},{9,11},{10,... | collective-permute-start | bytes 1179656 | tf_op jit(solution)/shard_map/ppermute | solution.py:350
  94.5 0.6 shard_map.80
  95.1 2.4 %all-gather.4 = f32[256,768]{1,0:T(8,128)S(1)} all-gather(f32[128,768]{1,0:T(8,128)S(1)} %get-tuple-element.51), channel_id=6, replica_groups={{0,1},{2,3},{4,5},{6,7},{8,9},{10,11},{12,13},{14,15},{16,17},{18,19},{..., dimensions={0}, use_global_device_ids=true | all-gather | bytes 1179648 | tf_op jit(solution)/shard_map/all_gather | solution.py:354
  97.5 0.0 collective-permute-done.2.more_ref
  97.5 0.1 shard_map.83
  97.6 7.2 %collective-permute-start.3 = (f32[128,768]{1,0:T(8,128)S(1)}, f32[128,768]{1,0:T(8,128)S(1)}, u32[]{:S(2)}, u32[]{:S(2)}) collective-permute-start(f32[128,768]{1,0:T(8,128)S(1)} %shard_map.83), channel_id=1, source_target_pairs={{0,2},{1,7},{2,4},{3,1},{4,6},{5,3},{6,0},{7,5},{8,10},{9,15},{10,... | collective-permute-start | bytes 1179656 | tf_op jit(solution)/shard_map/ppermute | solution.py:357
  104.7 4.9 %all-gather.3 = f32[256,768]{1,0:T(8,128)S(1)} all-gather(f32[128,768]{1,0:T(8,128)S(1)} %get-tuple-element.47), channel_id=5, replica_groups={{0,1},{2,3},{4,5},{6,7},{8,9},{10,11},{12,13},{14,15},{16,17},{18,19},{..., dimensions={0}, use_global_device_ids=true | all-gather | bytes 1179648 | tf_op jit(solution)/shard_map/all_gather | solution.py:355
  109.7 0.1 shard_map.82.one_ref
  109.7 5.0 %collective-permute-done.3.two_ref = f32[128,768]{1,0:T(8,128)S(1)} collective-permute-done((f32[128,768]{1,0:T(8,128)S(1)}, f32[128,768]{1,0:T(8,128)S(1)}, u32[]{:S(2)}, u32[]{:S(2)}) %collective-permute-start.3) | collective-permute-done | bytes 393248 | tf_op jit(solution)/shard_map/ppermute | solution.py:357
  114.7 0.7 shard_map.84
  (15 shorter events, 0.1 us)
Async XLA Ops:
  66.3 7.5 %collective-permute-start = (f32[576,128]{1,0:T(8,128)S(1)}, f32[576,128]{1,0:T(8,128)S(1)}, u32[]{:S(2)}, u32[]{:S(2)}) collective-permute-start(f32[576,128]{1,0:T(8,128)S(1)} %bitcast.18), channel_id=1, source_target_pairs={{0,8},{8,0},{16,24},{24,16},{32,40},{40,32},{48,56},{56,48},{64,72... | collective-permute-start | bytes 884744 | tf_op jit(solution)/shard_map/ppermute | solution.py:309
  69.5 3.1 %copy-start = (bf16[128,512]{1,0:T(8,128)(2,1)S(1)}, bf16[128,512]{1,0:T(8,128)(2,1)}, u32[]{:S(2)}) copy-start(bf16[128,512]{1,0:T(8,128)(2,1)} %query_ref.3) | copy-start | bytes 393220
  69.5 3.1 %copy-start.1 = (bf16[128,512]{1,0:T(8,128)(2,1)S(1)}, bf16[128,512]{1,0:T(8,128)(2,1)}, u32[]{:S(2)}) copy-start(bf16[128,512]{1,0:T(8,128)(2,1)} %key_ref.1) | copy-start | bytes 393220
  69.5 3.1 %copy-start.2 = (bf16[128,512]{1,0:T(8,128)(2,1)S(1)}, bf16[128,512]{1,0:T(8,128)(2,1)}, u32[]{:S(2)}) copy-start(bf16[128,512]{1,0:T(8,128)(2,1)} %value_ref.1) | copy-start | bytes 393220
  69.5 3.1 %copy-start.3 = (f32[4,128]{1,0:T(4,128)S(1)}, f32[4,128]{1,0:T(4,128)}, u32[]{:S(2)}) copy-start(f32[4,128]{1,0:T(4,128)} %log_ref.1) | copy-start | bytes 6148
  69.5 3.1 %copy-start.4 = (s32[128]{0:T(128)S(1)}, s32[128]{0:T(128)}, u32[]{:S(2)}) copy-start(s32[128]{0:T(128)} %param.11) | copy-start | bytes 1540
  69.5 4.2 %copy-start.5 = (f32[512]{0:T(512)S(1)}, f32[512]{0:T(512)}, u32[]{:S(2)}) copy-start(f32[512]{0:T(512)} %param.12) | copy-start | bytes 6148
  82.1 15.3 %collective-permute-start.2 = (f32[128,768]{1,0:T(8,128)S(1)}, f32[128,768]{1,0:T(8,128)S(1)}, u32[]{:S(2)}, u32[]{:S(2)}) collective-permute-start(f32[128,768]{1,0:T(8,128)S(1)} %shard_map.79), channel_id=1, source_target_pairs={{0,2},{1,7},{2,4},{3,1},{4,6},{5,3},{6,0},{7,5},{8,10},{9,15},{10,... | collective-permute-start | bytes 1179656 | tf_op jit(solution)/shard_map/ppermute | solution.py:346
  90.4 19.2 %collective-permute-start.1 = (f32[128,768]{1,0:T(8,128)S(1)}, f32[128,768]{1,0:T(8,128)S(1)}, u32[]{:S(2)}, u32[]{:S(2)}) collective-permute-start(f32[128,768]{1,0:T(8,128)S(1)} %shard_map.81), channel_id=1, source_target_pairs={{0,6},{1,3},{2,0},{3,5},{4,2},{5,7},{6,4},{7,1},{8,14},{9,11},{10,... | collective-permute-start | bytes 1179656 | tf_op jit(solution)/shard_map/ppermute | solution.py:350
  97.6 17.2 %collective-permute-start.3 = (f32[128,768]{1,0:T(8,128)S(1)}, f32[128,768]{1,0:T(8,128)S(1)}, u32[]{:S(2)}, u32[]{:S(2)}) collective-permute-start(f32[128,768]{1,0:T(8,128)S(1)} %shard_map.83), channel_id=1, source_target_pairs={{0,2},{1,7},{2,4},{3,1},{4,6},{5,3},{6,0},{7,5},{8,10},{9,15},{10,... | collective-permute-start | bytes 1179656 | tf_op jit(solution)/shard_map/ppermute | solution.py:357

commit v5 on v4

--- a/solution.py
+++ b/solution.py
@@ -18,6 +18,7 @@
 CHUNK = ROWS + 1
 HEAD_ROWS = PIECES * CHUNK
 PACKED = PAIRS * CHUNK
+RING = 4
 
 surge_log_factor = math.log(0.6)
 F32 = jnp.float32
@@ -194,35 +195,57 @@
         factor_ref[:, lanes] = jnp.broadcast_to(other[:, head : head + 1], (EVENTS, HEAD_DIM))
 
 
-def stage_kernel(w_hbm, staged_ref, sems):
-    copies = [
-        pltpu.make_async_copy(w_hbm.at[:, pl.ds(block * COLS, COLS)], staged_ref.at[block], sems.at[block])
-        for block in range(D // COLS)
-    ]
+def widen_kernel(place_ref, w_hbm, wide_hbm, narrow_ref, wide_ref, sems):
+    core = place_ref[0] & 1
+    incoming, outgoing = [], []
+    for t in range(RING):
+        columns = pl.ds(pl.multiple_of((2 * t + 1 - core) * COLS, COLS), COLS)
+        incoming.append(pltpu.make_async_copy(w_hbm.at[:, columns], narrow_ref.at[t], sems.at[t]))
+        outgoing.append(pltpu.make_async_copy(wide_ref.at[t], wide_hbm.at[t], sems.at[RING + t]))
+    for copy in incoming:
+        copy.start()
+    for t in range(RING):
+        incoming[t].wait()
+        wide_ref[t] = narrow_ref[t].astype(F32)
+        outgoing[t].start()
+    for copy in outgoing:
+        copy.wait()
+
+
+def stage_kernel(place_ref, w_hbm, wide_ref, staged_ref, sems):
+    rows = w_hbm.shape[0]
+    core = place_ref[0] & 1
+    copies = []
+    for t in range(RING):
+        columns = pl.ds(pl.multiple_of((2 * t + core) * COLS, COLS), COLS)
+        copies.append(
+            pltpu.make_async_copy(w_hbm.at[:, columns], staged_ref.at[t, pl.ds(0, rows)], sems.at[t])
+        )
     for copy in copies:
         copy.start()
+    for t in range(RING):
+        staged_ref[t, rows:, :] = wide_ref[t].astype(BF16)
     for copy in copies:
         copy.wait()
 
 
-def block_of(place, far, core):
-    return 2 * (((place >> 1) + far) & 3) + core
-
-
-def first_kernel(
-    place_ref,
-    query_ref,
-    total_ref,
-    factor_ref,
-    other_ref,
-    gain_ref,
-    w_ref,
-    normed_ref,
-    opposite_send_ref,
-    opposite_ref,
-    behind_send_ref,
-    behind_ref,
-):
+def stage(place, w_out, wide):
+    return pl.pallas_call(
+        stage_kernel,
+        in_specs=[
+            pl.BlockSpec(memory_space=pltpu.SMEM),
+            pl.BlockSpec(memory_space=pltpu.HBM),
+            pl.BlockSpec(memory_space=pltpu.VMEM),
+        ],
+        out_specs=pl.BlockSpec(memory_space=pltpu.VMEM),
+        out_shape=pltpu.VMEM((RING, 2 * w_out.shape[0], COLS), BF16),
+        scratch_shapes=[pltpu.SemaphoreType.DMA((RING,))],
+        compiler_params=pltpu.CompilerParams(vmem_limit_bytes=VMEM_LIMIT),
+        cost_estimate=pl.CostEstimate(flops=0, bytes_accessed=16_000_000, transcendentals=0),
+    )(place, pltpu.with_memory_space_constraint(w_out, pltpu.HBM), wide)
+
+
+def normed_kernel(query_ref, total_ref, factor_ref, other_ref, gain_ref, normed_ref):
     for head in range(HEADS_DEV):
         lanes = slice(head * HEAD_DIM, (head + 1) * HEAD_DIM)
         total = total_ref[:, lanes] + factor_ref[:, lanes] * times_state(
@@ -230,38 +253,31 @@
         )
         average = jnp.mean(total * total, axis=1, keepdims=True)
         scaled = total * lax.rsqrt(average + 1e-06) * gain_ref[:, lanes]
-        normed_ref[:, lanes] = scaled.astype(BF16)
+        normed_ref[:, lanes] = scaled.astype(BF16).astype(F32)
+
+
+def project(place, both_ref, w_ref, far):
+    core = place & 1
+    normed = jnp.concatenate([both_ref[core].astype(BF16), both_ref[1 - core].astype(BF16)], axis=1)
+    return jnp.dot(normed, w_ref[((place >> 1) + far) & 3], preferred_element_type=F32)
+
+
+def opposite_kernel(place_ref, both_ref, w_ref, out_ref):
+    out_ref[...] = project(place_ref[0], both_ref, w_ref, 2)
+
+
+def behind_kernel(place_ref, both_ref, w_ref, out_ref):
     place = place_ref[0]
-    core = place & 1
-    normed = normed_ref[...]
-    for out_ref, far, whose in (
-        (opposite_send_ref, 2, 1 - core),
-        (opposite_ref, 2, core),
-        (behind_send_ref, 1 + 2 * core, 1 - core),
-        (behind_ref, 3 - 2 * core, core),
-    ):
-        out_ref[...] = jnp.dot(normed, w_ref[block_of(place, far, whose)], preferred_element_type=F32)
-
-
-def rest_kernel(place_ref, normed_ref, w_ref, ahead_send_ref, ahead_ref, own_send_ref, own_ref):
+    out_ref[...] = project(place, both_ref, w_ref, 3 - 2 * (place & 1))
+
+
+def ahead_kernel(place_ref, both_ref, w_ref, got_ref, out_ref):
     place = place_ref[0]
-    core = place & 1
-    normed = normed_ref[...]
-    for out_ref, far, whose in (
-        (ahead_send_ref, 3 - 2 * core, 1 - core),
-        (ahead_ref, 1 + 2 * core, core),
-        (own_send_ref, 0, 1 - core),
-        (own_ref, 0, core),
-    ):
-        out_ref[...] = jnp.dot(normed, w_ref[block_of(place, far, whose)], preferred_element_type=F32)
-
-
-def core_sum_kernel(place_ref, mine_ref, both_ref, out_ref):
-    out_ref[...] = mine_ref[...] + both_ref[1 - (place_ref[0] & 1)]
-
-
-def three_kernel(place_ref, mine_ref, both_ref, more_ref, out_ref):
-    out_ref[...] = mine_ref[...] + both_ref[1 - (place_ref[0] & 1)] + more_ref[...]
+    out_ref[...] = project(place, both_ref, w_ref, 1 + 2 * (place & 1)) + got_ref[...]
+
+
+def own_kernel(place_ref, both_ref, w_ref, got_ref, out_ref):
+    out_ref[...] = project(place_ref[0], both_ref, w_ref, 0) + got_ref[...]
 
 
 def final_kernel(one_ref, two_ref, out_ref):
@@ -302,20 +318,28 @@
     pair_terms, got = call(
         combine_kernel, [packed, packed], (side, kept, both, decay), scalars=1, flops=200_000, moved=1_500_000
     )
+    pair_terms, w_late = lax.optimization_barrier((pair_terms, w_out))
+    (wide,) = call(
+        widen_kernel,
+        [((RING, 512, COLS), F32)],
+        (place, w_late),
+        scalars=1,
+        scratch=[
+            pltpu.VMEM((RING, 512, COLS), BF16),
+            pltpu.VMEM((RING, 512, COLS), F32),
+            pltpu.SemaphoreType.DMA((2 * RING,)),
+        ],
+        moved=9_500_000,
+        space=pltpu.HBM,
+        out_space=pltpu.HBM,
+    )
+    wide_got = lax.ppermute(wide, "tp", CORE_SWAP)
     slices = exchange_pieces(pair_terms)
-    (states,) = call(scan_kernel, [packed], (side, slices), scalars=1, flops=200_000, moved=600_000)
+    (states,) = call(scan_kernel, [packed], (side, slices), scalars=1, flops=50_000_000_000, moved=600_000)
     own = exchange_pieces(states)
-    own, w_late = lax.optimization_barrier((own, w_out))
+    own, w_late = lax.optimization_barrier((own, w_late))
     other = lax.ppermute(own, "ctx", SIDE_SWAP)
-    (staged,) = call(
-        stage_kernel,
-        [((D // COLS, 512, COLS), BF16)],
-        (w_late,),
-        scratch=[pltpu.SemaphoreType.DMA((D // COLS,))],
-        moved=12_600_000,
-        space=pltpu.HBM,
-        out_space=pltpu.VMEM,
-    )
+    staged = stage(place, w_late, wide_got)
     other, staged = lax.optimization_barrier((other, staged))
     inner = ((EVENTS, 512), F32)
     total, factor = call(
@@ -327,35 +351,19 @@
         moved=1_500_000,
     )
     block = ((EVENTS, COLS), F32)
-    two_blocks = ((2, EVENTS, COLS), F32)
-    normed, opposite_send, opposite_mine, behind_send, behind_mine = call(
-        first_kernel,
-        [((EVENTS, 512), BF16)] + [block] * 4,
-        (place, queries, total, factor, other, gain, staged),
-        scalars=1,
-        flops=430_000_000,
-        moved=6_000_000,
-    )
-
-    def core_sum(mine, both):
-        return call(core_sum_kernel, [block], (place, mine, both), scalars=1)[0]
-
-    opposite_both = lax.all_gather(opposite_send, "tp", axis_index_groups=CORE_PAIRS)
-    opposite = core_sum(opposite_mine, opposite_both)
-    opposite, behind_send = lax.optimization_barrier((opposite, behind_send))
-    ahead_got = lax.ppermute(opposite, "tp", ONWARD)
-    behind_both = lax.all_gather(behind_send, "tp", axis_index_groups=CORE_PAIRS)
-    behind_both, normed = lax.optimization_barrier((behind_both, normed))
-    behind = core_sum(behind_mine, behind_both)
-    one = lax.ppermute(behind, "tp", BACK)
-    ahead_send, ahead_mine, own_send, own_mine = call(
-        rest_kernel, [block] * 4, (place, normed, staged), scalars=1, flops=400_000_000, moved=5_000_000
-    )
-    ahead_both = lax.all_gather(ahead_send, "tp", axis_index_groups=CORE_PAIRS)
-    own_both = lax.all_gather(own_send, "tp", axis_index_groups=CORE_PAIRS)
-    (passed,) = call(three_kernel, [block], (place, ahead_mine, ahead_both, ahead_got), scalars=1)
-    two = lax.ppermute(passed, "tp", ONWARD)
-    (own_and_one,) = call(three_kernel, [block], (place, own_mine, own_both, one), scalars=1, moved=1_600_000)
+    (normed,) = call(
+        normed_kernel, [inner], (queries, total, factor, other, gain), flops=70_000_000, moved=1_300_000
+    )
+    both = lax.all_gather(normed, "tp", axis_index_groups=CORE_PAIRS)
+
+    def step(kernel, *args):
+        args = (place, both, staged) + args
+        return call(kernel, [block], args, scalars=1, flops=200_000_000, moved=2_500_000)[0]
+
+    ahead_got = lax.ppermute(step(opposite_kernel), "tp", ONWARD)
+    one = lax.ppermute(step(behind_kernel), "tp", BACK)
+    two = lax.ppermute(step(ahead_kernel, ahead_got), "tp", ONWARD)
+    own_and_one = step(own_kernel, one)
     (out,) = call(final_kernel, [((EVENTS, COLS), BF16)], (own_and_one, two), moved=1_000_000)
     return out
 

time: 118 us -> 119 us (level)
  blocking collectives: 81.6 us -> 35.7 us
  starting transfers between devices: 20.3 us -> 41.7 us
  waiting for transfers between devices: 5.48 us -> 24.8 us
  Pallas kernels: 7.83 us -> 14.4 us
    all_to_all x2 -> x1, blocking collectives: 57.5 us -> 22.3 us  [exchange_pieces(): pieces = lax.all_to_all(pieces, 'ctx', 0, 0, axis_index_groups=SIDE_GROUPS)]
    all_to_all x0 -> x1, starting transfers between devices: none -> 20.5 us  [exchange_pieces(): pieces = lax.all_to_all(pieces, 'ctx', 0, 0, axis_index_groups=SIDE_GROUPS)]
    ppermute x3 -> x4, waiting for transfers between devices: 5.02 us -> 17.5 us  [the longest x1 13.2 us: body(): ahead_got = lax.ppermute(step(opposite_kernel), 'tp', ONWARD)]
    all_gather x4 -> x1, blocking collectives: 17.2 us -> 6.48 us  [body(): both = lax.all_gather(normed, 'tp', axis_index_groups=CORE_PAIRS)]
    all_to_all x0 -> x1, waiting for transfers between devices: none -> 7.28 us  [exchange_pieces(): pieces = lax.all_to_all(pieces, 'ctx', 0, 0, axis_index_groups=SIDE_GROUPS)]
    pallas_call x0 -> x1, Pallas kernels: none -> 4.68 us  [stage(): pl.pallas_call(stage_kernel, in_specs=[pl.BlockSpec(memory_space=pltpu.SM...]
    pallas_call x12 -> x11, Pallas kernels: 7.83 us -> 9.77 us  [call(): pl.pallas_call(kernel, out_shape=shapes, in_specs=specs, out_specs=[pl.Bl...]
    ppermute x3 -> x4, starting transfers between devices: 17.1 us -> 18.1 us  [the longest x1 6.84 us: body(): two = lax.ppermute(step(ahead_kernel, ahead_got), 'tp', ONWARD)]
  transfers between devices with their start and end apart: 4 -> 6, of which waited for: 2 -> 3; matrix products, arithmetic and copies ran while one was open for 0% -> 0% of each run, Pallas kernels for 4% -> 9%
where the time goes in v5:
time: 119 us; the launch traced here: 117 us
  starting transfers between devices  41.7 us (35%)
  blocking collectives  35.7 us (30%)
  waiting for transfers between devices  24.8 us (21%)
  Pallas kernels  14.4 us (12%)
    all_to_all x1, blocking collectives, exchange_pieces(): pieces = lax.all_to_all(pieces, 'ctx', 0, 0, axis_index_groups=SIDE_GROUPS)  22.3 us
    all_to_all x1, starting transfers between devices, exchange_pieces(): pieces = lax.all_to_all(pieces, 'ctx', 0, 0, axis_index_groups=SIDE_GROUPS)  20.5 us
    ppermute x1, waiting for transfers between devices, body(): ahead_got = lax.ppermute(step(opposite_kernel), 'tp', ONWARD)  13.2 us
    pallas_call x11, Pallas kernels, call(): pl.pallas_call(kernel, out_shape=shapes, in_specs=specs, out_specs=[pl.Bl...  9.77 us
    all_to_all x1, waiting for transfers between devices, exchange_pieces(): pieces = lax.all_to_all(pieces, 'ctx', 0, 0, axis_index_groups=SIDE_GROUPS)  7.28 us
    all_gather x1, blocking collectives, body(): both = lax.all_gather(sent, 'ctx', axis_index_groups=SIDE_PAIRS)  6.91 us
    ppermute x1, starting transfers between devices, body(): two = lax.ppermute(step(ahead_kernel, ahead_got), 'tp', ONWARD)  6.84 us
    all_gather x1, blocking collectives, body(): both = lax.all_gather(normed, 'tp', axis_index_groups=CORE_PAIRS)  6.48 us
  transfers between devices with their start and end apart: 6, of which 3 were waited for; matrix products, arithmetic and copies ran while one was open for 0% of the time, Pallas kernels for 9%

profile of v5, /device:TPU:1, one launch (start us, length us, event | category | flops | bytes accessed | tf_op | source)
XLA Modules:
  0.0 117.0 jit_solution(9052005740399069480)
XLA Ops:
  0.0 1.7 %shard_map.73 = (f32[576,128]{1,0:T(8,128)S(1)}, f32[576,128]{1,0:T(8,128)S(1)}, f32[4,128]{1,0:T(4,128)S(1)}) custom-call(s32[1]{0:T(128)} %bitcast.1.side_ref, bf16[128,512]{1,0:T(8,128)(2,1)} %key_ref.1, bf16[128,512]{1,0:T(8,128)(2,1)} %value_ref.1, f32[4,128]{1,0:T(4,128)} %log_ref.1, s32[1,128]{1,0:T(1,128)} %bitcast.20), custom_call_target="tpu_custom_call" | custom-call | flops 70000000 | bytes 900000 | tf_op jit(solution)/shard_map/pallas_call | solution.py:47
  1.7 6.9 %all-gather = f32[1152,128]{1,0:T(8,128)S(1)} all-gather(f32[576,128]{1,0:T(8,128)S(1)} %get-tuple-element.19), channel_id=2, replica_groups={{0,8},{16,24},{32,40},{48,56},{64,72},{80,88},{96,104},{112,120},{128,1..., dimensions={0}, use_global_device_ids=true | all-gather | bytes 884736 | tf_op jit(solution)/shard_map/all_gather | solution.py:317
  8.6 0.8 shard_map.74
  9.4 20.5 %all-to-all-start = ((f32[48,3,4,128]{3,2,1,0:T(4,128)}), f32[48,3,4,128]{3,2,1,0:T(4,128)S(1)}, u32[]{:S(2)}, u32[]{:S(2)}) async-start(f32[48,3,4,128]{3,2,1,0:T(4,128)} %bitcast.4), calls=%async_computation | async-start | bytes 589824 | tf_op jit(solution)/shard_map/all_to_all | solution.py:289
  29.9 4.0 %shard_map.77 = f32[4,512,768]{2,1,0:T(8,128)} custom-call(s32[1]{0:T(128)} %bitcast.place_ref, bf16[512,6144]{1,0:T(8,128)(2,1)} %w_hbm.1), custom_call_target="tpu_custom_call" | custom-call | bytes 9500000 | tf_op jit(solution)/shard_map/pallas_call | solution.py:47
  33.9 3.7 %collective-permute-start.1 = (f32[4,512,768]{2,1,0:T(8,128)}, f32[4,512,768]{2,1,0:T(8,128)}, u32[]{:S(2)}, u32[]{:S(2)}) collective-permute-start(f32[4,512,768]{2,1,0:T(8,128)} %shard_map.77), channel_id=1, source_target_pairs={{0,1},{1,0},{2,3},{3,2},{4,5},{5,4},{6,7},{7,6},{8,9},{9,8},{10,11... | collective-permute-start | bytes 18874376 | tf_op jit(solution)/shard_map/ppermute | solution.py:336
  37.6 7.3 %all-to-all-done = f32[48,3,4,128]{3,2,1,0:T(4,128)S(1)} async-done(((f32[48,3,4,128]{3,2,1,0:T(4,128)}), f32[48,3,4,128]{3,2,1,0:T(4,128)S(1)}, u32[]{:S(2)}, u32[]{:S(2)}) %all-to-all-start) | async-done | bytes 294944 | tf_op jit(solution)/shard_map/all_to_all | solution.py:289
  44.9 0.1 shard_map.75
  45.0 22.3 %all_to_all.10 = f32[48,3,4,128]{3,2,1,0:T(4,128)S(1)} all-to-all(f32[48,3,4,128]{3,2,1,0:T(4,128)S(1)} %bitcast.18), channel_id=1, replica_groups={{0,16,32,48,64,80,96,112,128,144,160,176,192,208,224,240,256,272,288,30..., dimensions={0} | all-to-all | bytes 589824 | tf_op jit(solution)/shard_map/all_to_all | solution.py:289
  67.4 3.2 %collective-permute-start = (f32[576,128]{1,0:T(8,128)S(1)}, f32[576,128]{1,0:T(8,128)S(1)}, u32[]{:S(2)}, u32[]{:S(2)}) collective-permute-start(f32[576,128]{1,0:T(8,128)S(1)} %bitcast.15), channel_id=1, source_target_pairs={{0,8},{8,0},{16,24},{24,16},{32,40},{40,32},{48,56},{56,48},{64,72... | collective-permute-start | bytes 884744 | tf_op jit(solution)/shard_map/ppermute | solution.py:341
  70.6 0.7 shard_map.76
  71.3 4.7 %shard_map.78.w_ref = bf16[4,1024,768]{2,1,0:T(8,128)(2,1)S(1)} custom-call(s32[1]{0:T(128)} %bitcast.place_ref, bf16[512,6144]{1,0:T(8,128)(2,1)} %w_hbm.1, f32[4,512,768]{2,1,0:T(8,128)} %collective-permute-done.1.wide_ref), custom_call_target="tpu_custom_call" | custom-call | bytes 16000000 | tf_op jit(solution)/shard_map/pallas_call | solution.py:233
  76.0 0.3 shard_map.79
  76.3 6.5 %all-gather.1 = f32[256,512]{1,0:T(8,128)S(1)} all-gather(f32[128,512]{1,0:T(8,128)S(1)} %shard_map.79), channel_id=3, replica_groups={{0,1},{2,3},{4,5},{6,7},{8,9},{10,11},{12,13},{14,15},{16,17},{18,19},{..., dimensions={0}, use_global_device_ids=true | all-gather | bytes 786432 | tf_op jit(solution)/shard_map/all_gather | solution.py:357
  82.8 0.4 shard_map.82
  83.2 5.6 %collective-permute-start.3 = (f32[128,768]{1,0:T(8,128)S(1)}, f32[128,768]{1,0:T(8,128)S(1)}, u32[]{:S(2)}, u32[]{:S(2)}) collective-permute-start(f32[128,768]{1,0:T(8,128)S(1)} %shard_map.82), channel_id=1, source_target_pairs={{0,2},{1,7},{2,4},{3,1},{4,6},{5,3},{6,0},{7,5},{8,10},{9,15},{10,... | collective-permute-start | bytes 1179656 | tf_op jit(solution)/shard_map/ppermute | solution.py:363
  88.8 0.4 shard_map.80
  89.1 1.9 %collective-permute-start.2 = (f32[128,768]{1,0:T(8,128)S(1)}, f32[128,768]{1,0:T(8,128)S(1)}, u32[]{:S(2)}, u32[]{:S(2)}) collective-permute-start(f32[128,768]{1,0:T(8,128)S(1)} %shard_map.80), channel_id=1, source_target_pairs={{0,6},{1,3},{2,0},{3,5},{4,2},{5,7},{6,4},{7,1},{8,14},{9,11},{10,... | collective-permute-start | bytes 1179656 | tf_op jit(solution)/shard_map/ppermute | solution.py:364
  91.1 13.2 %collective-permute-done.3.got_ref = f32[128,768]{1,0:T(8,128)S(1)} collective-permute-done((f32[128,768]{1,0:T(8,128)S(1)}, f32[128,768]{1,0:T(8,128)S(1)}, u32[]{:S(2)}, u32[]{:S(2)}) %collective-permute-start.3) | collective-permute-done | bytes 393248 | tf_op jit(solution)/shard_map/ppermute | solution.py:363
  104.3 0.4 shard_map.83
  104.7 6.8 %collective-permute-start.4 = (f32[128,768]{1,0:T(8,128)S(1)}, f32[128,768]{1,0:T(8,128)S(1)}, u32[]{:S(2)}, u32[]{:S(2)}) collective-permute-start(f32[128,768]{1,0:T(8,128)S(1)} %shard_map.83), channel_id=1, source_target_pairs={{0,2},{1,7},{2,4},{3,1},{4,6},{5,3},{6,0},{7,5},{8,10},{9,15},{10,... | collective-permute-start | bytes 1179656 | tf_op jit(solution)/shard_map/ppermute | solution.py:365
  111.6 0.4 shard_map.81.one_ref
  112.0 4.3 %collective-permute-done.4.two_ref = f32[128,768]{1,0:T(8,128)S(1)} collective-permute-done((f32[128,768]{1,0:T(8,128)S(1)}, f32[128,768]{1,0:T(8,128)S(1)}, u32[]{:S(2)}, u32[]{:S(2)}) %collective-permute-start.4) | collective-permute-done | bytes 393248 | tf_op jit(solution)/shard_map/ppermute | solution.py:365
  116.3 0.7 shard_map.84
  (15 shorter events, 0.0 us)
Async XLA Ops:
  9.4 35.5 %all-to-all-start = ((f32[48,3,4,128]{3,2,1,0:T(4,128)}), f32[48,3,4,128]{3,2,1,0:T(4,128)S(1)}, u32[]{:S(2)}, u32[]{:S(2)}) async-start(f32[48,3,4,128]{3,2,1,0:T(4,128)} %bitcast.4), calls=%async_computation | async-start | bytes 589824 | tf_op jit(solution)/shard_map/all_to_all | solution.py:289
  33.9 37.4 %collective-permute-start.1 = (f32[4,512,768]{2,1,0:T(8,128)}, f32[4,512,768]{2,1,0:T(8,128)}, u32[]{:S(2)}, u32[]{:S(2)}) collective-permute-start(f32[4,512,768]{2,1,0:T(8,128)} %shard_map.77), channel_id=1, source_target_pairs={{0,1},{1,0},{2,3},{3,2},{4,5},{5,4},{6,7},{7,6},{8,9},{9,8},{10,11... | collective-permute-start | bytes 18874376 | tf_op jit(solution)/shard_map/ppermute | solution.py:336
  44.9 25.7 %copy-start = (bf16[128,512]{1,0:T(8,128)(2,1)S(1)}, bf16[128,512]{1,0:T(8,128)(2,1)}, u32[]{:S(2)}) copy-start(bf16[128,512]{1,0:T(8,128)(2,1)} %query_ref.3) | copy-start | bytes 393220
  44.9 25.7 %copy-start.1 = (bf16[128,512]{1,0:T(8,128)(2,1)S(1)}, bf16[128,512]{1,0:T(8,128)(2,1)}, u32[]{:S(2)}) copy-start(bf16[128,512]{1,0:T(8,128)(2,1)} %key_ref.1) | copy-start | bytes 393220
  44.9 25.7 %copy-start.2 = (bf16[128,512]{1,0:T(8,128)(2,1)S(1)}, bf16[128,512]{1,0:T(8,128)(2,1)}, u32[]{:S(2)}) copy-start(bf16[128,512]{1,0:T(8,128)(2,1)} %value_ref.1) | copy-start | bytes 393220
  44.9 25.7 %copy-start.3 = (f32[4,128]{1,0:T(4,128)S(1)}, f32[4,128]{1,0:T(4,128)}, u32[]{:S(2)}) copy-start(f32[4,128]{1,0:T(4,128)} %log_ref.1) | copy-start | bytes 6148
  44.9 25.7 %copy-start.5 = (s32[128]{0:T(128)S(1)}, s32[128]{0:T(128)}, u32[]{:S(2)}) copy-start(s32[128]{0:T(128)} %param.11) | copy-start | bytes 1540
  67.4 8.6 %collective-permute-start = (f32[576,128]{1,0:T(8,128)S(1)}, f32[576,128]{1,0:T(8,128)S(1)}, u32[]{:S(2)}, u32[]{:S(2)}) collective-permute-start(f32[576,128]{1,0:T(8,128)S(1)} %bitcast.15), channel_id=1, source_target_pairs={{0,8},{8,0},{16,24},{24,16},{32,40},{40,32},{48,56},{56,48},{64,72... | collective-permute-start | bytes 884744 | tf_op jit(solution)/shard_map/ppermute | solution.py:341
  71.3 4.7 %copy-start.4 = (f32[512]{0:T(512)S(1)}, f32[512]{0:T(512)}, u32[]{:S(2)}) copy-start(f32[512]{0:T(512)} %param.12) | copy-start | bytes 6148
  83.2 21.1 %collective-permute-start.3 = (f32[128,768]{1,0:T(8,128)S(1)}, f32[128,768]{1,0:T(8,128)S(1)}, u32[]{:S(2)}, u32[]{:S(2)}) collective-permute-start(f32[128,768]{1,0:T(8,128)S(1)} %shard_map.82), channel_id=1, source_target_pairs={{0,2},{1,7},{2,4},{3,1},{4,6},{5,3},{6,0},{7,5},{8,10},{9,15},{10,... | collective-permute-start | bytes 1179656 | tf_op jit(solution)/shard_map/ppermute | solution.py:363
  89.1 22.4 %collective-permute-start.2 = (f32[128,768]{1,0:T(8,128)S(1)}, f32[128,768]{1,0:T(8,128)S(1)}, u32[]{:S(2)}, u32[]{:S(2)}) collective-permute-start(f32[128,768]{1,0:T(8,128)S(1)} %shard_map.80), channel_id=1, source_target_pairs={{0,6},{1,3},{2,0},{3,5},{4,2},{5,7},{6,4},{7,1},{8,14},{9,11},{10,... | collective-permute-start | bytes 1179656 | tf_op jit(solution)/shard_map/ppermute | solution.py:364
  104.7 11.5 %collective-permute-start.4 = (f32[128,768]{1,0:T(8,128)S(1)}, f32[128,768]{1,0:T(8,128)S(1)}, u32[]{:S(2)}, u32[]{:S(2)}) collective-permute-start(f32[128,768]{1,0:T(8,128)S(1)} %shard_map.83), channel_id=1, source_target_pairs={{0,2},{1,7},{2,4},{3,1},{4,6},{5,3},{6,0},{7,5},{8,10},{9,15},{10,... | collective-permute-start | bytes 1179656 | tf_op jit(solution)/shard_map/ppermute | solution.py:365

commit v6 on v4

--- a/solution.py
+++ b/solution.py
@@ -264,8 +264,9 @@
     out_ref[...] = mine_ref[...] + both_ref[1 - (place_ref[0] & 1)] + more_ref[...]
 
 
-def final_kernel(one_ref, two_ref, out_ref):
-    out_ref[...] = (one_ref[...] + two_ref[...]).astype(BF16)
+def final_kernel(place_ref, mine_ref, both_ref, one_ref, two_ref, out_ref):
+    own = mine_ref[...] + both_ref[1 - (place_ref[0] & 1)]
+    out_ref[...] = (own + (one_ref[...] + two_ref[...])).astype(BF16)
 
 
 def exchange_pieces(packed):
@@ -347,16 +348,22 @@
     behind_both = lax.all_gather(behind_send, "tp", axis_index_groups=CORE_PAIRS)
     behind_both, normed = lax.optimization_barrier((behind_both, normed))
     behind = core_sum(behind_mine, behind_both)
-    one = lax.ppermute(behind, "tp", BACK)
     ahead_send, ahead_mine, own_send, own_mine = call(
         rest_kernel, [block] * 4, (place, normed, staged), scalars=1, flops=400_000_000, moved=5_000_000
     )
     ahead_both = lax.all_gather(ahead_send, "tp", axis_index_groups=CORE_PAIRS)
     own_both = lax.all_gather(own_send, "tp", axis_index_groups=CORE_PAIRS)
+    ahead_got, behind = lax.optimization_barrier((ahead_got, behind))
+    one = lax.ppermute(behind, "tp", BACK)
     (passed,) = call(three_kernel, [block], (place, ahead_mine, ahead_both, ahead_got), scalars=1)
     two = lax.ppermute(passed, "tp", ONWARD)
-    (own_and_one,) = call(three_kernel, [block], (place, own_mine, own_both, one), scalars=1, moved=1_600_000)
-    (out,) = call(final_kernel, [((EVENTS, COLS), BF16)], (own_and_one, two), moved=1_000_000)
+    (out,) = call(
+        final_kernel,
+        [((EVENTS, COLS), BF16)],
+        (place, own_mine, own_both, one, two),
+        scalars=1,
+        moved=2_000_000,
+    )
     return out
 
 

time: 118 us -> 122 us (1.034); the launches traced: 115 us -> 121 us
  waiting for transfers between devices: 5.48 us -> 16.9 us
  starting transfers between devices: 20.3 us -> 16.9 us
  blocking collectives: 81.6 us -> 79 us
    ppermute x1, waiting for transfers between devices: 0.01 us -> 6.04 us  [body(): one = lax.ppermute(behind, 'tp', BACK)]
    ppermute x1, waiting for transfers between devices: 0.02 us -> 3.53 us  [body(): ahead_got = lax.ppermute(opposite, 'tp', ONWARD)]
    all_gather x1, blocking collectives: 4.93 us -> 2.37 us  [body(): own_both = lax.all_gather(own_send, 'tp', axis_index_groups=CORE_PAIRS)]
    ppermute x1, starting transfers between devices: 4.05 us -> 1.92 us  [body(): one = lax.ppermute(behind, 'tp', BACK)]
    ppermute x1, waiting for transfers between devices: 5 us -> 6.84 us  [body(): two = lax.ppermute(passed, 'tp', ONWARD)]
    ppermute x1, starting transfers between devices: 7.16 us -> 5.92 us  [body(): two = lax.ppermute(passed, 'tp', ONWARD)]
    pallas_call x12 -> x11, Pallas kernels: 7.83 us -> 7.81 us  [call(): pl.pallas_call(kernel, out_shape=shapes, in_specs=specs, out_specs=[pl.Bl...]
  transfers between devices with their start and end apart: 4 -> 4, of which waited for: 2 -> 4; matrix products, arithmetic and copies ran while one was open for 0% -> 0% of each run, Pallas kernels for 4% -> 4%
where the time goes in v6:
time: 122 us; the launch traced here: 121 us
  blocking collectives  79 us (65%)
  starting transfers between devices  16.9 us (14%)
  waiting for transfers between devices  16.9 us (14%)
  Pallas kernels  7.81 us (6%)
    all_to_all x2, blocking collectives, exchange_pieces(): pieces = lax.all_to_all(pieces, 'ctx', 0, 0, axis_index_groups=SIDE_GROUPS)  57.5 us
    pallas_call x11, Pallas kernels, call(): pl.pallas_call(kernel, out_shape=shapes, in_specs=specs, out_specs=[pl.Bl...  7.81 us
    all_gather x1, blocking collectives, body(): lax.all_gather(opposite_send, 'tp', axis_index_groups=CORE_PAIRS)  7.55 us
    all_gather x1, blocking collectives, body(): both = lax.all_gather(sent, 'ctx', axis_index_groups=SIDE_PAIRS)  6.91 us
    ppermute x1, waiting for transfers between devices, body(): two = lax.ppermute(passed, 'tp', ONWARD)  6.84 us
    ppermute x1, waiting for transfers between devices, body(): one = lax.ppermute(behind, 'tp', BACK)  6.04 us
    ppermute x1, starting transfers between devices, body(): two = lax.ppermute(passed, 'tp', ONWARD)  5.92 us
    ppermute x1, starting transfers between devices, body(): ahead_got = lax.ppermute(opposite, 'tp', ONWARD)  5.88 us
  transfers between devices with their start and end apart: 4, of which 4 were waited for; matrix products, arithmetic and copies ran while one was open for 0% of the time, Pallas kernels for 4%

profile of v6, /device:TPU:1, one launch (start us, length us, event | category | flops | bytes accessed | tf_op | source)
XLA Modules:
  0.0 120.9 jit_solution(5611752041210216508)
XLA Ops:
  0.0 1.7 %shard_map.73 = (f32[576,128]{1,0:T(8,128)S(1)}, f32[576,128]{1,0:T(8,128)S(1)}, f32[4,128]{1,0:T(4,128)S(1)}) custom-call(s32[1]{0:T(128)} %bitcast.1.side_ref, bf16[128,512]{1,0:T(8,128)(2,1)} %key_ref.1, bf16[128,512]{1,0:T(8,128)(2,1)} %value_ref.1, f32[4,128]{1,0:T(4,128)} %log_ref.1, s32[1,128]{1,0:T(1,128)} %bitcast.23), custom_call_target="tpu_custom_call" | custom-call | flops 70000000 | bytes 900000 | tf_op jit(solution)/shard_map/pallas_call | solution.py:46
  1.7 6.9 %all-gather = f32[1152,128]{1,0:T(8,128)S(1)} all-gather(f32[576,128]{1,0:T(8,128)S(1)} %get-tuple-element.32), channel_id=2, replica_groups={{0,8},{16,24},{32,40},{48,56},{64,72},{80,88},{96,104},{112,120},{128,1..., dimensions={0}, use_global_device_ids=true | all-gather | bytes 884736 | tf_op jit(solution)/shard_map/all_gather | solution.py:302
  8.6 0.1 shard_map.74
  8.7 35.3 %all_to_all.10 = f32[48,3,4,128]{3,2,1,0:T(4,128)S(1)} all-to-all(f32[48,3,4,128]{3,2,1,0:T(4,128)S(1)} %bitcast.22), channel_id=1, replica_groups={{0,16,32,48,64,80,96,112,128,144,160,176,192,208,224,240,256,272,288,30..., dimensions={0} | all-to-all | bytes 589824 | tf_op jit(solution)/shard_map/all_to_all | solution.py:274
  44.0 0.1 shard_map.75
  44.1 22.2 %all_to_all.11 = f32[48,3,4,128]{3,2,1,0:T(4,128)S(1)} all-to-all(f32[48,3,4,128]{3,2,1,0:T(4,128)S(1)} %bitcast.21), channel_id=1, replica_groups={{0,16,32,48,64,80,96,112,128,144,160,176,192,208,224,240,256,272,288,30..., dimensions={0} | all-to-all | bytes 589824 | tf_op jit(solution)/shard_map/all_to_all | solution.py:274
  66.3 3.2 %collective-permute-start = (f32[576,128]{1,0:T(8,128)S(1)}, f32[576,128]{1,0:T(8,128)S(1)}, u32[]{:S(2)}, u32[]{:S(2)}) collective-permute-start(f32[576,128]{1,0:T(8,128)S(1)} %bitcast.18), channel_id=1, source_target_pairs={{0,8},{8,0},{16,24},{24,16},{32,40},{40,32},{48,56},{56,48},{64,72... | collective-permute-start | bytes 884744 | tf_op jit(solution)/shard_map/ppermute | solution.py:310
  69.5 3.0 %shard_map.77.w_ref = bf16[8,512,768]{2,1,0:T(8,128)(2,1)S(1)} custom-call(bf16[512,6144]{1,0:T(8,128)(2,1)} %w_hbm), custom_call_target="tpu_custom_call" | custom-call | bytes 12600000 | tf_op jit(solution)/shard_map/pallas_call | solution.py:46
  72.6 0.7 shard_map.76
  73.3 0.5 collective-permute-done.other_ref
  73.7 0.8 shard_map.78
  74.5 7.6 %all-gather.1 = f32[256,768]{1,0:T(8,128)S(1)} all-gather(f32[128,768]{1,0:T(8,128)S(1)} %get-tuple-element.43), channel_id=3, replica_groups={{0,1},{2,3},{4,5},{6,7},{8,9},{10,11},{12,13},{14,15},{16,17},{18,19},{..., dimensions={0}, use_global_device_ids=true | all-gather | bytes 1179648 | tf_op jit(solution)/shard_map/all_gather | solution.py:344
  82.1 5.9 %collective-permute-start.1 = (f32[128,768]{1,0:T(8,128)S(1)}, f32[128,768]{1,0:T(8,128)S(1)}, u32[]{:S(2)}, u32[]{:S(2)}) collective-permute-start(f32[128,768]{1,0:T(8,128)S(1)} %shard_map.79), channel_id=1, source_target_pairs={{0,2},{1,7},{2,4},{3,1},{4,6},{5,3},{6,0},{7,5},{8,10},{9,15},{10,... | collective-permute-start | bytes 1179656 | tf_op jit(solution)/shard_map/ppermute | solution.py:347
  88.0 2.4 %all-gather.2 = f32[256,768]{1,0:T(8,128)S(1)} all-gather(f32[128,768]{1,0:T(8,128)S(1)} %get-tuple-element.45), channel_id=4, replica_groups={{0,1},{2,3},{4,5},{6,7},{8,9},{10,11},{12,13},{14,15},{16,17},{18,19},{..., dimensions={0}, use_global_device_ids=true | all-gather | bytes 1179648 | tf_op jit(solution)/shard_map/all_gather | solution.py:348
  90.4 0.6 shard_map.80
  91.0 2.4 %all-gather.4 = f32[256,768]{1,0:T(8,128)S(1)} all-gather(f32[128,768]{1,0:T(8,128)S(1)} %get-tuple-element.55), channel_id=6, replica_groups={{0,1},{2,3},{4,5},{6,7},{8,9},{10,11},{12,13},{14,15},{16,17},{18,19},{..., dimensions={0}, use_global_device_ids=true | all-gather | bytes 1179648 | tf_op jit(solution)/shard_map/all_gather | solution.py:354
  93.4 3.5 %collective-permute-done.1.more_ref = f32[128,768]{1,0:T(8,128)S(1)} collective-permute-done((f32[128,768]{1,0:T(8,128)S(1)}, f32[128,768]{1,0:T(8,128)S(1)}, u32[]{:S(2)}, u32[]{:S(2)}) %collective-permute-start.1) | collective-permute-done | bytes 393248 | tf_op jit(solution)/shard_map/ppermute | solution.py:347
  96.9 0.1 shard_map.82
  97.0 5.9 %collective-permute-start.3 = (f32[128,768]{1,0:T(8,128)S(1)}, f32[128,768]{1,0:T(8,128)S(1)}, u32[]{:S(2)}, u32[]{:S(2)}) collective-permute-start(f32[128,768]{1,0:T(8,128)S(1)} %shard_map.82), channel_id=1, source_target_pairs={{0,2},{1,7},{2,4},{3,1},{4,6},{5,3},{6,0},{7,5},{8,10},{9,15},{10,... | collective-permute-start | bytes 1179656 | tf_op jit(solution)/shard_map/ppermute | solution.py:359
  102.9 1.9 %collective-permute-start.2 = (f32[128,768]{1,0:T(8,128)S(1)}, f32[128,768]{1,0:T(8,128)S(1)}, u32[]{:S(2)}, u32[]{:S(2)}) collective-permute-start(f32[128,768]{1,0:T(8,128)S(1)} %shard_map.81), channel_id=1, source_target_pairs={{0,6},{1,3},{2,0},{3,5},{4,2},{5,7},{6,4},{7,1},{8,14},{9,11},{10,... | collective-permute-start | bytes 1179656 | tf_op jit(solution)/shard_map/ppermute | solution.py:357
  104.9 2.4 %all-gather.3 = f32[256,768]{1,0:T(8,128)S(1)} all-gather(f32[128,768]{1,0:T(8,128)S(1)} %get-tuple-element.49), channel_id=5, replica_groups={{0,1},{2,3},{4,5},{6,7},{8,9},{10,11},{12,13},{14,15},{16,17},{18,19},{..., dimensions={0}, use_global_device_ids=true | all-gather | bytes 1179648 | tf_op jit(solution)/shard_map/all_gather | solution.py:355
  107.2 6.8 %collective-permute-done.3.two_ref = f32[128,768]{1,0:T(8,128)S(1)} collective-permute-done((f32[128,768]{1,0:T(8,128)S(1)}, f32[128,768]{1,0:T(8,128)S(1)}, u32[]{:S(2)}, u32[]{:S(2)}) %collective-permute-start.3) | collective-permute-done | bytes 393248 | tf_op jit(solution)/shard_map/ppermute | solution.py:359
  114.1 6.0 %collective-permute-done.2.one_ref = f32[128,768]{1,0:T(8,128)S(1)} collective-permute-done((f32[128,768]{1,0:T(8,128)S(1)}, f32[128,768]{1,0:T(8,128)S(1)}, u32[]{:S(2)}, u32[]{:S(2)}) %collective-permute-start.2) | collective-permute-done | bytes 393248 | tf_op jit(solution)/shard_map/ppermute | solution.py:357
  120.1 0.7 shard_map.83
  (14 shorter events, 0.1 us)
Async XLA Ops:
  66.3 7.5 %collective-permute-start = (f32[576,128]{1,0:T(8,128)S(1)}, f32[576,128]{1,0:T(8,128)S(1)}, u32[]{:S(2)}, u32[]{:S(2)}) collective-permute-start(f32[576,128]{1,0:T(8,128)S(1)} %bitcast.18), channel_id=1, source_target_pairs={{0,8},{8,0},{16,24},{24,16},{32,40},{40,32},{48,56},{56,48},{64,72... | collective-permute-start | bytes 884744 | tf_op jit(solution)/shard_map/ppermute | solution.py:310
  69.5 3.1 %copy-start = (bf16[128,512]{1,0:T(8,128)(2,1)S(1)}, bf16[128,512]{1,0:T(8,128)(2,1)}, u32[]{:S(2)}) copy-start(bf16[128,512]{1,0:T(8,128)(2,1)} %query_ref.3) | copy-start | bytes 393220
  69.5 3.1 %copy-start.1 = (bf16[128,512]{1,0:T(8,128)(2,1)S(1)}, bf16[128,512]{1,0:T(8,128)(2,1)}, u32[]{:S(2)}) copy-start(bf16[128,512]{1,0:T(8,128)(2,1)} %key_ref.1) | copy-start | bytes 393220
  69.5 3.1 %copy-start.2 = (bf16[128,512]{1,0:T(8,128)(2,1)S(1)}, bf16[128,512]{1,0:T(8,128)(2,1)}, u32[]{:S(2)}) copy-start(bf16[128,512]{1,0:T(8,128)(2,1)} %value_ref.1) | copy-start | bytes 393220
  69.5 3.1 %copy-start.3 = (f32[4,128]{1,0:T(4,128)S(1)}, f32[4,128]{1,0:T(4,128)}, u32[]{:S(2)}) copy-start(f32[4,128]{1,0:T(4,128)} %log_ref.1) | copy-start | bytes 6148
  69.5 3.1 %copy-start.4 = (s32[128]{0:T(128)S(1)}, s32[128]{0:T(128)}, u32[]{:S(2)}) copy-start(s32[128]{0:T(128)} %param.11) | copy-start | bytes 1540
  69.5 4.2 %copy-start.5 = (f32[512]{0:T(512)S(1)}, f32[512]{0:T(512)}, u32[]{:S(2)}) copy-start(f32[512]{0:T(512)} %param.12) | copy-start | bytes 6148
  82.1 14.8 %collective-permute-start.1 = (f32[128,768]{1,0:T(8,128)S(1)}, f32[128,768]{1,0:T(8,128)S(1)}, u32[]{:S(2)}, u32[]{:S(2)}) collective-permute-start(f32[128,768]{1,0:T(8,128)S(1)} %shard_map.79), channel_id=1, source_target_pairs={{0,2},{1,7},{2,4},{3,1},{4,6},{5,3},{6,0},{7,5},{8,10},{9,15},{10,... | collective-permute-start | bytes 1179656 | tf_op jit(solution)/shard_map/ppermute | solution.py:347
  97.0 17.1 %collective-permute-start.3 = (f32[128,768]{1,0:T(8,128)S(1)}, f32[128,768]{1,0:T(8,128)S(1)}, u32[]{:S(2)}, u32[]{:S(2)}) collective-permute-start(f32[128,768]{1,0:T(8,128)S(1)} %shard_map.82), channel_id=1, source_target_pairs={{0,2},{1,7},{2,4},{3,1},{4,6},{5,3},{6,0},{7,5},{8,10},{9,15},{10,... | collective-permute-start | bytes 1179656 | tf_op jit(solution)/shard_map/ppermute | solution.py:359
  102.9 17.2 %collective-permute-start.2 = (f32[128,768]{1,0:T(8,128)S(1)}, f32[128,768]{1,0:T(8,128)S(1)}, u32[]{:S(2)}, u32[]{:S(2)}) collective-permute-start(f32[128,768]{1,0:T(8,128)S(1)} %shard_map.81), channel_id=1, source_target_pairs={{0,6},{1,3},{2,0},{3,5},{4,2},{5,7},{6,4},{7,1},{8,14},{9,11},{10,... | collective-permute-start | bytes 1179656 | tf_op jit(solution)/shard_map/ppermute | solution.py:357

commit v7 on v4

--- a/solution.py
+++ b/solution.py
@@ -347,12 +347,13 @@
     behind_both = lax.all_gather(behind_send, "tp", axis_index_groups=CORE_PAIRS)
     behind_both, normed = lax.optimization_barrier((behind_both, normed))
     behind = core_sum(behind_mine, behind_both)
-    one = lax.ppermute(behind, "tp", BACK)
     ahead_send, ahead_mine, own_send, own_mine = call(
         rest_kernel, [block] * 4, (place, normed, staged), scalars=1, flops=400_000_000, moved=5_000_000
     )
     ahead_both = lax.all_gather(ahead_send, "tp", axis_index_groups=CORE_PAIRS)
     own_both = lax.all_gather(own_send, "tp", axis_index_groups=CORE_PAIRS)
+    behind, ahead_both = lax.optimization_barrier((behind, ahead_both))
+    one = lax.ppermute(behind, "tp", BACK)
     (passed,) = call(three_kernel, [block], (place, ahead_mine, ahead_both, ahead_got), scalars=1)
     two = lax.ppermute(passed, "tp", ONWARD)
     (own_and_one,) = call(three_kernel, [block], (place, own_mine, own_both, one), scalars=1, moved=1_600_000)

time: 118 us -> 118 us (level); the launches traced: 115 us -> 117 us
  waiting for transfers between devices: 5.48 us -> 8.27 us
  starting transfers between devices: 20.3 us -> 18.6 us
    ppermute x1, waiting for transfers between devices: 0.01 us -> 6.44 us  [body(): one = lax.ppermute(behind, 'tp', BACK)]
    ppermute x1, waiting for transfers between devices: 5 us -> 1.38 us  [body(): two = lax.ppermute(passed, 'tp', ONWARD)]
    ppermute x1, starting transfers between devices: 7.16 us -> 5.49 us  [body(): two = lax.ppermute(passed, 'tp', ONWARD)]
  transfers between devices with their start and end apart: 4 -> 4, of which waited for: 2 -> 3; matrix products, arithmetic and copies ran while one was open for 0% -> 0% of each run, Pallas kernels for 4% -> 4%
where the time goes in v7:
time: 118 us; the launch traced here: 117 us
  blocking collectives  82.1 us (70%)
  starting transfers between devices  18.6 us (16%)
  waiting for transfers between devices  8.27 us (7%)
  Pallas kernels  7.83 us (7%)
    all_to_all x2, blocking collectives, exchange_pieces(): pieces = lax.all_to_all(pieces, 'ctx', 0, 0, axis_index_groups=SIDE_GROUPS)  57.5 us
    pallas_call x12, Pallas kernels, call(): pl.pallas_call(kernel, out_shape=shapes, in_specs=specs, out_specs=[pl.Bl...  7.83 us
    all_gather x1, blocking collectives, body(): lax.all_gather(opposite_send, 'tp', axis_index_groups=CORE_PAIRS)  7.55 us
    all_gather x1, blocking collectives, body(): both = lax.all_gather(sent, 'ctx', axis_index_groups=SIDE_PAIRS)  6.91 us
    ppermute x1, waiting for transfers between devices, body(): one = lax.ppermute(behind, 'tp', BACK)  6.44 us
    ppermute x1, starting transfers between devices, body(): ahead_got = lax.ppermute(opposite, 'tp', ONWARD)  5.88 us
    ppermute x1, starting transfers between devices, body(): two = lax.ppermute(passed, 'tp', ONWARD)  5.49 us
    all_gather x1, blocking collectives, body(): own_both = lax.all_gather(own_send, 'tp', axis_index_groups=CORE_PAIRS)  5.43 us
  transfers between devices with their start and end apart: 4, of which 3 were waited for; matrix products, arithmetic and copies ran while one was open for 0% of the time, Pallas kernels for 4%

profile of v7, /device:TPU:1, one launch (start us, length us, event | category | flops | bytes accessed | tf_op | source)
XLA Modules:
  0.0 117.1 jit_solution(3538920077878459916)
XLA Ops:
  0.0 1.7 %shard_map.73 = (f32[576,128]{1,0:T(8,128)S(1)}, f32[576,128]{1,0:T(8,128)S(1)}, f32[4,128]{1,0:T(4,128)S(1)}) custom-call(s32[1]{0:T(128)} %bitcast.1.side_ref, bf16[128,512]{1,0:T(8,128)(2,1)} %key_ref.1, bf16[128,512]{1,0:T(8,128)(2,1)} %value_ref.1, f32[4,128]{1,0:T(4,128)} %log_ref.1, s32[1,128]{1,0:T(1,128)} %bitcast.23), custom_call_target="tpu_custom_call" | custom-call | flops 70000000 | bytes 900000 | tf_op jit(solution)/shard_map/pallas_call | solution.py:46
  1.7 6.9 %all-gather = f32[1152,128]{1,0:T(8,128)S(1)} all-gather(f32[576,128]{1,0:T(8,128)S(1)} %get-tuple-element.32), channel_id=2, replica_groups={{0,8},{16,24},{32,40},{48,56},{64,72},{80,88},{96,104},{112,120},{128,1..., dimensions={0}, use_global_device_ids=true | all-gather | bytes 884736 | tf_op jit(solution)/shard_map/all_gather | solution.py:301
  8.6 0.1 shard_map.74
  8.7 35.3 %all_to_all.10 = f32[48,3,4,128]{3,2,1,0:T(4,128)S(1)} all-to-all(f32[48,3,4,128]{3,2,1,0:T(4,128)S(1)} %bitcast.22), channel_id=1, replica_groups={{0,16,32,48,64,80,96,112,128,144,160,176,192,208,224,240,256,272,288,30..., dimensions={0} | all-to-all | bytes 589824 | tf_op jit(solution)/shard_map/all_to_all | solution.py:273
  44.0 0.1 shard_map.75
  44.1 22.2 %all_to_all.11 = f32[48,3,4,128]{3,2,1,0:T(4,128)S(1)} all-to-all(f32[48,3,4,128]{3,2,1,0:T(4,128)S(1)} %bitcast.21), channel_id=1, replica_groups={{0,16,32,48,64,80,96,112,128,144,160,176,192,208,224,240,256,272,288,30..., dimensions={0} | all-to-all | bytes 589824 | tf_op jit(solution)/shard_map/all_to_all | solution.py:273
  66.3 3.2 %collective-permute-start = (f32[576,128]{1,0:T(8,128)S(1)}, f32[576,128]{1,0:T(8,128)S(1)}, u32[]{:S(2)}, u32[]{:S(2)}) collective-permute-start(f32[576,128]{1,0:T(8,128)S(1)} %bitcast.18), channel_id=1, source_target_pairs={{0,8},{8,0},{16,24},{24,16},{32,40},{40,32},{48,56},{56,48},{64,72... | collective-permute-start | bytes 884744 | tf_op jit(solution)/shard_map/ppermute | solution.py:309
  69.5 3.0 %shard_map.77.w_ref = bf16[8,512,768]{2,1,0:T(8,128)(2,1)S(1)} custom-call(bf16[512,6144]{1,0:T(8,128)(2,1)} %w_hbm), custom_call_target="tpu_custom_call" | custom-call | bytes 12600000 | tf_op jit(solution)/shard_map/pallas_call | solution.py:46
  72.6 0.7 shard_map.76
  73.3 0.5 collective-permute-done.other_ref
  73.7 0.8 shard_map.78
  74.5 7.6 %all-gather.1 = f32[256,768]{1,0:T(8,128)S(1)} all-gather(f32[128,768]{1,0:T(8,128)S(1)} %get-tuple-element.43), channel_id=3, replica_groups={{0,1},{2,3},{4,5},{6,7},{8,9},{10,11},{12,13},{14,15},{16,17},{18,19},{..., dimensions={0}, use_global_device_ids=true | all-gather | bytes 1179648 | tf_op jit(solution)/shard_map/all_gather | solution.py:343
  82.1 5.9 %collective-permute-start.2 = (f32[128,768]{1,0:T(8,128)S(1)}, f32[128,768]{1,0:T(8,128)S(1)}, u32[]{:S(2)}, u32[]{:S(2)}) collective-permute-start(f32[128,768]{1,0:T(8,128)S(1)} %shard_map.79), channel_id=1, source_target_pairs={{0,2},{1,7},{2,4},{3,1},{4,6},{5,3},{6,0},{7,5},{8,10},{9,15},{10,... | collective-permute-start | bytes 1179656 | tf_op jit(solution)/shard_map/ppermute | solution.py:346
  88.0 2.4 %all-gather.2 = f32[256,768]{1,0:T(8,128)S(1)} all-gather(f32[128,768]{1,0:T(8,128)S(1)} %get-tuple-element.45), channel_id=4, replica_groups={{0,1},{2,3},{4,5},{6,7},{8,9},{10,11},{12,13},{14,15},{16,17},{18,19},{..., dimensions={0}, use_global_device_ids=true | all-gather | bytes 1179648 | tf_op jit(solution)/shard_map/all_gather | solution.py:347
  90.4 0.6 shard_map.80
  91.0 2.4 %all-gather.4 = f32[256,768]{1,0:T(8,128)S(1)} all-gather(f32[128,768]{1,0:T(8,128)S(1)} %get-tuple-element.52), channel_id=6, replica_groups={{0,1},{2,3},{4,5},{6,7},{8,9},{10,11},{12,13},{14,15},{16,17},{18,19},{..., dimensions={0}, use_global_device_ids=true | all-gather | bytes 1179648 | tf_op jit(solution)/shard_map/all_gather | solution.py:353
  93.4 4.0 %collective-permute-start.1 = (f32[128,768]{1,0:T(8,128)S(1)}, f32[128,768]{1,0:T(8,128)S(1)}, u32[]{:S(2)}, u32[]{:S(2)}) collective-permute-start(f32[128,768]{1,0:T(8,128)S(1)} %shard_map.81), channel_id=1, source_target_pairs={{0,6},{1,3},{2,0},{3,5},{4,2},{5,7},{6,4},{7,1},{8,14},{9,11},{10,... | collective-permute-start | bytes 1179656 | tf_op jit(solution)/shard_map/ppermute | solution.py:356
  97.5 0.1 shard_map.83
  97.5 5.5 %collective-permute-start.3 = (f32[128,768]{1,0:T(8,128)S(1)}, f32[128,768]{1,0:T(8,128)S(1)}, u32[]{:S(2)}, u32[]{:S(2)}) collective-permute-start(f32[128,768]{1,0:T(8,128)S(1)} %shard_map.83), channel_id=1, source_target_pairs={{0,2},{1,7},{2,4},{3,1},{4,6},{5,3},{6,0},{7,5},{8,10},{9,15},{10,... | collective-permute-start | bytes 1179656 | tf_op jit(solution)/shard_map/ppermute | solution.py:358
  103.0 5.4 %all-gather.3 = f32[256,768]{1,0:T(8,128)S(1)} all-gather(f32[128,768]{1,0:T(8,128)S(1)} %get-tuple-element.49), channel_id=5, replica_groups={{0,1},{2,3},{4,5},{6,7},{8,9},{10,11},{12,13},{14,15},{16,17},{18,19},{..., dimensions={0}, use_global_device_ids=true | all-gather | bytes 1179648 | tf_op jit(solution)/shard_map/all_gather | solution.py:354
  108.5 6.4 %collective-permute-done.1.more_ref = f32[128,768]{1,0:T(8,128)S(1)} collective-permute-done((f32[128,768]{1,0:T(8,128)S(1)}, f32[128,768]{1,0:T(8,128)S(1)}, u32[]{:S(2)}, u32[]{:S(2)}) %collective-permute-start.1) | collective-permute-done | bytes 393248 | tf_op jit(solution)/shard_map/ppermute | solution.py:356
  114.9 0.1 shard_map.82.one_ref
  115.0 1.4 %collective-permute-done.3.two_ref = f32[128,768]{1,0:T(8,128)S(1)} collective-permute-done((f32[128,768]{1,0:T(8,128)S(1)}, f32[128,768]{1,0:T(8,128)S(1)}, u32[]{:S(2)}, u32[]{:S(2)}) %collective-permute-start.3) | collective-permute-done | bytes 393248 | tf_op jit(solution)/shard_map/ppermute | solution.py:358
  116.3 0.7 shard_map.84
  (15 shorter events, 0.1 us)
Async XLA Ops:
  66.3 7.5 %collective-permute-start = (f32[576,128]{1,0:T(8,128)S(1)}, f32[576,128]{1,0:T(8,128)S(1)}, u32[]{:S(2)}, u32[]{:S(2)}) collective-permute-start(f32[576,128]{1,0:T(8,128)S(1)} %bitcast.18), channel_id=1, source_target_pairs={{0,8},{8,0},{16,24},{24,16},{32,40},{40,32},{48,56},{56,48},{64,72... | collective-permute-start | bytes 884744 | tf_op jit(solution)/shard_map/ppermute | solution.py:309
  69.5 3.1 %copy-start = (bf16[128,512]{1,0:T(8,128)(2,1)S(1)}, bf16[128,512]{1,0:T(8,128)(2,1)}, u32[]{:S(2)}) copy-start(bf16[128,512]{1,0:T(8,128)(2,1)} %query_ref.3) | copy-start | bytes 393220
  69.5 3.1 %copy-start.1 = (bf16[128,512]{1,0:T(8,128)(2,1)S(1)}, bf16[128,512]{1,0:T(8,128)(2,1)}, u32[]{:S(2)}) copy-start(bf16[128,512]{1,0:T(8,128)(2,1)} %key_ref.1) | copy-start | bytes 393220
  69.5 3.1 %copy-start.2 = (bf16[128,512]{1,0:T(8,128)(2,1)S(1)}, bf16[128,512]{1,0:T(8,128)(2,1)}, u32[]{:S(2)}) copy-start(bf16[128,512]{1,0:T(8,128)(2,1)} %value_ref.1) | copy-start | bytes 393220
  69.5 3.1 %copy-start.3 = (f32[4,128]{1,0:T(4,128)S(1)}, f32[4,128]{1,0:T(4,128)}, u32[]{:S(2)}) copy-start(f32[4,128]{1,0:T(4,128)} %log_ref.1) | copy-start | bytes 6148
  69.5 3.1 %copy-start.4 = (s32[128]{0:T(128)S(1)}, s32[128]{0:T(128)}, u32[]{:S(2)}) copy-start(s32[128]{0:T(128)} %param.11) | copy-start | bytes 1540
  69.5 4.2 %copy-start.5 = (f32[512]{0:T(512)S(1)}, f32[512]{0:T(512)}, u32[]{:S(2)}) copy-start(f32[512]{0:T(512)} %param.12) | copy-start | bytes 6148
  82.1 15.3 %collective-permute-start.2 = (f32[128,768]{1,0:T(8,128)S(1)}, f32[128,768]{1,0:T(8,128)S(1)}, u32[]{:S(2)}, u32[]{:S(2)}) collective-permute-start(f32[128,768]{1,0:T(8,128)S(1)} %shard_map.79), channel_id=1, source_target_pairs={{0,2},{1,7},{2,4},{3,1},{4,6},{5,3},{6,0},{7,5},{8,10},{9,15},{10,... | collective-permute-start | bytes 1179656 | tf_op jit(solution)/shard_map/ppermute | solution.py:346
  93.4 21.5 %collective-permute-start.1 = (f32[128,768]{1,0:T(8,128)S(1)}, f32[128,768]{1,0:T(8,128)S(1)}, u32[]{:S(2)}, u32[]{:S(2)}) collective-permute-start(f32[128,768]{1,0:T(8,128)S(1)} %shard_map.81), channel_id=1, source_target_pairs={{0,6},{1,3},{2,0},{3,5},{4,2},{5,7},{6,4},{7,1},{8,14},{9,11},{10,... | collective-permute-start | bytes 1179656 | tf_op jit(solution)/shard_map/ppermute | solution.py:356
  97.5 18.8 %collective-permute-start.3 = (f32[128,768]{1,0:T(8,128)S(1)}, f32[128,768]{1,0:T(8,128)S(1)}, u32[]{:S(2)}, u32[]{:S(2)}) collective-permute-start(f32[128,768]{1,0:T(8,128)S(1)} %shard_map.83), channel_id=1, source_target_pairs={{0,2},{1,7},{2,4},{3,1},{4,6},{5,3},{6,0},{7,5},{8,10},{9,15},{10,... | collective-permute-start | bytes 1179656 | tf_op jit(solution)/shard_map/ppermute | solution.py:358

commit v8 on v4

--- a/solution.py
+++ b/solution.py
@@ -18,6 +18,8 @@
 CHUNK = ROWS + 1
 HEAD_ROWS = PIECES * CHUNK
 PACKED = PAIRS * CHUNK
+STATE_ROWS = HEADS_DEV * HEAD_DIM
+SENT_ROWS = STATE_ROWS + 8
 
 surge_log_factor = math.log(0.6)
 F32 = jnp.float32
@@ -104,13 +106,14 @@
     ]
     for copy in copies:
         copy.start()
-    for copy in copies:
+    for copy in copies[:2]:
         copy.wait()
     _, columns, _ = event_sums(log_ref, boundary_ref)
     ends, sent, kept = factors(side_ref[0], columns)
     decay = jnp.exp(ends)
-    sent_ref[...] = jnp.zeros_like(sent_ref)
-    kept_ref[...] = jnp.zeros_like(kept_ref)
+    for copy in copies[2:]:
+        copy.wait()
+    sent_ref[STATE_ROWS:, :] = jnp.zeros((SENT_ROWS - STATE_ROWS, HEAD_DIM), F32)
     for head in range(HEADS_DEV):
         lanes = slice(head * HEAD_DIM, (head + 1) * HEAD_DIM)
         value = value_ref[:, lanes].astype(F32)
@@ -121,23 +124,27 @@
             (((0,), (0,)), ((), ())),
             preferred_element_type=F32,
         )
-        sent_term = product[:, :128] + product[:, 128:256]
-        kept_term = product[:, 256:384] + product[:, 384:]
+        sent_ref[lanes, :] = product[:, :128] + product[:, 128:256]
+        kept_ref[lanes, :] = product[:, 256:384] + product[:, 384:]
         whole_row = jnp.broadcast_to(decay[:, head : head + 1], (1, HEAD_DIM))
         decay_ref[head : head + 1, :] = whole_row
+        sent_ref[STATE_ROWS + head : STATE_ROWS + head + 1, :] = whole_row
+
+
+def combine_kernel(side_ref, kept_ref, both_ref, decay_ref, out_ref):
+    other = 1 - side_ref[0]
+    for head in range(HEADS_DEV):
+        decay = decay_ref[head : head + 1, :]
+        rows = slice(head * HEAD_DIM, (head + 1) * HEAD_DIM)
+        state = kept_ref[rows, :] + decay * both_ref[other, rows, :]
+        last = STATE_ROWS + head
+        decay = decay * both_ref[other, last : last + 1, :]
         for piece in range(PIECES):
             count, first = piece_rows(piece), head * HEAD_ROWS + piece * CHUNK
-            rows = slice(ROWS * piece, ROWS * piece + count)
-            sent_ref[first : first + count, :] = sent_term[rows]
-            kept_ref[first : first + count, :] = kept_term[rows]
-            sent_ref[first + ROWS : first + CHUNK, :] = whole_row
-
-
-def combine_kernel(side_ref, kept_ref, both_ref, decay_ref, out_ref, got_ref):
-    got_ref[...] = both_ref[1 - side_ref[0]]
-    for head in range(HEADS_DEV):
-        rows = slice(head * HEAD_ROWS, (head + 1) * HEAD_ROWS)
-        out_ref[rows, :] = kept_ref[rows, :] + decay_ref[head : head + 1, :] * got_ref[rows, :]
+            part = [state[ROWS * piece : ROWS * piece + count]]
+            if count < ROWS:
+                part.append(jnp.zeros((ROWS - count, HEAD_DIM), F32))
+            out_ref[first : first + CHUNK, :] = jnp.concatenate(part + [decay], axis=0)
 
 
 def scan_kernel(side_ref, term_ref, out_ref):
@@ -158,12 +165,12 @@
         run(range(PAIRS - 1, -1, -1))
 
 
-def unpack(packed_ref, head):
-    parts = []
-    for piece in range(PIECES):
-        first = head * HEAD_ROWS + piece * CHUNK
-        parts.append(packed_ref[first : first + piece_rows(piece), :])
-    return jnp.concatenate(parts, axis=0)
+def unpack_kernel(packed_ref, state_ref):
+    for piece in range(PAIRS):
+        head, place = divmod(piece, PIECES)
+        first = head * HEAD_DIM + ROWS * place
+        count = piece_rows(place)
+        state_ref[first : first + count, :] = packed_ref[piece * CHUNK : piece * CHUNK + count, :]
 
 
 def times_state(query, state):
@@ -172,13 +179,14 @@
 
 
 def inner_kernel(
-    side_ref, query_ref, key_ref, value_ref, log_ref, boundary_ref, got_ref, own_ref, total_ref, factor_ref
+    side_ref, query_ref, key_ref, value_ref, log_ref, boundary_ref, both_ref, own_ref, total_ref, factor_ref
 ):
     rate, columns, upper = event_sums(log_ref, boundary_ref)
     rows_cum = lax.dot_general(
         rate, upper, (((1,), (0,)), ((), ())), precision=lax.Precision.HIGHEST, preferred_element_type=F32
     )
-    _, own, other = factors(side_ref[0], columns)
+    side = side_ref[0]
+    _, own, other = factors(side, columns)
     for head in range(HEADS_DEV):
         lanes = slice(head * HEAD_DIM, (head + 1) * HEAD_DIM)
         query = query_ref[:, lanes]
@@ -188,8 +196,9 @@
         weight = jnp.exp(-jnp.abs(columns[:, head : head + 1] - rows_cum[head : head + 1, :]))
         probs = (logits * weight).astype(BF16)
         intra = jnp.dot(probs, value_ref[:, lanes], preferred_element_type=F32)
-        last = head * HEAD_ROWS + ROWS
-        state = unpack(got_ref, head) + got_ref[last : last + 1, :] * unpack(own_ref, head)
+        last = STATE_ROWS + head
+        got_decay = both_ref[1 - side, last : last + 1, :]
+        state = both_ref[1 - side, lanes, :] + got_decay * own_ref[lanes, :]
         total_ref[:, lanes] = intra + own[:, head : head + 1] * times_state(query, state)
         factor_ref[:, lanes] = jnp.broadcast_to(other[:, head : head + 1], (EVENTS, HEAD_DIM))
 
@@ -220,13 +229,11 @@
     normed_ref,
     opposite_send_ref,
     opposite_ref,
-    behind_send_ref,
-    behind_ref,
 ):
     for head in range(HEADS_DEV):
         lanes = slice(head * HEAD_DIM, (head + 1) * HEAD_DIM)
         total = total_ref[:, lanes] + factor_ref[:, lanes] * times_state(
-            query_ref[:, lanes], unpack(other_ref, head)
+            query_ref[:, lanes], other_ref[lanes, :]
         )
         average = jnp.mean(total * total, axis=1, keepdims=True)
         scaled = total * lax.rsqrt(average + 1e-06) * gain_ref[:, lanes]
@@ -234,13 +241,16 @@
     place = place_ref[0]
     core = place & 1
     normed = normed_ref[...]
-    for out_ref, far, whose in (
-        (opposite_send_ref, 2, 1 - core),
-        (opposite_ref, 2, core),
-        (behind_send_ref, 1 + 2 * core, 1 - core),
-        (behind_ref, 3 - 2 * core, core),
-    ):
-        out_ref[...] = jnp.dot(normed, w_ref[block_of(place, far, whose)], preferred_element_type=F32)
+    for out_ref, whose in ((opposite_send_ref, 1 - core), (opposite_ref, core)):
+        out_ref[...] = jnp.dot(normed, w_ref[block_of(place, 2, whose)], preferred_element_type=F32)
+
+
+def behind_kernel(place_ref, normed_ref, w_ref, send_ref, mine_ref):
+    place = place_ref[0]
+    core = place & 1
+    normed = normed_ref[...]
+    for out_ref, whose in ((send_ref, 1 - core), (mine_ref, core)):
+        out_ref[...] = jnp.dot(normed, w_ref[block_of(place, 3 - 2 * whose, whose)], preferred_element_type=F32)
 
 
 def rest_kernel(place_ref, normed_ref, w_ref, ahead_send_ref, ahead_ref, own_send_ref, own_ref):
@@ -280,10 +290,11 @@
     boundary = boundary.reshape(1, EVENTS)
     gain = gain.reshape(1, 512)
     packed = ((PACKED, HEAD_DIM), F32)
+    state = ((STATE_ROWS, HEAD_DIM), F32)
 
     sent, kept, decay = call(
         terms_kernel,
-        [packed, packed, ((HEADS_DEV, HEAD_DIM), F32)],
+        [((SENT_ROWS, HEAD_DIM), F32), state, ((HEADS_DEV, HEAD_DIM), F32)],
         (side, keys, values, state_retention_log, boundary),
         scalars=1,
         scratch=[
@@ -299,12 +310,12 @@
         out_space=pltpu.VMEM,
     )
     both = lax.all_gather(sent, "ctx", axis_index_groups=SIDE_PAIRS)
-    pair_terms, got = call(
-        combine_kernel, [packed, packed], (side, kept, both, decay), scalars=1, flops=200_000, moved=1_500_000
+    (pair_terms,) = call(
+        combine_kernel, [packed], (side, kept, both, decay), scalars=1, flops=200_000, moved=1_100_000
     )
     slices = exchange_pieces(pair_terms)
     (states,) = call(scan_kernel, [packed], (side, slices), scalars=1, flops=200_000, moved=600_000)
-    own = exchange_pieces(states)
+    (own,) = call(unpack_kernel, [state], (exchange_pieces(states),), moved=600_000)
     own, w_late = lax.optimization_barrier((own, w_out))
     other = lax.ppermute(own, "ctx", SIDE_SWAP)
     (staged,) = call(
@@ -321,20 +332,20 @@
     total, factor = call(
         inner_kernel,
         [inner, inner],
-        (side, queries, keys, values, state_retention_log, boundary, got, own),
+        (side, queries, keys, values, state_retention_log, boundary, both, own),
         scalars=1,
         flops=100_000_000,
         moved=1_500_000,
     )
     block = ((EVENTS, COLS), F32)
     two_blocks = ((2, EVENTS, COLS), F32)
-    normed, opposite_send, opposite_mine, behind_send, behind_mine = call(
+    normed, opposite_send, opposite_mine = call(
         first_kernel,
-        [((EVENTS, 512), BF16)] + [block] * 4,
+        [((EVENTS, 512), BF16), block, block],
         (place, queries, total, factor, other, gain, staged),
         scalars=1,
-        flops=430_000_000,
-        moved=6_000_000,
+        flops=230_000_000,
+        moved=4_000_000,
     )
 
     def core_sum(mine, both):
@@ -342,8 +353,11 @@
 
     opposite_both = lax.all_gather(opposite_send, "tp", axis_index_groups=CORE_PAIRS)
     opposite = core_sum(opposite_mine, opposite_both)
-    opposite, behind_send = lax.optimization_barrier((opposite, behind_send))
+    opposite, normed = lax.optimization_barrier((opposite, normed))
     ahead_got = lax.ppermute(opposite, "tp", ONWARD)
+    behind_send, behind_mine = call(
+        behind_kernel, [block, block], (place, normed, staged), scalars=1, flops=200_000_000, moved=2_500_000
+    )
     behind_both = lax.all_gather(behind_send, "tp", axis_index_groups=CORE_PAIRS)
     behind_both, normed = lax.optimization_barrier((behind_both, normed))
     behind = core_sum(behind_mine, behind_both)

time: 118 us -> 116 us (0.983)
  the two profiles are of different devices: /device:TPU:1 before, /device:TPU:16 now
where the time goes in v8:
time: 116 us
  blocking collectives  76.1 us (66%)
  starting transfers between devices  17.9 us (15%)
  waiting for transfers between devices  13.6 us (12%)
  Pallas kernels  7.79 us (7%)
    all_to_all x2, blocking collectives, exchange_pieces(): pieces = lax.all_to_all(pieces, 'ctx', 0, 0, axis_index_groups=SIDE_GROUPS)  57.9 us
    all_gather x1, blocking collectives, body(): both = lax.all_gather(sent, 'ctx', axis_index_groups=SIDE_PAIRS)  8.81 us
    pallas_call x14, Pallas kernels, call(): pl.pallas_call(kernel, out_shape=shapes, in_specs=specs, out_specs=[pl.Bl...  7.79 us
    ppermute x1, waiting for transfers between devices, body(): ahead_got = lax.ppermute(opposite, 'tp', ONWARD)  6.88 us
    ppermute x1, starting transfers between devices, body(): two = lax.ppermute(passed, 'tp', ONWARD)  6.5 us
    ppermute x1, waiting for transfers between devices, body(): two = lax.ppermute(passed, 'tp', ONWARD)  5.77 us
    ppermute x1, starting transfers between devices, body(): ahead_got = lax.ppermute(opposite, 'tp', ONWARD)  5.71 us
    ppermute x1, starting transfers between devices, body(): other = lax.ppermute(own, 'ctx', SIDE_SWAP)  3.5 us
  transfers between devices with their start and end apart: 4, of which 3 were waited for; matrix products, arithmetic and copies ran while one was open for 0% of the time, Pallas kernels for 4%

profile of v8, /device:TPU:16, one launch (start us, length us, event | category | flops | bytes accessed | tf_op | source)
XLA Modules:
  0.0 115.7 jit_solution(625479381760146404)
XLA Ops:
  0.0 1.5 %shard_map.73 = (f32[520,128]{1,0:T(8,128)S(1)}, f32[512,128]{1,0:T(8,128)S(1)}, f32[4,128]{1,0:T(4,128)S(1)}) custom-call(s32[1]{0:T(128)} %bitcast.1.side_ref, bf16[128,512]{1,0:T(8,128)(2,1)} %key_ref.1, bf16[128,512]{1,0:T(8,128)(2,1)} %value_ref.1, f32[4,128]{1,0:T(4,128)} %log_ref.1, s32[1,128]{1,0:T(1,128)} %bitcast.23), custom_call_target="tpu_custom_call" | custom-call | flops 70000000 | bytes 900000 | tf_op jit(solution)/shard_map/pallas_call | solution.py:48
  1.5 8.8 %all-gather = f32[1040,128]{1,0:T(8,128)S(1)} all-gather(f32[520,128]{1,0:T(8,128)S(1)} %get-tuple-element.27), channel_id=2, replica_groups={{0,8},{16,24},{32,40},{48,56},{64,72},{80,88},{96,104},{112,120},{128,1..., dimensions={0}, use_global_device_ids=true | all-gather | bytes 798720 | tf_op jit(solution)/shard_map/all_gather | solution.py:312
  10.4 35.8 %all_to_all.10 = f32[48,3,4,128]{3,2,1,0:T(4,128)S(1)} all-to-all(f32[48,3,4,128]{3,2,1,0:T(4,128)S(1)} %bitcast.22), channel_id=1, replica_groups={{0,16,32,48,64,80,96,112,128,144,160,176,192,208,224,240,256,272,288,30..., dimensions={0} | all-to-all | bytes 589824 | tf_op jit(solution)/shard_map/all_to_all | solution.py:283
  46.2 0.1 shard_map.75
  46.3 22.0 %all_to_all.11 = f32[48,3,4,128]{3,2,1,0:T(4,128)S(1)} all-to-all(f32[48,3,4,128]{3,2,1,0:T(4,128)S(1)} %bitcast.21), channel_id=1, replica_groups={{0,16,32,48,64,80,96,112,128,144,160,176,192,208,224,240,256,272,288,30..., dimensions={0} | all-to-all | bytes 589824 | tf_op jit(solution)/shard_map/all_to_all | solution.py:283
  68.3 3.5 %collective-permute-start = (f32[512,128]{1,0:T(8,128)S(1)}, f32[512,128]{1,0:T(8,128)S(1)}, u32[]{:S(2)}, u32[]{:S(2)}) collective-permute-start(f32[512,128]{1,0:T(8,128)S(1)} %shard_map.76.own_ref), channel_id=1, source_target_pairs={{0,8},{8,0},{16,24},{24,16},{32,40},{40,32},{48,56},{56,48},{64,72... | collective-permute-start | bytes 786440 | tf_op jit(solution)/shard_map/ppermute | solution.py:320
  71.9 3.0 %shard_map.78.w_ref = bf16[8,512,768]{2,1,0:T(8,128)(2,1)S(1)} custom-call(bf16[512,6144]{1,0:T(8,128)(2,1)} %w_hbm), custom_call_target="tpu_custom_call" | custom-call | bytes 12600000 | tf_op jit(solution)/shard_map/pallas_call | solution.py:48
  75.0 0.7 shard_map.77
  75.6 1.0 collective-permute-done.other_ref
  76.6 0.6 shard_map.79
  77.2 2.4 %all-gather.1 = f32[256,768]{1,0:T(8,128)S(1)} all-gather(f32[128,768]{1,0:T(8,128)S(1)} %get-tuple-element.37), channel_id=3, replica_groups={{0,1},{2,3},{4,5},{6,7},{8,9},{10,11},{12,13},{14,15},{16,17},{18,19},{..., dimensions={0}, use_global_device_ids=true | all-gather | bytes 1179648 | tf_op jit(solution)/shard_map/all_gather | solution.py:354
  79.6 5.7 %collective-permute-start.2 = (f32[128,768]{1,0:T(8,128)S(1)}, f32[128,768]{1,0:T(8,128)S(1)}, u32[]{:S(2)}, u32[]{:S(2)}) collective-permute-start(f32[128,768]{1,0:T(8,128)S(1)} %shard_map.80), channel_id=1, source_target_pairs={{0,2},{1,7},{2,4},{3,1},{4,6},{5,3},{6,0},{7,5},{8,10},{9,15},{10,... | collective-permute-start | bytes 1179656 | tf_op jit(solution)/shard_map/ppermute | solution.py:357
  85.4 0.4 shard_map.81
  85.7 2.4 %all-gather.2 = f32[256,768]{1,0:T(8,128)S(1)} all-gather(f32[128,768]{1,0:T(8,128)S(1)} %get-tuple-element.40), channel_id=4, replica_groups={{0,1},{2,3},{4,5},{6,7},{8,9},{10,11},{12,13},{14,15},{16,17},{18,19},{..., dimensions={0}, use_global_device_ids=true | all-gather | bytes 1179648 | tf_op jit(solution)/shard_map/all_gather | solution.py:361
  88.2 2.2 %collective-permute-start.1 = (f32[128,768]{1,0:T(8,128)S(1)}, f32[128,768]{1,0:T(8,128)S(1)}, u32[]{:S(2)}, u32[]{:S(2)}) collective-permute-start(f32[128,768]{1,0:T(8,128)S(1)} %shard_map.83), channel_id=1, source_target_pairs={{0,6},{1,3},{2,0},{3,5},{4,2},{5,7},{6,4},{7,1},{8,14},{9,11},{10,... | collective-permute-start | bytes 1179656 | tf_op jit(solution)/shard_map/ppermute | solution.py:364
  90.3 0.6 shard_map.82
  90.9 2.4 %all-gather.4 = f32[256,768]{1,0:T(8,128)S(1)} all-gather(f32[128,768]{1,0:T(8,128)S(1)} %get-tuple-element.47), channel_id=6, replica_groups={{0,1},{2,3},{4,5},{6,7},{8,9},{10,11},{12,13},{14,15},{16,17},{18,19},{..., dimensions={0}, use_global_device_ids=true | all-gather | bytes 1179648 | tf_op jit(solution)/shard_map/all_gather | solution.py:368
  93.3 6.9 %collective-permute-done.2.more_ref = f32[128,768]{1,0:T(8,128)S(1)} collective-permute-done((f32[128,768]{1,0:T(8,128)S(1)}, f32[128,768]{1,0:T(8,128)S(1)}, u32[]{:S(2)}, u32[]{:S(2)}) %collective-permute-start.2) | collective-permute-done | bytes 393248 | tf_op jit(solution)/shard_map/ppermute | solution.py:357
  100.2 0.1 shard_map.85
  100.3 6.5 %collective-permute-start.3 = (f32[128,768]{1,0:T(8,128)S(1)}, f32[128,768]{1,0:T(8,128)S(1)}, u32[]{:S(2)}, u32[]{:S(2)}) collective-permute-start(f32[128,768]{1,0:T(8,128)S(1)} %shard_map.85), channel_id=1, source_target_pairs={{0,2},{1,7},{2,4},{3,1},{4,6},{5,3},{6,0},{7,5},{8,10},{9,15},{10,... | collective-permute-start | bytes 1179656 | tf_op jit(solution)/shard_map/ppermute | solution.py:371
  106.8 2.4 %all-gather.3 = f32[256,768]{1,0:T(8,128)S(1)} all-gather(f32[128,768]{1,0:T(8,128)S(1)} %get-tuple-element.43), channel_id=5, replica_groups={{0,1},{2,3},{4,5},{6,7},{8,9},{10,11},{12,13},{14,15},{16,17},{18,19},{..., dimensions={0}, use_global_device_ids=true | all-gather | bytes 1179648 | tf_op jit(solution)/shard_map/all_gather | solution.py:369
  109.1 0.1 shard_map.84.one_ref
  109.2 5.8 %collective-permute-done.3.two_ref = f32[128,768]{1,0:T(8,128)S(1)} collective-permute-done((f32[128,768]{1,0:T(8,128)S(1)}, f32[128,768]{1,0:T(8,128)S(1)}, u32[]{:S(2)}, u32[]{:S(2)}) %collective-permute-start.3) | collective-permute-done | bytes 393248 | tf_op jit(solution)/shard_map/ppermute | solution.py:371
  115.0 0.7 shard_map.86
  (17 shorter events, 0.2 us)
Async XLA Ops:
  68.3 8.3 %collective-permute-start = (f32[512,128]{1,0:T(8,128)S(1)}, f32[512,128]{1,0:T(8,128)S(1)}, u32[]{:S(2)}, u32[]{:S(2)}) collective-permute-start(f32[512,128]{1,0:T(8,128)S(1)} %shard_map.76.own_ref), channel_id=1, source_target_pairs={{0,8},{8,0},{16,24},{24,16},{32,40},{40,32},{48,56},{56,48},{64,72... | collective-permute-start | bytes 786440 | tf_op jit(solution)/shard_map/ppermute | solution.py:320
  71.9 3.1 %copy-start = (bf16[128,512]{1,0:T(8,128)(2,1)S(1)}, bf16[128,512]{1,0:T(8,128)(2,1)}, u32[]{:S(2)}) copy-start(bf16[128,512]{1,0:T(8,128)(2,1)} %query_ref.3) | copy-start | bytes 393220
  71.9 3.1 %copy-start.1 = (bf16[128,512]{1,0:T(8,128)(2,1)S(1)}, bf16[128,512]{1,0:T(8,128)(2,1)}, u32[]{:S(2)}) copy-start(bf16[128,512]{1,0:T(8,128)(2,1)} %key_ref.1) | copy-start | bytes 393220
  71.9 3.1 %copy-start.2 = (bf16[128,512]{1,0:T(8,128)(2,1)S(1)}, bf16[128,512]{1,0:T(8,128)(2,1)}, u32[]{:S(2)}) copy-start(bf16[128,512]{1,0:T(8,128)(2,1)} %value_ref.1) | copy-start | bytes 393220
  71.9 3.1 %copy-start.3 = (f32[4,128]{1,0:T(4,128)S(1)}, f32[4,128]{1,0:T(4,128)}, u32[]{:S(2)}) copy-start(f32[4,128]{1,0:T(4,128)} %log_ref.1) | copy-start | bytes 6148
  71.9 3.1 %copy-start.4 = (s32[128]{0:T(128)S(1)}, s32[128]{0:T(128)}, u32[]{:S(2)}) copy-start(s32[128]{0:T(128)} %param.11) | copy-start | bytes 1540
  71.9 4.7 %copy-start.5 = (f32[512]{0:T(512)S(1)}, f32[512]{0:T(512)}, u32[]{:S(2)}) copy-start(f32[512]{0:T(512)} %param.12) | copy-start | bytes 6148
  79.6 20.6 %collective-permute-start.2 = (f32[128,768]{1,0:T(8,128)S(1)}, f32[128,768]{1,0:T(8,128)S(1)}, u32[]{:S(2)}, u32[]{:S(2)}) collective-permute-start(f32[128,768]{1,0:T(8,128)S(1)} %shard_map.80), channel_id=1, source_target_pairs={{0,2},{1,7},{2,4},{3,1},{4,6},{5,3},{6,0},{7,5},{8,10},{9,15},{10,... | collective-permute-start | bytes 1179656 | tf_op jit(solution)/shard_map/ppermute | solution.py:357
  88.2 21.0 %collective-permute-start.1 = (f32[128,768]{1,0:T(8,128)S(1)}, f32[128,768]{1,0:T(8,128)S(1)}, u32[]{:S(2)}, u32[]{:S(2)}) collective-permute-start(f32[128,768]{1,0:T(8,128)S(1)} %shard_map.83), channel_id=1, source_target_pairs={{0,6},{1,3},{2,0},{3,5},{4,2},{5,7},{6,4},{7,1},{8,14},{9,11},{10,... | collective-permute-start | bytes 1179656 | tf_op jit(solution)/shard_map/ppermute | solution.py:364
  100.3 14.7 %collective-permute-start.3 = (f32[128,768]{1,0:T(8,128)S(1)}, f32[128,768]{1,0:T(8,128)S(1)}, u32[]{:S(2)}, u32[]{:S(2)}) collective-permute-start(f32[128,768]{1,0:T(8,128)S(1)} %shard_map.85), channel_id=1, source_target_pairs={{0,2},{1,7},{2,4},{3,1},{4,6},{5,3},{6,0},{7,5},{8,10},{9,15},{10,... | collective-permute-start | bytes 1179656 | tf_op jit(solution)/shard_map/ppermute | solution.py:371

commit v9 on v8

--- a/solution.py
+++ b/solution.py
@@ -20,6 +20,7 @@
 PACKED = PAIRS * CHUNK
 STATE_ROWS = HEADS_DEV * HEAD_DIM
 SENT_ROWS = STATE_ROWS + 8
+HALF = EVENTS // 2
 
 surge_log_factor = math.log(0.6)
 F32 = jnp.float32
@@ -270,12 +271,27 @@
     out_ref[...] = mine_ref[...] + both_ref[1 - (place_ref[0] & 1)]
 
 
+def core_sum_halves_kernel(place_ref, mine_ref, both_ref, top_ref, bottom_ref):
+    total = mine_ref[...] + both_ref[1 - (place_ref[0] & 1)]
+    top_ref[...] = total[:HALF]
+    bottom_ref[...] = total[HALF:]
+
+
+def top_kernel(ahead_ref, got_ref, out_ref):
+    out_ref[...] = ahead_ref[:HALF] + got_ref[...]
+
+
+def bottom_kernel(ahead_ref, got_ref, out_ref):
+    out_ref[...] = ahead_ref[HALF:] + got_ref[...]
+
+
 def three_kernel(place_ref, mine_ref, both_ref, more_ref, out_ref):
     out_ref[...] = mine_ref[...] + both_ref[1 - (place_ref[0] & 1)] + more_ref[...]
 
 
-def final_kernel(one_ref, two_ref, out_ref):
-    out_ref[...] = (one_ref[...] + two_ref[...]).astype(BF16)
+def final_kernel(one_ref, top_ref, bottom_ref, out_ref):
+    out_ref[:HALF] = (one_ref[:HALF] + top_ref[...]).astype(BF16)
+    out_ref[HALF:] = (one_ref[HALF:] + bottom_ref[...]).astype(BF16)
 
 
 def exchange_pieces(packed):
@@ -352,9 +368,13 @@
         return call(core_sum_kernel, [block], (place, mine, both), scalars=1)[0]
 
     opposite_both = lax.all_gather(opposite_send, "tp", axis_index_groups=CORE_PAIRS)
-    opposite = core_sum(opposite_mine, opposite_both)
-    opposite, normed = lax.optimization_barrier((opposite, normed))
-    ahead_got = lax.ppermute(opposite, "tp", ONWARD)
+    half = ((HALF, COLS), F32)
+    top, bottom = call(
+        core_sum_halves_kernel, [half, half], (place, opposite_mine, opposite_both), scalars=1
+    )
+    top, bottom, normed = lax.optimization_barrier((top, bottom, normed))
+    top_got = lax.ppermute(top, "tp", ONWARD)
+    bottom_got = lax.ppermute(bottom, "tp", ONWARD)
     behind_send, behind_mine = call(
         behind_kernel, [block, block], (place, normed, staged), scalars=1, flops=200_000_000, moved=2_500_000
     )
@@ -367,10 +387,15 @@
     )
     ahead_both = lax.all_gather(ahead_send, "tp", axis_index_groups=CORE_PAIRS)
     own_both = lax.all_gather(own_send, "tp", axis_index_groups=CORE_PAIRS)
-    (passed,) = call(three_kernel, [block], (place, ahead_mine, ahead_both, ahead_got), scalars=1)
-    two = lax.ppermute(passed, "tp", ONWARD)
+    ahead = core_sum(ahead_mine, ahead_both)
+    (top,) = call(top_kernel, [half], (ahead, top_got))
+    top_two = lax.ppermute(top, "tp", ONWARD)
+    (bottom,) = call(bottom_kernel, [half], (ahead, bottom_got))
+    bottom_two = lax.ppermute(bottom, "tp", ONWARD)
     (own_and_one,) = call(three_kernel, [block], (place, own_mine, own_both, one), scalars=1, moved=1_600_000)
-    (out,) = call(final_kernel, [((EVENTS, COLS), BF16)], (own_and_one, two), moved=1_000_000)
+    (out,) = call(
+        final_kernel, [((EVENTS, COLS), BF16)], (own_and_one, top_two, bottom_two), moved=1_000_000
+    )
     return out
 
 

time: 116 us -> 119 us (1.026)
  the two profiles are of different devices: /device:TPU:16 before, /device:TPU:1 now
where the time goes in v9:
time: 119 us; the launch traced here: 118 us
  blocking collectives  79.6 us (67%)
  starting transfers between devices  22.9 us (19%)
  Pallas kernels  7.82 us (7%)
  waiting for transfers between devices  7.73 us (6%)
    all_to_all x2, blocking collectives, exchange_pieces(): pieces = lax.all_to_all(pieces, 'ctx', 0, 0, axis_index_groups=SIDE_GROUPS)  57.2 us
    pallas_call x16, Pallas kernels, call(): pl.pallas_call(kernel, out_shape=shapes, in_specs=specs, out_specs=[pl.Bl...  7.82 us
    all_gather x1, blocking collectives, body(): lax.all_gather(opposite_send, 'tp', axis_index_groups=CORE_PAIRS)  7.55 us
    all_gather x1, blocking collectives, body(): both = lax.all_gather(sent, 'ctx', axis_index_groups=SIDE_PAIRS)  6.6 us
    ppermute x1, starting transfers between devices, body(): top_got = lax.ppermute(top, 'tp', ONWARD)  5.88 us
    ppermute x1, waiting for transfers between devices, body(): one = lax.ppermute(behind, 'tp', BACK)  4.98 us
    ppermute x1, starting transfers between devices, body(): top_two = lax.ppermute(top, 'tp', ONWARD)  4.97 us
    ppermute x1, starting transfers between devices, body(): bottom_got = lax.ppermute(bottom, 'tp', ONWARD)  3.76 us
  transfers between devices with their start and end apart: 6, of which 3 were waited for; matrix products, arithmetic and copies ran while one was open for 0% of the time, Pallas kernels for 4%

profile of v9, /device:TPU:1, one launch (start us, length us, event | category | flops | bytes accessed | tf_op | source)
XLA Modules:
  0.0 118.3 jit_solution(16813581059507529591)
XLA Ops:
  0.0 1.5 %shard_map.73 = (f32[520,128]{1,0:T(8,128)S(1)}, f32[512,128]{1,0:T(8,128)S(1)}, f32[4,128]{1,0:T(4,128)S(1)}) custom-call(s32[1]{0:T(128)} %bitcast.1.side_ref, bf16[128,512]{1,0:T(8,128)(2,1)} %key_ref.1, bf16[128,512]{1,0:T(8,128)(2,1)} %value_ref.1, f32[4,128]{1,0:T(4,128)} %log_ref.1, s32[1,128]{1,0:T(1,128)} %bitcast.23), custom_call_target="tpu_custom_call" | custom-call | flops 70000000 | bytes 900000 | tf_op jit(solution)/shard_map/pallas_call | solution.py:49
  1.5 6.6 %all-gather = f32[1040,128]{1,0:T(8,128)S(1)} all-gather(f32[520,128]{1,0:T(8,128)S(1)} %get-tuple-element.30), channel_id=2, replica_groups={{0,8},{16,24},{32,40},{48,56},{64,72},{80,88},{96,104},{112,120},{128,1..., dimensions={0}, use_global_device_ids=true | all-gather | bytes 798720 | tf_op jit(solution)/shard_map/all_gather | solution.py:328
  8.1 35.0 %all_to_all.10 = f32[48,3,4,128]{3,2,1,0:T(4,128)S(1)} all-to-all(f32[48,3,4,128]{3,2,1,0:T(4,128)S(1)} %bitcast.22), channel_id=1, replica_groups={{0,16,32,48,64,80,96,112,128,144,160,176,192,208,224,240,256,272,288,30..., dimensions={0} | all-to-all | bytes 589824 | tf_op jit(solution)/shard_map/all_to_all | solution.py:299
  43.1 0.1 shard_map.75
  43.2 22.2 %all_to_all.11 = f32[48,3,4,128]{3,2,1,0:T(4,128)S(1)} all-to-all(f32[48,3,4,128]{3,2,1,0:T(4,128)S(1)} %bitcast.21), channel_id=1, replica_groups={{0,16,32,48,64,80,96,112,128,144,160,176,192,208,224,240,256,272,288,30..., dimensions={0} | all-to-all | bytes 589824 | tf_op jit(solution)/shard_map/all_to_all | solution.py:299
  65.4 3.2 %collective-permute-start = (f32[512,128]{1,0:T(8,128)S(1)}, f32[512,128]{1,0:T(8,128)S(1)}, u32[]{:S(2)}, u32[]{:S(2)}) collective-permute-start(f32[512,128]{1,0:T(8,128)S(1)} %shard_map.76.own_ref), channel_id=1, source_target_pairs={{0,8},{8,0},{16,24},{24,16},{32,40},{40,32},{48,56},{56,48},{64,72... | collective-permute-start | bytes 786440 | tf_op jit(solution)/shard_map/ppermute | solution.py:336
  68.7 3.0 %shard_map.78.w_ref = bf16[8,512,768]{2,1,0:T(8,128)(2,1)S(1)} custom-call(bf16[512,6144]{1,0:T(8,128)(2,1)} %w_hbm), custom_call_target="tpu_custom_call" | custom-call | bytes 12600000 | tf_op jit(solution)/shard_map/pallas_call | solution.py:49
  71.8 0.7 shard_map.77
  72.5 0.1 collective-permute-done.other_ref
  72.6 0.6 shard_map.79
  73.2 7.6 %all-gather.1 = f32[256,768]{1,0:T(8,128)S(1)} all-gather(f32[128,768]{1,0:T(8,128)S(1)} %get-tuple-element.40), channel_id=3, replica_groups={{0,1},{2,3},{4,5},{6,7},{8,9},{10,11},{12,13},{14,15},{16,17},{18,19},{..., dimensions={0}, use_global_device_ids=true | all-gather | bytes 1179648 | tf_op jit(solution)/shard_map/all_gather | solution.py:370
  80.8 5.9 %collective-permute-start.2 = (f32[64,768]{1,0:T(8,128)S(1)}, f32[64,768]{1,0:T(8,128)S(1)}, u32[]{:S(2)}, u32[]{:S(2)}) collective-permute-start(f32[64,768]{1,0:T(8,128)S(1)} %get-tuple-element.53), channel_id=1, source_target_pairs={{0,2},{1,7},{2,4},{3,1},{4,6},{5,3},{6,0},{7,5},{8,10},{9,15},{10,... | collective-permute-start | bytes 589832 | tf_op jit(solution)/shard_map/ppermute | solution.py:376
  86.7 3.8 %collective-permute-start.4 = (f32[64,768]{1,0:T(8,128)S(1)}, f32[64,768]{1,0:T(8,128)S(1)}, u32[]{:S(2)}, u32[]{:S(2)}) collective-permute-start(f32[64,768]{1,0:T(8,128)S(1)} %get-tuple-element.54), channel_id=1, source_target_pairs={{0,2},{1,7},{2,4},{3,1},{4,6},{5,3},{6,0},{7,5},{8,10},{9,15},{10,... | collective-permute-start | bytes 589832 | tf_op jit(solution)/shard_map/ppermute | solution.py:377
  90.4 0.4 shard_map.81
  90.8 2.9 %all-gather.2 = f32[256,768]{1,0:T(8,128)S(1)} all-gather(f32[128,768]{1,0:T(8,128)S(1)} %get-tuple-element.45), channel_id=4, replica_groups={{0,1},{2,3},{4,5},{6,7},{8,9},{10,11},{12,13},{14,15},{16,17},{18,19},{..., dimensions={0}, use_global_device_ids=true | all-gather | bytes 1179648 | tf_op jit(solution)/shard_map/all_gather | solution.py:381
  93.7 0.6 shard_map.82
  94.4 2.4 %collective-permute-start.1 = (f32[128,768]{1,0:T(8,128)S(1)}, f32[128,768]{1,0:T(8,128)S(1)}, u32[]{:S(2)}, u32[]{:S(2)}) collective-permute-start(f32[128,768]{1,0:T(8,128)S(1)} %shard_map.83), channel_id=1, source_target_pairs={{0,6},{1,3},{2,0},{3,5},{4,2},{5,7},{6,4},{7,1},{8,14},{9,11},{10,... | collective-permute-start | bytes 1179656 | tf_op jit(solution)/shard_map/ppermute | solution.py:384
  96.8 2.4 %all-gather.4 = f32[256,768]{1,0:T(8,128)S(1)} all-gather(f32[128,768]{1,0:T(8,128)S(1)} %get-tuple-element.52), channel_id=6, replica_groups={{0,1},{2,3},{4,5},{6,7},{8,9},{10,11},{12,13},{14,15},{16,17},{18,19},{..., dimensions={0}, use_global_device_ids=true | all-gather | bytes 1179648 | tf_op jit(solution)/shard_map/all_gather | solution.py:388
  99.3 5.0 %collective-permute-start.3 = (f32[64,768]{1,0:T(8,128)S(1)}, f32[64,768]{1,0:T(8,128)S(1)}, u32[]{:S(2)}, u32[]{:S(2)}) collective-permute-start(f32[64,768]{1,0:T(8,128)S(1)} %shard_map.86), channel_id=1, source_target_pairs={{0,2},{1,7},{2,4},{3,1},{4,6},{5,3},{6,0},{7,5},{8,10},{9,15},{10,... | collective-permute-start | bytes 589832 | tf_op jit(solution)/shard_map/ppermute | solution.py:392
  104.3 2.7 %collective-permute-start.5 = (f32[64,768]{1,0:T(8,128)S(1)}, f32[64,768]{1,0:T(8,128)S(1)}, u32[]{:S(2)}, u32[]{:S(2)}) collective-permute-start(f32[64,768]{1,0:T(8,128)S(1)} %shard_map.87), channel_id=1, source_target_pairs={{0,2},{1,7},{2,4},{3,1},{4,6},{5,3},{6,0},{7,5},{8,10},{9,15},{10,... | collective-permute-start | bytes 589832 | tf_op jit(solution)/shard_map/ppermute | solution.py:394
  107.0 2.9 %all-gather.3 = f32[256,768]{1,0:T(8,128)S(1)} all-gather(f32[128,768]{1,0:T(8,128)S(1)} %get-tuple-element.48), channel_id=5, replica_groups={{0,1},{2,3},{4,5},{6,7},{8,9},{10,11},{12,13},{14,15},{16,17},{18,19},{..., dimensions={0}, use_global_device_ids=true | all-gather | bytes 1179648 | tf_op jit(solution)/shard_map/all_gather | solution.py:389
  109.9 5.0 %collective-permute-done.1.more_ref = f32[128,768]{1,0:T(8,128)S(1)} collective-permute-done((f32[128,768]{1,0:T(8,128)S(1)}, f32[128,768]{1,0:T(8,128)S(1)}, u32[]{:S(2)}, u32[]{:S(2)}) %collective-permute-start.1) | collective-permute-done | bytes 393248 | tf_op jit(solution)/shard_map/ppermute | solution.py:384
  115.0 2.6 %collective-permute-done.5.bottom_ref = f32[64,768]{1,0:T(8,128)S(1)} collective-permute-done((f32[64,768]{1,0:T(8,128)S(1)}, f32[64,768]{1,0:T(8,128)S(1)}, u32[]{:S(2)}, u32[]{:S(2)}) %collective-permute-start.5) | collective-permute-done | bytes 196640 | tf_op jit(solution)/shard_map/ppermute | solution.py:394
  117.6 0.7 shard_map.88
  (23 shorter events, 0.4 us)
Async XLA Ops:
  65.4 7.1 %collective-permute-start = (f32[512,128]{1,0:T(8,128)S(1)}, f32[512,128]{1,0:T(8,128)S(1)}, u32[]{:S(2)}, u32[]{:S(2)}) collective-permute-start(f32[512,128]{1,0:T(8,128)S(1)} %shard_map.76.own_ref), channel_id=1, source_target_pairs={{0,8},{8,0},{16,24},{24,16},{32,40},{40,32},{48,56},{56,48},{64,72... | collective-permute-start | bytes 786440 | tf_op jit(solution)/shard_map/ppermute | solution.py:336
  68.7 3.1 %copy-start = (bf16[128,512]{1,0:T(8,128)(2,1)S(1)}, bf16[128,512]{1,0:T(8,128)(2,1)}, u32[]{:S(2)}) copy-start(bf16[128,512]{1,0:T(8,128)(2,1)} %query_ref.3) | copy-start | bytes 393220
  68.7 3.1 %copy-start.1 = (bf16[128,512]{1,0:T(8,128)(2,1)S(1)}, bf16[128,512]{1,0:T(8,128)(2,1)}, u32[]{:S(2)}) copy-start(bf16[128,512]{1,0:T(8,128)(2,1)} %key_ref.1) | copy-start | bytes 393220
  68.7 3.1 %copy-start.2 = (bf16[128,512]{1,0:T(8,128)(2,1)S(1)}, bf16[128,512]{1,0:T(8,128)(2,1)}, u32[]{:S(2)}) copy-start(bf16[128,512]{1,0:T(8,128)(2,1)} %value_ref.1) | copy-start | bytes 393220
  68.7 3.1 %copy-start.3 = (f32[4,128]{1,0:T(4,128)S(1)}, f32[4,128]{1,0:T(4,128)}, u32[]{:S(2)}) copy-start(f32[4,128]{1,0:T(4,128)} %log_ref.1) | copy-start | bytes 6148
  68.7 3.1 %copy-start.4 = (s32[128]{0:T(128)S(1)}, s32[128]{0:T(128)}, u32[]{:S(2)}) copy-start(s32[128]{0:T(128)} %param.11) | copy-start | bytes 1540
  68.7 3.8 %copy-start.5 = (f32[512]{0:T(512)S(1)}, f32[512]{0:T(512)}, u32[]{:S(2)}) copy-start(f32[512]{0:T(512)} %param.12) | copy-start | bytes 6148
  80.8 18.5 %collective-permute-start.2 = (f32[64,768]{1,0:T(8,128)S(1)}, f32[64,768]{1,0:T(8,128)S(1)}, u32[]{:S(2)}, u32[]{:S(2)}) collective-permute-start(f32[64,768]{1,0:T(8,128)S(1)} %get-tuple-element.53), channel_id=1, source_target_pairs={{0,2},{1,7},{2,4},{3,1},{4,6},{5,3},{6,0},{7,5},{8,10},{9,15},{10,... | collective-permute-start | bytes 589832 | tf_op jit(solution)/shard_map/ppermute | solution.py:376
  86.7 17.6 %collective-permute-start.4 = (f32[64,768]{1,0:T(8,128)S(1)}, f32[64,768]{1,0:T(8,128)S(1)}, u32[]{:S(2)}, u32[]{:S(2)}) collective-permute-start(f32[64,768]{1,0:T(8,128)S(1)} %get-tuple-element.54), channel_id=1, source_target_pairs={{0,2},{1,7},{2,4},{3,1},{4,6},{5,3},{6,0},{7,5},{8,10},{9,15},{10,... | collective-permute-start | bytes 589832 | tf_op jit(solution)/shard_map/ppermute | solution.py:377
  94.4 20.5 %collective-permute-start.1 = (f32[128,768]{1,0:T(8,128)S(1)}, f32[128,768]{1,0:T(8,128)S(1)}, u32[]{:S(2)}, u32[]{:S(2)}) collective-permute-start(f32[128,768]{1,0:T(8,128)S(1)} %shard_map.83), channel_id=1, source_target_pairs={{0,6},{1,3},{2,0},{3,5},{4,2},{5,7},{6,4},{7,1},{8,14},{9,11},{10,... | collective-permute-start | bytes 1179656 | tf_op jit(solution)/shard_map/ppermute | solution.py:384
  99.3 15.7 %collective-permute-start.3 = (f32[64,768]{1,0:T(8,128)S(1)}, f32[64,768]{1,0:T(8,128)S(1)}, u32[]{:S(2)}, u32[]{:S(2)}) collective-permute-start(f32[64,768]{1,0:T(8,128)S(1)} %shard_map.86), channel_id=1, source_target_pairs={{0,2},{1,7},{2,4},{3,1},{4,6},{5,3},{6,0},{7,5},{8,10},{9,15},{10,... | collective-permute-start | bytes 589832 | tf_op jit(solution)/shard_map/ppermute | solution.py:392
  104.3 13.3 %collective-permute-start.5 = (f32[64,768]{1,0:T(8,128)S(1)}, f32[64,768]{1,0:T(8,128)S(1)}, u32[]{:S(2)}, u32[]{:S(2)}) collective-permute-start(f32[64,768]{1,0:T(8,128)S(1)} %shard_map.87), channel_id=1, source_target_pairs={{0,2},{1,7},{2,4},{3,1},{4,6},{5,3},{6,0},{7,5},{8,10},{9,15},{10,... | collective-permute-start | bytes 589832 | tf_op jit(solution)/shard_map/ppermute | solution.py:394

commit v10 on v5

--- a/solution.py
+++ b/solution.py
@@ -18,6 +18,9 @@
 CHUNK = ROWS + 1
 HEAD_ROWS = PIECES * CHUNK
 PACKED = PAIRS * CHUNK
+STATE_ROWS = HEADS_DEV * HEAD_DIM
+SENT_ROWS = STATE_ROWS + 8
+HALF = EVENTS // 2
 RING = 4
 
 surge_log_factor = math.log(0.6)
@@ -105,13 +108,14 @@
     ]
     for copy in copies:
         copy.start()
-    for copy in copies:
+    for copy in copies[:2]:
         copy.wait()
     _, columns, _ = event_sums(log_ref, boundary_ref)
     ends, sent, kept = factors(side_ref[0], columns)
     decay = jnp.exp(ends)
-    sent_ref[...] = jnp.zeros_like(sent_ref)
-    kept_ref[...] = jnp.zeros_like(kept_ref)
+    for copy in copies[2:]:
+        copy.wait()
+    sent_ref[STATE_ROWS:, :] = jnp.zeros((SENT_ROWS - STATE_ROWS, HEAD_DIM), F32)
     for head in range(HEADS_DEV):
         lanes = slice(head * HEAD_DIM, (head + 1) * HEAD_DIM)
         value = value_ref[:, lanes].astype(F32)
@@ -122,23 +126,27 @@
             (((0,), (0,)), ((), ())),
             preferred_element_type=F32,
         )
-        sent_term = product[:, :128] + product[:, 128:256]
-        kept_term = product[:, 256:384] + product[:, 384:]
+        sent_ref[lanes, :] = product[:, :128] + product[:, 128:256]
+        kept_ref[lanes, :] = product[:, 256:384] + product[:, 384:]
         whole_row = jnp.broadcast_to(decay[:, head : head + 1], (1, HEAD_DIM))
         decay_ref[head : head + 1, :] = whole_row
+        sent_ref[STATE_ROWS + head : STATE_ROWS + head + 1, :] = whole_row
+
+
+def combine_kernel(side_ref, kept_ref, both_ref, decay_ref, out_ref):
+    other = 1 - side_ref[0]
+    for head in range(HEADS_DEV):
+        decay = decay_ref[head : head + 1, :]
+        rows = slice(head * HEAD_DIM, (head + 1) * HEAD_DIM)
+        state = kept_ref[rows, :] + decay * both_ref[other, rows, :]
+        last = STATE_ROWS + head
+        decay = decay * both_ref[other, last : last + 1, :]
         for piece in range(PIECES):
             count, first = piece_rows(piece), head * HEAD_ROWS + piece * CHUNK
-            rows = slice(ROWS * piece, ROWS * piece + count)
-            sent_ref[first : first + count, :] = sent_term[rows]
-            kept_ref[first : first + count, :] = kept_term[rows]
-            sent_ref[first + ROWS : first + CHUNK, :] = whole_row
-
-
-def combine_kernel(side_ref, kept_ref, both_ref, decay_ref, out_ref, got_ref):
-    got_ref[...] = both_ref[1 - side_ref[0]]
-    for head in range(HEADS_DEV):
-        rows = slice(head * HEAD_ROWS, (head + 1) * HEAD_ROWS)
-        out_ref[rows, :] = kept_ref[rows, :] + decay_ref[head : head + 1, :] * got_ref[rows, :]
+            part = [state[ROWS * piece : ROWS * piece + count]]
+            if count < ROWS:
+                part.append(jnp.zeros((ROWS - count, HEAD_DIM), F32))
+            out_ref[first : first + CHUNK, :] = jnp.concatenate(part + [decay], axis=0)
 
 
 def scan_kernel(side_ref, term_ref, out_ref):
@@ -159,12 +167,12 @@
         run(range(PAIRS - 1, -1, -1))
 
 
-def unpack(packed_ref, head):
-    parts = []
-    for piece in range(PIECES):
-        first = head * HEAD_ROWS + piece * CHUNK
-        parts.append(packed_ref[first : first + piece_rows(piece), :])
-    return jnp.concatenate(parts, axis=0)
+def unpack_kernel(packed_ref, state_ref):
+    for piece in range(PAIRS):
+        head, place = divmod(piece, PIECES)
+        first = head * HEAD_DIM + ROWS * place
+        count = piece_rows(place)
+        state_ref[first : first + count, :] = packed_ref[piece * CHUNK : piece * CHUNK + count, :]
 
 
 def times_state(query, state):
@@ -173,13 +181,14 @@
 
 
 def inner_kernel(
-    side_ref, query_ref, key_ref, value_ref, log_ref, boundary_ref, got_ref, own_ref, total_ref, factor_ref
+    side_ref, query_ref, key_ref, value_ref, log_ref, boundary_ref, both_ref, own_ref, total_ref, factor_ref
 ):
     rate, columns, upper = event_sums(log_ref, boundary_ref)
     rows_cum = lax.dot_general(
         rate, upper, (((1,), (0,)), ((), ())), precision=lax.Precision.HIGHEST, preferred_element_type=F32
     )
-    _, own, other = factors(side_ref[0], columns)
+    side = side_ref[0]
+    _, own, other = factors(side, columns)
     for head in range(HEADS_DEV):
         lanes = slice(head * HEAD_DIM, (head + 1) * HEAD_DIM)
         query = query_ref[:, lanes]
@@ -189,8 +198,9 @@
         weight = jnp.exp(-jnp.abs(columns[:, head : head + 1] - rows_cum[head : head + 1, :]))
         probs = (logits * weight).astype(BF16)
         intra = jnp.dot(probs, value_ref[:, lanes], preferred_element_type=F32)
-        last = head * HEAD_ROWS + ROWS
-        state = unpack(got_ref, head) + got_ref[last : last + 1, :] * unpack(own_ref, head)
+        last = STATE_ROWS + head
+        got_decay = both_ref[1 - side, last : last + 1, :]
+        state = both_ref[1 - side, lanes, :] + got_decay * own_ref[lanes, :]
         total_ref[:, lanes] = intra + own[:, head : head + 1] * times_state(query, state)
         factor_ref[:, lanes] = jnp.broadcast_to(other[:, head : head + 1], (EVENTS, HEAD_DIM))
 
@@ -249,7 +259,7 @@
     for head in range(HEADS_DEV):
         lanes = slice(head * HEAD_DIM, (head + 1) * HEAD_DIM)
         total = total_ref[:, lanes] + factor_ref[:, lanes] * times_state(
-            query_ref[:, lanes], unpack(other_ref, head)
+            query_ref[:, lanes], other_ref[lanes, :]
         )
         average = jnp.mean(total * total, axis=1, keepdims=True)
         scaled = total * lax.rsqrt(average + 1e-06) * gain_ref[:, lanes]
@@ -262,8 +272,10 @@
     return jnp.dot(normed, w_ref[((place >> 1) + far) & 3], preferred_element_type=F32)
 
 
-def opposite_kernel(place_ref, both_ref, w_ref, out_ref):
-    out_ref[...] = project(place_ref[0], both_ref, w_ref, 2)
+def opposite_kernel(place_ref, both_ref, w_ref, top_ref, bottom_ref):
+    total = project(place_ref[0], both_ref, w_ref, 2)
+    top_ref[...] = total[:HALF]
+    bottom_ref[...] = total[HALF:]
 
 
 def behind_kernel(place_ref, both_ref, w_ref, out_ref):
@@ -271,17 +283,26 @@
     out_ref[...] = project(place, both_ref, w_ref, 3 - 2 * (place & 1))
 
 
-def ahead_kernel(place_ref, both_ref, w_ref, got_ref, out_ref):
+def ahead_kernel(place_ref, both_ref, w_ref, out_ref):
     place = place_ref[0]
-    out_ref[...] = project(place, both_ref, w_ref, 1 + 2 * (place & 1)) + got_ref[...]
+    out_ref[...] = project(place, both_ref, w_ref, 1 + 2 * (place & 1))
+
+
+def top_kernel(ahead_ref, got_ref, out_ref):
+    out_ref[...] = ahead_ref[:HALF] + got_ref[...]
+
+
+def bottom_kernel(ahead_ref, got_ref, out_ref):
+    out_ref[...] = ahead_ref[HALF:] + got_ref[...]
 
 
 def own_kernel(place_ref, both_ref, w_ref, got_ref, out_ref):
     out_ref[...] = project(place_ref[0], both_ref, w_ref, 0) + got_ref[...]
 
 
-def final_kernel(one_ref, two_ref, out_ref):
-    out_ref[...] = (one_ref[...] + two_ref[...]).astype(BF16)
+def final_kernel(one_ref, top_ref, bottom_ref, out_ref):
+    out_ref[:HALF] = (one_ref[:HALF] + top_ref[...]).astype(BF16)
+    out_ref[HALF:] = (one_ref[HALF:] + bottom_ref[...]).astype(BF16)
 
 
 def exchange_pieces(packed):
@@ -296,10 +317,11 @@
     boundary = boundary.reshape(1, EVENTS)
     gain = gain.reshape(1, 512)
     packed = ((PACKED, HEAD_DIM), F32)
+    state = ((STATE_ROWS, HEAD_DIM), F32)
 
     sent, kept, decay = call(
         terms_kernel,
-        [packed, packed, ((HEADS_DEV, HEAD_DIM), F32)],
+        [((SENT_ROWS, HEAD_DIM), F32), state, ((HEADS_DEV, HEAD_DIM), F32)],
         (side, keys, values, state_retention_log, boundary),
         scalars=1,
         scratch=[
@@ -315,8 +337,8 @@
         out_space=pltpu.VMEM,
     )
     both = lax.all_gather(sent, "ctx", axis_index_groups=SIDE_PAIRS)
-    pair_terms, got = call(
-        combine_kernel, [packed, packed], (side, kept, both, decay), scalars=1, flops=200_000, moved=1_500_000
+    (pair_terms,) = call(
+        combine_kernel, [packed], (side, kept, both, decay), scalars=1, flops=200_000, moved=1_100_000
     )
     pair_terms, w_late = lax.optimization_barrier((pair_terms, w_out))
     (wide,) = call(
@@ -336,7 +358,7 @@
     wide_got = lax.ppermute(wide, "tp", CORE_SWAP)
     slices = exchange_pieces(pair_terms)
     (states,) = call(scan_kernel, [packed], (side, slices), scalars=1, flops=50_000_000_000, moved=600_000)
-    own = exchange_pieces(states)
+    (own,) = call(unpack_kernel, [state], (exchange_pieces(states),), moved=600_000)
     own, w_late = lax.optimization_barrier((own, w_late))
     other = lax.ppermute(own, "ctx", SIDE_SWAP)
     staged = stage(place, w_late, wide_got)
@@ -345,26 +367,37 @@
     total, factor = call(
         inner_kernel,
         [inner, inner],
-        (side, queries, keys, values, state_retention_log, boundary, got, own),
+        (side, queries, keys, values, state_retention_log, boundary, both, own),
         scalars=1,
         flops=100_000_000,
         moved=1_500_000,
     )
     block = ((EVENTS, COLS), F32)
+    half = ((HALF, COLS), F32)
     (normed,) = call(
         normed_kernel, [inner], (queries, total, factor, other, gain), flops=70_000_000, moved=1_300_000
     )
-    both = lax.all_gather(normed, "tp", axis_index_groups=CORE_PAIRS)
-
-    def step(kernel, *args):
-        args = (place, both, staged) + args
-        return call(kernel, [block], args, scalars=1, flops=200_000_000, moved=2_500_000)[0]
-
-    ahead_got = lax.ppermute(step(opposite_kernel), "tp", ONWARD)
-    one = lax.ppermute(step(behind_kernel), "tp", BACK)
-    two = lax.ppermute(step(ahead_kernel, ahead_got), "tp", ONWARD)
-    own_and_one = step(own_kernel, one)
-    (out,) = call(final_kernel, [((EVENTS, COLS), BF16)], (own_and_one, two), moved=1_000_000)
+    both_normed = lax.all_gather(normed, "tp", axis_index_groups=CORE_PAIRS)
+
+    def step(kernel, outs, *args):
+        args = (place, both_normed, staged) + args
+        return call(kernel, outs, args, scalars=1)
+
+    top, bottom = step(opposite_kernel, [half, half])
+    top, bottom, both_normed = lax.optimization_barrier((top, bottom, both_normed))
+    top_got = lax.ppermute(top, "tp", ONWARD)
+    bottom_got = lax.ppermute(bottom, "tp", ONWARD)
+    (behind,) = step(behind_kernel, [block])
+    one = lax.ppermute(behind, "tp", BACK)
+    (ahead,) = step(ahead_kernel, [block])
+    (top,) = call(top_kernel, [half], (ahead, top_got))
+    top_two = lax.ppermute(top, "tp", ONWARD)
+    (bottom,) = call(bottom_kernel, [half], (ahead, bottom_got))
+    bottom_two = lax.ppermute(bottom, "tp", ONWARD)
+    (own_and_one,) = step(own_kernel, [block], one)
+    (out,) = call(
+        final_kernel, [((EVENTS, COLS), BF16)], (own_and_one, top_two, bottom_two), moved=1_000_000
+    )
     return out
 
 

time: 119 us -> 119 us (level)
  the two profiles are of different devices: /device:TPU:1 before, /device:TPU:40 now
where the time goes in v10:
time: 119 us
  starting transfers between devices  37.6 us (32%)
  blocking collectives  33.2 us (28%)
  waiting for transfers between devices  33.2 us (28%)
  Pallas kernels  14.3 us (12%)
    all_to_all x1, blocking collectives, exchange_pieces(): pieces = lax.all_to_all(pieces, 'ctx', 0, 0, axis_index_groups=SIDE_GROUPS)  22.2 us
    all_to_all x1, starting transfers between devices, exchange_pieces(): pieces = lax.all_to_all(pieces, 'ctx', 0, 0, axis_index_groups=SIDE_GROUPS)  18.3 us
    all_to_all x1, waiting for transfers between devices, exchange_pieces(): pieces = lax.all_to_all(pieces, 'ctx', 0, 0, axis_index_groups=SIDE_GROUPS)  11.8 us
    pallas_call x14, Pallas kernels, call(): pl.pallas_call(kernel, out_shape=shapes, in_specs=specs, out_specs=[pl.Bl...  9.63 us
    ppermute x1, waiting for transfers between devices, body(): bottom_got = lax.ppermute(bottom, 'tp', ONWARD)  9.12 us
    all_gather x1, blocking collectives, body(): both = lax.all_gather(sent, 'ctx', axis_index_groups=SIDE_PAIRS)  8.81 us
    ppermute x1, waiting for transfers between devices, body(): bottom_two = lax.ppermute(bottom, 'tp', ONWARD)  8.06 us
    ppermute x1, starting transfers between devices, body(): one = lax.ppermute(behind, 'tp', BACK)  5.26 us
  transfers between devices with their start and end apart: 8, of which 5 were waited for; matrix products, arithmetic and copies ran while one was open for 0% of the time, Pallas kernels for 9%

profile of v10, /device:TPU:40, one launch (start us, length us, event | category | flops | bytes accessed | tf_op | source)
XLA Modules:
  0.0 118.6 jit_solution(13231020369534750771)
XLA Ops:
  0.0 1.5 %shard_map.73 = (f32[520,128]{1,0:T(8,128)S(1)}, f32[512,128]{1,0:T(8,128)S(1)}, f32[4,128]{1,0:T(4,128)S(1)}) custom-call(s32[1]{0:T(128)} %bitcast.1.side_ref, bf16[128,512]{1,0:T(8,128)(2,1)} %key_ref.1, bf16[128,512]{1,0:T(8,128)(2,1)} %value_ref.1, f32[4,128]{1,0:T(4,128)} %log_ref.1, s32[1,128]{1,0:T(1,128)} %bitcast.20), custom_call_target="tpu_custom_call" | custom-call | flops 70000000 | bytes 900000 | tf_op jit(solution)/shard_map/pallas_call | solution.py:50
  1.5 8.8 %all-gather = f32[1040,128]{1,0:T(8,128)S(1)} all-gather(f32[520,128]{1,0:T(8,128)S(1)} %get-tuple-element.21), channel_id=2, replica_groups={{0,8},{16,24},{32,40},{48,56},{64,72},{80,88},{96,104},{112,120},{128,1..., dimensions={0}, use_global_device_ids=true | all-gather | bytes 798720 | tf_op jit(solution)/shard_map/all_gather | solution.py:339
  10.3 0.8 shard_map.74
  11.1 18.3 %all-to-all-start = ((f32[48,3,4,128]{3,2,1,0:T(4,128)}), f32[48,3,4,128]{3,2,1,0:T(4,128)S(1)}, u32[]{:S(2)}, u32[]{:S(2)}) async-start(f32[48,3,4,128]{3,2,1,0:T(4,128)} %bitcast.4), calls=%async_computation | async-start | bytes 589824 | tf_op jit(solution)/shard_map/all_to_all | solution.py:310
  29.4 4.0 %shard_map.78 = f32[4,512,768]{2,1,0:T(8,128)} custom-call(s32[1]{0:T(128)} %bitcast.place_ref, bf16[512,6144]{1,0:T(8,128)(2,1)} %w_hbm.1), custom_call_target="tpu_custom_call" | custom-call | bytes 9500000 | tf_op jit(solution)/shard_map/pallas_call | solution.py:50
  33.4 1.9 %collective-permute-start.1 = (f32[4,512,768]{2,1,0:T(8,128)}, f32[4,512,768]{2,1,0:T(8,128)}, u32[]{:S(2)}, u32[]{:S(2)}) collective-permute-start(f32[4,512,768]{2,1,0:T(8,128)} %shard_map.78), channel_id=1, source_target_pairs={{0,1},{1,0},{2,3},{3,2},{4,5},{5,4},{6,7},{7,6},{8,9},{9,8},{10,11... | collective-permute-start | bytes 18874376 | tf_op jit(solution)/shard_map/ppermute | solution.py:358
  35.3 11.8 %all-to-all-done = f32[48,3,4,128]{3,2,1,0:T(4,128)S(1)} async-done(((f32[48,3,4,128]{3,2,1,0:T(4,128)}), f32[48,3,4,128]{3,2,1,0:T(4,128)S(1)}, u32[]{:S(2)}, u32[]{:S(2)}) %all-to-all-start) | async-done | bytes 294944 | tf_op jit(solution)/shard_map/all_to_all | solution.py:310
  47.2 22.2 %all_to_all.10 = f32[48,3,4,128]{3,2,1,0:T(4,128)S(1)} all-to-all(f32[48,3,4,128]{3,2,1,0:T(4,128)S(1)} %bitcast.18), channel_id=1, replica_groups={{0,16,32,48,64,80,96,112,128,144,160,176,192,208,224,240,256,272,288,30..., dimensions={0} | all-to-all | bytes 589824 | tf_op jit(solution)/shard_map/all_to_all | solution.py:310
  69.4 3.3 %collective-permute-start = (f32[512,128]{1,0:T(8,128)S(1)}, f32[512,128]{1,0:T(8,128)S(1)}, u32[]{:S(2)}, u32[]{:S(2)}) collective-permute-start(f32[512,128]{1,0:T(8,128)S(1)} %shard_map.76.own_ref), channel_id=1, source_target_pairs={{0,8},{8,0},{16,24},{24,16},{32,40},{40,32},{48,56},{56,48},{64,72... | collective-permute-start | bytes 786440 | tf_op jit(solution)/shard_map/ppermute | solution.py:363
  72.8 0.7 shard_map.77
  73.5 4.7 %shard_map.79.w_ref = bf16[4,1024,768]{2,1,0:T(8,128)(2,1)S(1)} custom-call(s32[1]{0:T(128)} %bitcast.place_ref, bf16[512,6144]{1,0:T(8,128)(2,1)} %w_hbm.1, f32[4,512,768]{2,1,0:T(8,128)} %collective-permute-done.1.wide_ref), custom_call_target="tpu_custom_call" | custom-call | bytes 16000000 | tf_op jit(solution)/shard_map/pallas_call | solution.py:243
  78.5 2.2 %all-gather.1 = f32[256,512]{1,0:T(8,128)S(1)} all-gather(f32[128,512]{1,0:T(8,128)S(1)} %shard_map.80), channel_id=3, replica_groups={{0,1},{2,3},{4,5},{6,7},{8,9},{10,11},{12,13},{14,15},{16,17},{18,19},{..., dimensions={0}, use_global_device_ids=true | all-gather | bytes 786432 | tf_op jit(solution)/shard_map/all_gather | solution.py:380
  81.0 2.7 %collective-permute-start.3 = (f32[64,768]{1,0:T(8,128)S(1)}, f32[64,768]{1,0:T(8,128)S(1)}, u32[]{:S(2)}, u32[]{:S(2)}) collective-permute-start(f32[64,768]{1,0:T(8,128)S(1)} %get-tuple-element.35), channel_id=1, source_target_pairs={{0,2},{1,7},{2,4},{3,1},{4,6},{5,3},{6,0},{7,5},{8,10},{9,15},{10,... | collective-permute-start | bytes 589832 | tf_op jit(solution)/shard_map/ppermute | solution.py:388
  84.1 5.3 %collective-permute-start.2 = (f32[128,768]{1,0:T(8,128)S(1)}, f32[128,768]{1,0:T(8,128)S(1)}, u32[]{:S(2)}, u32[]{:S(2)}) collective-permute-start(f32[128,768]{1,0:T(8,128)S(1)} %shard_map.82), channel_id=1, source_target_pairs={{0,6},{1,3},{2,0},{3,5},{4,2},{5,7},{6,4},{7,1},{8,14},{9,11},{10,... | collective-permute-start | bytes 1179656 | tf_op jit(solution)/shard_map/ppermute | solution.py:391
  89.4 1.9 %collective-permute-start.5 = (f32[64,768]{1,0:T(8,128)S(1)}, f32[64,768]{1,0:T(8,128)S(1)}, u32[]{:S(2)}, u32[]{:S(2)}) collective-permute-start(f32[64,768]{1,0:T(8,128)S(1)} %get-tuple-element.36), channel_id=1, source_target_pairs={{0,2},{1,7},{2,4},{3,1},{4,6},{5,3},{6,0},{7,5},{8,10},{9,15},{10,... | collective-permute-start | bytes 589832 | tf_op jit(solution)/shard_map/ppermute | solution.py:389
  91.3 0.4 shard_map.84.ahead_ref
  91.7 3.0 %collective-permute-done.3.got_ref = f32[64,768]{1,0:T(8,128)S(1)} collective-permute-done((f32[64,768]{1,0:T(8,128)S(1)}, f32[64,768]{1,0:T(8,128)S(1)}, u32[]{:S(2)}, u32[]{:S(2)}) %collective-permute-start.3) | collective-permute-done | bytes 196640 | tf_op jit(solution)/shard_map/ppermute | solution.py:388
  94.7 2.4 %collective-permute-start.4 = (f32[64,768]{1,0:T(8,128)S(1)}, f32[64,768]{1,0:T(8,128)S(1)}, u32[]{:S(2)}, u32[]{:S(2)}) collective-permute-start(f32[64,768]{1,0:T(8,128)S(1)} %shard_map.85), channel_id=1, source_target_pairs={{0,2},{1,7},{2,4},{3,1},{4,6},{5,3},{6,0},{7,5},{8,10},{9,15},{10,... | collective-permute-start | bytes 589832 | tf_op jit(solution)/shard_map/ppermute | solution.py:394
  97.1 9.1 %collective-permute-done.5.got_ref = f32[64,768]{1,0:T(8,128)S(1)} collective-permute-done((f32[64,768]{1,0:T(8,128)S(1)}, f32[64,768]{1,0:T(8,128)S(1)}, u32[]{:S(2)}, u32[]{:S(2)}) %collective-permute-start.5) | collective-permute-done | bytes 196640 | tf_op jit(solution)/shard_map/ppermute | solution.py:389
  106.3 1.9 %collective-permute-start.6 = (f32[64,768]{1,0:T(8,128)S(1)}, f32[64,768]{1,0:T(8,128)S(1)}, u32[]{:S(2)}, u32[]{:S(2)}) collective-permute-start(f32[64,768]{1,0:T(8,128)S(1)} %shard_map.86), channel_id=1, source_target_pairs={{0,2},{1,7},{2,4},{3,1},{4,6},{5,3},{6,0},{7,5},{8,10},{9,15},{10,... | collective-permute-start | bytes 589832 | tf_op jit(solution)/shard_map/ppermute | solution.py:396
  108.2 0.4 shard_map.83.one_ref
  108.6 1.2 collective-permute-done.4.top_ref
  109.8 8.1 %collective-permute-done.6.bottom_ref = f32[64,768]{1,0:T(8,128)S(1)} collective-permute-done((f32[64,768]{1,0:T(8,128)S(1)}, f32[64,768]{1,0:T(8,128)S(1)}, u32[]{:S(2)}, u32[]{:S(2)}) %collective-permute-start.6) | collective-permute-done | bytes 196640 | tf_op jit(solution)/shard_map/ppermute | solution.py:396
  117.9 0.7 shard_map.87
  (22 shorter events, 1.3 us)
Async XLA Ops:
  11.1 36.0 %all-to-all-start = ((f32[48,3,4,128]{3,2,1,0:T(4,128)}), f32[48,3,4,128]{3,2,1,0:T(4,128)S(1)}, u32[]{:S(2)}, u32[]{:S(2)}) async-start(f32[48,3,4,128]{3,2,1,0:T(4,128)} %bitcast.4), calls=%async_computation | async-start | bytes 589824 | tf_op jit(solution)/shard_map/all_to_all | solution.py:310
  33.4 40.1 %collective-permute-start.1 = (f32[4,512,768]{2,1,0:T(8,128)}, f32[4,512,768]{2,1,0:T(8,128)}, u32[]{:S(2)}, u32[]{:S(2)}) collective-permute-start(f32[4,512,768]{2,1,0:T(8,128)} %shard_map.78), channel_id=1, source_target_pairs={{0,1},{1,0},{2,3},{3,2},{4,5},{5,4},{6,7},{7,6},{8,9},{9,8},{10,11... | collective-permute-start | bytes 18874376 | tf_op jit(solution)/shard_map/ppermute | solution.py:358
  47.1 25.6 %copy-start = (bf16[128,512]{1,0:T(8,128)(2,1)S(1)}, bf16[128,512]{1,0:T(8,128)(2,1)}, u32[]{:S(2)}) copy-start(bf16[128,512]{1,0:T(8,128)(2,1)} %query_ref.3) | copy-start | bytes 393220
  47.1 25.6 %copy-start.1 = (bf16[128,512]{1,0:T(8,128)(2,1)S(1)}, bf16[128,512]{1,0:T(8,128)(2,1)}, u32[]{:S(2)}) copy-start(bf16[128,512]{1,0:T(8,128)(2,1)} %key_ref.1) | copy-start | bytes 393220
  47.1 25.6 %copy-start.2 = (bf16[128,512]{1,0:T(8,128)(2,1)S(1)}, bf16[128,512]{1,0:T(8,128)(2,1)}, u32[]{:S(2)}) copy-start(bf16[128,512]{1,0:T(8,128)(2,1)} %value_ref.1) | copy-start | bytes 393220
  47.1 25.6 %copy-start.3 = (f32[4,128]{1,0:T(4,128)S(1)}, f32[4,128]{1,0:T(4,128)}, u32[]{:S(2)}) copy-start(f32[4,128]{1,0:T(4,128)} %log_ref.1) | copy-start | bytes 6148
  47.1 25.6 %copy-start.5 = (s32[128]{0:T(128)S(1)}, s32[128]{0:T(128)}, u32[]{:S(2)}) copy-start(s32[128]{0:T(128)} %param.11) | copy-start | bytes 1540
  69.4 8.7 %collective-permute-start = (f32[512,128]{1,0:T(8,128)S(1)}, f32[512,128]{1,0:T(8,128)S(1)}, u32[]{:S(2)}, u32[]{:S(2)}) collective-permute-start(f32[512,128]{1,0:T(8,128)S(1)} %shard_map.76.own_ref), channel_id=1, source_target_pairs={{0,8},{8,0},{16,24},{24,16},{32,40},{40,32},{48,56},{56,48},{64,72... | collective-permute-start | bytes 786440 | tf_op jit(solution)/shard_map/ppermute | solution.py:363
  73.4 4.7 %copy-start.4 = (f32[512]{0:T(512)S(1)}, f32[512]{0:T(512)}, u32[]{:S(2)}) copy-start(f32[512]{0:T(512)} %param.12) | copy-start | bytes 6148
  81.0 13.7 %collective-permute-start.3 = (f32[64,768]{1,0:T(8,128)S(1)}, f32[64,768]{1,0:T(8,128)S(1)}, u32[]{:S(2)}, u32[]{:S(2)}) collective-permute-start(f32[64,768]{1,0:T(8,128)S(1)} %get-tuple-element.35), channel_id=1, source_target_pairs={{0,2},{1,7},{2,4},{3,1},{4,6},{5,3},{6,0},{7,5},{8,10},{9,15},{10,... | collective-permute-start | bytes 589832 | tf_op jit(solution)/shard_map/ppermute | solution.py:388
  84.1 24.1 %collective-permute-start.2 = (f32[128,768]{1,0:T(8,128)S(1)}, f32[128,768]{1,0:T(8,128)S(1)}, u32[]{:S(2)}, u32[]{:S(2)}) collective-permute-start(f32[128,768]{1,0:T(8,128)S(1)} %shard_map.82), channel_id=1, source_target_pairs={{0,6},{1,3},{2,0},{3,5},{4,2},{5,7},{6,4},{7,1},{8,14},{9,11},{10,... | collective-permute-start | bytes 1179656 | tf_op jit(solution)/shard_map/ppermute | solution.py:391
  89.4 16.8 %collective-permute-start.5 = (f32[64,768]{1,0:T(8,128)S(1)}, f32[64,768]{1,0:T(8,128)S(1)}, u32[]{:S(2)}, u32[]{:S(2)}) collective-permute-start(f32[64,768]{1,0:T(8,128)S(1)} %get-tuple-element.36), channel_id=1, source_target_pairs={{0,2},{1,7},{2,4},{3,1},{4,6},{5,3},{6,0},{7,5},{8,10},{9,15},{10,... | collective-permute-start | bytes 589832 | tf_op jit(solution)/shard_map/ppermute | solution.py:389
  94.7 15.0 %collective-permute-start.4 = (f32[64,768]{1,0:T(8,128)S(1)}, f32[64,768]{1,0:T(8,128)S(1)}, u32[]{:S(2)}, u32[]{:S(2)}) collective-permute-start(f32[64,768]{1,0:T(8,128)S(1)} %shard_map.85), channel_id=1, source_target_pairs={{0,2},{1,7},{2,4},{3,1},{4,6},{5,3},{6,0},{7,5},{8,10},{9,15},{10,... | collective-permute-start | bytes 589832 | tf_op jit(solution)/shard_map/ppermute | solution.py:394
  106.3 11.6 %collective-permute-start.6 = (f32[64,768]{1,0:T(8,128)S(1)}, f32[64,768]{1,0:T(8,128)S(1)}, u32[]{:S(2)}, u32[]{:S(2)}) collective-permute-start(f32[64,768]{1,0:T(8,128)S(1)} %shard_map.86), channel_id=1, source_target_pairs={{0,2},{1,7},{2,4},{3,1},{4,6},{5,3},{6,0},{7,5},{8,10},{9,15},{10,... | collective-permute-start | bytes 589832 | tf_op jit(solution)/shard_map/ppermute | solution.py:396

commit v11 on v8

--- a/solution.py
+++ b/solution.py
@@ -151,9 +151,8 @@
     def run(pairs):
         state = jnp.zeros((CHUNK, HEAD_DIM), F32)
         for pair in pairs:
-            rows = slice(pair * CHUNK, (pair + 1) * CHUNK)
-            out_ref[rows, :] = state
-            term = term_ref[rows, :]
+            out_ref[pair * ROWS : (pair + 1) * ROWS, :] = state[:ROWS]
+            term = term_ref[pair * CHUNK : (pair + 1) * CHUNK, :]
             state = term[ROWS:, :] * state + term
 
     @pl.when(side_ref[0] == 1)
@@ -165,12 +164,8 @@
         run(range(PAIRS - 1, -1, -1))
 
 
-def unpack_kernel(packed_ref, state_ref):
-    for piece in range(PAIRS):
-        head, place = divmod(piece, PIECES)
-        first = head * HEAD_DIM + ROWS * place
-        count = piece_rows(place)
-        state_ref[first : first + count, :] = packed_ref[piece * CHUNK : piece * CHUNK + count, :]
+def state_rows(head):
+    return slice(head * PIECES * ROWS, head * PIECES * ROWS + HEAD_DIM)
 
 
 def times_state(query, state):
@@ -198,7 +193,7 @@
         intra = jnp.dot(probs, value_ref[:, lanes], preferred_element_type=F32)
         last = STATE_ROWS + head
         got_decay = both_ref[1 - side, last : last + 1, :]
-        state = both_ref[1 - side, lanes, :] + got_decay * own_ref[lanes, :]
+        state = both_ref[1 - side, lanes, :] + got_decay * own_ref[state_rows(head), :]
         total_ref[:, lanes] = intra + own[:, head : head + 1] * times_state(query, state)
         factor_ref[:, lanes] = jnp.broadcast_to(other[:, head : head + 1], (EVENTS, HEAD_DIM))
 
@@ -233,7 +228,7 @@
     for head in range(HEADS_DEV):
         lanes = slice(head * HEAD_DIM, (head + 1) * HEAD_DIM)
         total = total_ref[:, lanes] + factor_ref[:, lanes] * times_state(
-            query_ref[:, lanes], other_ref[lanes, :]
+            query_ref[:, lanes], other_ref[state_rows(head), :]
         )
         average = jnp.mean(total * total, axis=1, keepdims=True)
         scaled = total * lax.rsqrt(average + 1e-06) * gain_ref[:, lanes]
@@ -278,10 +273,10 @@
     out_ref[...] = (one_ref[...] + two_ref[...]).astype(BF16)
 
 
-def exchange_pieces(packed):
-    pieces = packed.reshape(PAIRS, 3, 4, HEAD_DIM)
+def exchange_pieces(packed, shape):
+    pieces = packed.reshape((PAIRS,) + shape + (HEAD_DIM,))
     pieces = lax.all_to_all(pieces, "ctx", 0, 0, axis_index_groups=SIDE_GROUPS)
-    return pieces.reshape(PACKED, HEAD_DIM)
+    return pieces.reshape(packed.shape)
 
 
 def body(queries, keys, values, state_retention_log, boundary, gain, w_out):
@@ -313,9 +308,10 @@
     (pair_terms,) = call(
         combine_kernel, [packed], (side, kept, both, decay), scalars=1, flops=200_000, moved=1_100_000
     )
-    slices = exchange_pieces(pair_terms)
-    (states,) = call(scan_kernel, [packed], (side, slices), scalars=1, flops=200_000, moved=600_000)
-    (own,) = call(unpack_kernel, [state], (exchange_pieces(states),), moved=600_000)
+    slices = exchange_pieces(pair_terms, (3, 4))
+    returned = ((PAIRS * ROWS, HEAD_DIM), F32)
+    (states,) = call(scan_kernel, [returned], (side, slices), scalars=1, flops=200_000, moved=600_000)
+    own = exchange_pieces(states, (ROWS, 1))
     own, w_late = lax.optimization_barrier((own, w_out))
     other = lax.ppermute(own, "ctx", SIDE_SWAP)
     (staged,) = call(

time: 116 us -> 115 us (level)
    pallas_call x14 -> x13, Pallas kernels: 7.79 us -> 7.76 us  [call(): pl.pallas_call(kernel, out_shape=shapes, in_specs=specs, out_specs=[pl.Bl...]
where the time goes in v11:
time: 115 us
  blocking collectives  75.5 us (66%)
  starting transfers between devices  17.9 us (16%)
  waiting for transfers between devices  13.7 us (12%)
  Pallas kernels  7.76 us (7%)
    all_to_all x2, blocking collectives, exchange_pieces(): pieces = lax.all_to_all(pieces, 'ctx', 0, 0, axis_index_groups=SIDE_GROUPS)  57.3 us
    all_gather x1, blocking collectives, body(): both = lax.all_gather(sent, 'ctx', axis_index_groups=SIDE_PAIRS)  8.81 us
    pallas_call x13, Pallas kernels, call(): pl.pallas_call(kernel, out_shape=shapes, in_specs=specs, out_specs=[pl.Bl...  7.76 us
    ppermute x1, waiting for transfers between devices, body(): ahead_got = lax.ppermute(opposite, 'tp', ONWARD)  6.89 us
    ppermute x1, starting transfers between devices, body(): two = lax.ppermute(passed, 'tp', ONWARD)  6.5 us
    ppermute x1, waiting for transfers between devices, body(): two = lax.ppermute(passed, 'tp', ONWARD)  5.77 us
    ppermute x1, starting transfers between devices, body(): ahead_got = lax.ppermute(opposite, 'tp', ONWARD)  5.72 us
    ppermute x1, starting transfers between devices, body(): other = lax.ppermute(own, 'ctx', SIDE_SWAP)  3.49 us
  transfers between devices with their start and end apart: 4, of which 3 were waited for; matrix products, arithmetic and copies ran while one was open for 0% of the time, Pallas kernels for 4%

profile of v11, /device:TPU:16, one launch (start us, length us, event | category | flops | bytes accessed | tf_op | source)
XLA Modules:
  0.0 115.1 jit_solution(17895374140106626391)
XLA Ops:
  0.0 1.5 %shard_map.73 = (f32[520,128]{1,0:T(8,128)S(1)}, f32[512,128]{1,0:T(8,128)S(1)}, f32[4,128]{1,0:T(4,128)S(1)}) custom-call(s32[1]{0:T(128)} %bitcast.1.side_ref, bf16[128,512]{1,0:T(8,128)(2,1)} %key_ref.1, bf16[128,512]{1,0:T(8,128)(2,1)} %value_ref.1, f32[4,128]{1,0:T(4,128)} %log_ref.1, s32[1,128]{1,0:T(1,128)} %bitcast.25), custom_call_target="tpu_custom_call" | custom-call | flops 70000000 | bytes 900000 | tf_op jit(solution)/shard_map/pallas_call | solution.py:48
  1.5 8.8 %all-gather = f32[1040,128]{1,0:T(8,128)S(1)} all-gather(f32[520,128]{1,0:T(8,128)S(1)} %get-tuple-element.27), channel_id=2, replica_groups={{0,8},{16,24},{32,40},{48,56},{64,72},{80,88},{96,104},{112,120},{128,1..., dimensions={0}, use_global_device_ids=true | all-gather | bytes 798720 | tf_op jit(solution)/shard_map/all_gather | solution.py:307
  10.4 35.8 %all_to_all.10 = f32[48,3,4,128]{3,2,1,0:T(4,128)S(1)} all-to-all(f32[48,3,4,128]{3,2,1,0:T(4,128)S(1)} %bitcast.20), channel_id=1, replica_groups={{0,16,32,48,64,80,96,112,128,144,160,176,192,208,224,240,256,272,288,30..., dimensions={0} | all-to-all | bytes 589824 | tf_op jit(solution)/shard_map/all_to_all | solution.py:278
  46.2 0.1 shard_map.75
  46.3 21.4 %all_to_all.11 = f32[48,11,1,128]{3,2,1,0:T(1,128)S(1)} all-to-all(f32[48,11,1,128]{3,2,1,0:T(1,128)S(1)} %bitcast.21), channel_id=1, replica_groups={{0,16,32,48,64,80,96,112,128,144,160,176,192,208,224,240,256,272,288,30..., dimensions={0} | all-to-all | bytes 540672 | tf_op jit(solution)/shard_map/all_to_all | solution.py:278
  67.7 3.5 %collective-permute-start = (f32[528,128]{1,0:T(8,128)S(1)}, f32[528,128]{1,0:T(8,128)S(1)}, u32[]{:S(2)}, u32[]{:S(2)}) collective-permute-start(f32[528,128]{1,0:T(8,128)S(1)} %bitcast.22), channel_id=1, source_target_pairs={{0,8},{8,0},{16,24},{24,16},{32,40},{40,32},{48,56},{56,48},{64,72... | collective-permute-start | bytes 811016 | tf_op jit(solution)/shard_map/ppermute | solution.py:316
  71.3 3.0 %shard_map.77.w_ref = bf16[8,512,768]{2,1,0:T(8,128)(2,1)S(1)} custom-call(bf16[512,6144]{1,0:T(8,128)(2,1)} %w_hbm), custom_call_target="tpu_custom_call" | custom-call | bytes 12600000 | tf_op jit(solution)/shard_map/pallas_call | solution.py:48
  74.3 0.7 shard_map.76
  75.0 1.0 collective-permute-done.other_ref
  76.1 0.6 shard_map.78
  76.7 2.4 %all-gather.1 = f32[256,768]{1,0:T(8,128)S(1)} all-gather(f32[128,768]{1,0:T(8,128)S(1)} %get-tuple-element.37), channel_id=3, replica_groups={{0,1},{2,3},{4,5},{6,7},{8,9},{10,11},{12,13},{14,15},{16,17},{18,19},{..., dimensions={0}, use_global_device_ids=true | all-gather | bytes 1179648 | tf_op jit(solution)/shard_map/all_gather | solution.py:350
  79.1 5.7 %collective-permute-start.2 = (f32[128,768]{1,0:T(8,128)S(1)}, f32[128,768]{1,0:T(8,128)S(1)}, u32[]{:S(2)}, u32[]{:S(2)}) collective-permute-start(f32[128,768]{1,0:T(8,128)S(1)} %shard_map.79), channel_id=1, source_target_pairs={{0,2},{1,7},{2,4},{3,1},{4,6},{5,3},{6,0},{7,5},{8,10},{9,15},{10,... | collective-permute-start | bytes 1179656 | tf_op jit(solution)/shard_map/ppermute | solution.py:353
  84.8 0.4 shard_map.80
  85.2 2.4 %all-gather.2 = f32[256,768]{1,0:T(8,128)S(1)} all-gather(f32[128,768]{1,0:T(8,128)S(1)} %get-tuple-element.40), channel_id=4, replica_groups={{0,1},{2,3},{4,5},{6,7},{8,9},{10,11},{12,13},{14,15},{16,17},{18,19},{..., dimensions={0}, use_global_device_ids=true | all-gather | bytes 1179648 | tf_op jit(solution)/shard_map/all_gather | solution.py:357
  87.6 2.2 %collective-permute-start.1 = (f32[128,768]{1,0:T(8,128)S(1)}, f32[128,768]{1,0:T(8,128)S(1)}, u32[]{:S(2)}, u32[]{:S(2)}) collective-permute-start(f32[128,768]{1,0:T(8,128)S(1)} %shard_map.82), channel_id=1, source_target_pairs={{0,6},{1,3},{2,0},{3,5},{4,2},{5,7},{6,4},{7,1},{8,14},{9,11},{10,... | collective-permute-start | bytes 1179656 | tf_op jit(solution)/shard_map/ppermute | solution.py:360
  89.8 0.6 shard_map.81
  90.4 2.4 %all-gather.4 = f32[256,768]{1,0:T(8,128)S(1)} all-gather(f32[128,768]{1,0:T(8,128)S(1)} %get-tuple-element.47), channel_id=6, replica_groups={{0,1},{2,3},{4,5},{6,7},{8,9},{10,11},{12,13},{14,15},{16,17},{18,19},{..., dimensions={0}, use_global_device_ids=true | all-gather | bytes 1179648 | tf_op jit(solution)/shard_map/all_gather | solution.py:364
  92.8 6.9 %collective-permute-done.2.more_ref = f32[128,768]{1,0:T(8,128)S(1)} collective-permute-done((f32[128,768]{1,0:T(8,128)S(1)}, f32[128,768]{1,0:T(8,128)S(1)}, u32[]{:S(2)}, u32[]{:S(2)}) %collective-permute-start.2) | collective-permute-done | bytes 393248 | tf_op jit(solution)/shard_map/ppermute | solution.py:353
  99.6 0.1 shard_map.84
  99.7 6.5 %collective-permute-start.3 = (f32[128,768]{1,0:T(8,128)S(1)}, f32[128,768]{1,0:T(8,128)S(1)}, u32[]{:S(2)}, u32[]{:S(2)}) collective-permute-start(f32[128,768]{1,0:T(8,128)S(1)} %shard_map.84), channel_id=1, source_target_pairs={{0,2},{1,7},{2,4},{3,1},{4,6},{5,3},{6,0},{7,5},{8,10},{9,15},{10,... | collective-permute-start | bytes 1179656 | tf_op jit(solution)/shard_map/ppermute | solution.py:367
  106.2 2.4 %all-gather.3 = f32[256,768]{1,0:T(8,128)S(1)} all-gather(f32[128,768]{1,0:T(8,128)S(1)} %get-tuple-element.43), channel_id=5, replica_groups={{0,1},{2,3},{4,5},{6,7},{8,9},{10,11},{12,13},{14,15},{16,17},{18,19},{..., dimensions={0}, use_global_device_ids=true | all-gather | bytes 1179648 | tf_op jit(solution)/shard_map/all_gather | solution.py:365
  108.6 0.1 shard_map.83.one_ref
  108.6 5.8 %collective-permute-done.3.two_ref = f32[128,768]{1,0:T(8,128)S(1)} collective-permute-done((f32[128,768]{1,0:T(8,128)S(1)}, f32[128,768]{1,0:T(8,128)S(1)}, u32[]{:S(2)}, u32[]{:S(2)}) %collective-permute-start.3) | collective-permute-done | bytes 393248 | tf_op jit(solution)/shard_map/ppermute | solution.py:367
  114.4 0.7 shard_map.85
  (16 shorter events, 0.2 us)
Async XLA Ops:
  67.7 8.3 %collective-permute-start = (f32[528,128]{1,0:T(8,128)S(1)}, f32[528,128]{1,0:T(8,128)S(1)}, u32[]{:S(2)}, u32[]{:S(2)}) collective-permute-start(f32[528,128]{1,0:T(8,128)S(1)} %bitcast.22), channel_id=1, source_target_pairs={{0,8},{8,0},{16,24},{24,16},{32,40},{40,32},{48,56},{56,48},{64,72... | collective-permute-start | bytes 811016 | tf_op jit(solution)/shard_map/ppermute | solution.py:316
  71.2 3.1 %copy-start = (bf16[128,512]{1,0:T(8,128)(2,1)S(1)}, bf16[128,512]{1,0:T(8,128)(2,1)}, u32[]{:S(2)}) copy-start(bf16[128,512]{1,0:T(8,128)(2,1)} %query_ref.3) | copy-start | bytes 393220
  71.2 3.1 %copy-start.1 = (bf16[128,512]{1,0:T(8,128)(2,1)S(1)}, bf16[128,512]{1,0:T(8,128)(2,1)}, u32[]{:S(2)}) copy-start(bf16[128,512]{1,0:T(8,128)(2,1)} %key_ref.1) | copy-start | bytes 393220
  71.2 3.1 %copy-start.2 = (bf16[128,512]{1,0:T(8,128)(2,1)S(1)}, bf16[128,512]{1,0:T(8,128)(2,1)}, u32[]{:S(2)}) copy-start(bf16[128,512]{1,0:T(8,128)(2,1)} %value_ref.1) | copy-start | bytes 393220
  71.2 3.1 %copy-start.3 = (f32[4,128]{1,0:T(4,128)S(1)}, f32[4,128]{1,0:T(4,128)}, u32[]{:S(2)}) copy-start(f32[4,128]{1,0:T(4,128)} %log_ref.1) | copy-start | bytes 6148
  71.3 3.1 %copy-start.5 = (s32[128]{0:T(128)S(1)}, s32[128]{0:T(128)}, u32[]{:S(2)}) copy-start(s32[128]{0:T(128)} %param.11) | copy-start | bytes 1540
  71.3 4.8 %copy-start.4 = (f32[512]{0:T(512)S(1)}, f32[512]{0:T(512)}, u32[]{:S(2)}) copy-start(f32[512]{0:T(512)} %param.12) | copy-start | bytes 6148
  79.1 20.6 %collective-permute-start.2 = (f32[128,768]{1,0:T(8,128)S(1)}, f32[128,768]{1,0:T(8,128)S(1)}, u32[]{:S(2)}, u32[]{:S(2)}) collective-permute-start(f32[128,768]{1,0:T(8,128)S(1)} %shard_map.79), channel_id=1, source_target_pairs={{0,2},{1,7},{2,4},{3,1},{4,6},{5,3},{6,0},{7,5},{8,10},{9,15},{10,... | collective-permute-start | bytes 1179656 | tf_op jit(solution)/shard_map/ppermute | solution.py:353
  87.6 21.0 %collective-permute-start.1 = (f32[128,768]{1,0:T(8,128)S(1)}, f32[128,768]{1,0:T(8,128)S(1)}, u32[]{:S(2)}, u32[]{:S(2)}) collective-permute-start(f32[128,768]{1,0:T(8,128)S(1)} %shard_map.82), channel_id=1, source_target_pairs={{0,6},{1,3},{2,0},{3,5},{4,2},{5,7},{6,4},{7,1},{8,14},{9,11},{10,... | collective-permute-start | bytes 1179656 | tf_op jit(solution)/shard_map/ppermute | solution.py:360
  99.7 14.7 %collective-permute-start.3 = (f32[128,768]{1,0:T(8,128)S(1)}, f32[128,768]{1,0:T(8,128)S(1)}, u32[]{:S(2)}, u32[]{:S(2)}) collective-permute-start(f32[128,768]{1,0:T(8,128)S(1)} %shard_map.84), channel_id=1, source_target_pairs={{0,2},{1,7},{2,4},{3,1},{4,6},{5,3},{6,0},{7,5},{8,10},{9,15},{10,... | collective-permute-start | bytes 1179656 | tf_op jit(solution)/shard_map/ppermute | solution.py:367

commit v12 on v11

--- a/solution.py
+++ b/solution.py
@@ -26,7 +26,8 @@
 BF16 = jnp.bfloat16
 VMEM_LIMIT = 24 * 1024 * 1024
 
-SIDE_GROUPS = [[2 * pair + side for pair in range(PAIRS)] for side in range(2)]
+SLOTS = [4 * z + x for x in range(4) for z in range(PAIRS // 4)]
+SIDE_GROUPS = [[2 * SLOTS.index(slot) + side for slot in range(PAIRS)] for side in range(2)]
 SIDE_SWAP = [(i, i ^ 1) for i in range(2 * PAIRS)]
 SIDE_PAIRS = [[i, i + 1] for i in range(0, 2 * PAIRS, 2)]
 CORE_SWAP = [(i, i ^ 1) for i in range(8)]
@@ -151,8 +152,9 @@
     def run(pairs):
         state = jnp.zeros((CHUNK, HEAD_DIM), F32)
         for pair in pairs:
-            out_ref[pair * ROWS : (pair + 1) * ROWS, :] = state[:ROWS]
-            term = term_ref[pair * CHUNK : (pair + 1) * CHUNK, :]
+            slot = SLOTS[pair]
+            out_ref[slot * ROWS : (slot + 1) * ROWS, :] = state[:ROWS]
+            term = term_ref[slot * CHUNK : (slot + 1) * CHUNK, :]
             state = term[ROWS:, :] * state + term
 
     @pl.when(side_ref[0] == 1)

time: 115 us -> 116 us (level)
  no operation moved by 1% of the time
where the time goes in v12:
time: 116 us; the launch traced here: 115 us
  blocking collectives  75.8 us (65%)
  starting transfers between devices  17.9 us (15%)
  waiting for transfers between devices  13.7 us (12%)
  Pallas kernels  7.76 us (7%)
    all_to_all x2, blocking collectives, exchange_pieces(): pieces = lax.all_to_all(pieces, 'ctx', 0, 0, axis_index_groups=SIDE_GROUPS)  57.5 us
    all_gather x1, blocking collectives, body(): both = lax.all_gather(sent, 'ctx', axis_index_groups=SIDE_PAIRS)  8.81 us
    pallas_call x13, Pallas kernels, call(): pl.pallas_call(kernel, out_shape=shapes, in_specs=specs, out_specs=[pl.Bl...  7.76 us
    ppermute x1, waiting for transfers between devices, body(): ahead_got = lax.ppermute(opposite, 'tp', ONWARD)  6.89 us
    ppermute x1, starting transfers between devices, body(): two = lax.ppermute(passed, 'tp', ONWARD)  6.5 us
    ppermute x1, waiting for transfers between devices, body(): two = lax.ppermute(passed, 'tp', ONWARD)  5.76 us
    ppermute x1, starting transfers between devices, body(): ahead_got = lax.ppermute(opposite, 'tp', ONWARD)  5.71 us
    ppermute x1, starting transfers between devices, body(): other = lax.ppermute(own, 'ctx', SIDE_SWAP)  3.49 us
  transfers between devices with their start and end apart: 4, of which 3 were waited for; matrix products, arithmetic and copies ran while one was open for 0% of the time, Pallas kernels for 4%

profile of v12, /device:TPU:16, one launch (start us, length us, event | category | flops | bytes accessed | tf_op | source)
XLA Modules:
  0.0 115.4 jit_solution(10445719682327016908)
XLA Ops:
  0.0 1.5 %shard_map.73 = (f32[520,128]{1,0:T(8,128)S(1)}, f32[512,128]{1,0:T(8,128)S(1)}, f32[4,128]{1,0:T(4,128)S(1)}) custom-call(s32[1]{0:T(128)} %bitcast.1.side_ref, bf16[128,512]{1,0:T(8,128)(2,1)} %key_ref.1, bf16[128,512]{1,0:T(8,128)(2,1)} %value_ref.1, f32[4,128]{1,0:T(4,128)} %log_ref.1, s32[1,128]{1,0:T(1,128)} %bitcast.25), custom_call_target="tpu_custom_call" | custom-call | flops 70000000 | bytes 900000 | tf_op jit(solution)/shard_map/pallas_call | solution.py:49
  1.5 8.8 %all-gather = f32[1040,128]{1,0:T(8,128)S(1)} all-gather(f32[520,128]{1,0:T(8,128)S(1)} %get-tuple-element.27), channel_id=2, replica_groups={{0,8},{16,24},{32,40},{48,56},{64,72},{80,88},{96,104},{112,120},{128,1..., dimensions={0}, use_global_device_ids=true | all-gather | bytes 798720 | tf_op jit(solution)/shard_map/all_gather | solution.py:309
  10.4 35.9 %all_to_all.10 = f32[48,3,4,128]{3,2,1,0:T(4,128)S(1)} all-to-all(f32[48,3,4,128]{3,2,1,0:T(4,128)S(1)} %bitcast.20), channel_id=1, replica_groups={{0,192,384,576,16,208,400,592,32,224,416,608,48,240,432,624,64,256,448,..., dimensions={0} | all-to-all | bytes 589824 | tf_op jit(solution)/shard_map/all_to_all | solution.py:280
  46.2 0.1 shard_map.75
  46.3 21.6 %all_to_all.11 = f32[48,11,1,128]{3,2,1,0:T(1,128)S(1)} all-to-all(f32[48,11,1,128]{3,2,1,0:T(1,128)S(1)} %bitcast.21), channel_id=1, replica_groups={{0,192,384,576,16,208,400,592,32,224,416,608,48,240,432,624,64,256,448,..., dimensions={0} | all-to-all | bytes 540672 | tf_op jit(solution)/shard_map/all_to_all | solution.py:280
  68.0 3.5 %collective-permute-start = (f32[528,128]{1,0:T(8,128)S(1)}, f32[528,128]{1,0:T(8,128)S(1)}, u32[]{:S(2)}, u32[]{:S(2)}) collective-permute-start(f32[528,128]{1,0:T(8,128)S(1)} %bitcast.22), channel_id=1, source_target_pairs={{0,8},{8,0},{16,24},{24,16},{32,40},{40,32},{48,56},{56,48},{64,72... | collective-permute-start | bytes 811016 | tf_op jit(solution)/shard_map/ppermute | solution.py:318
  71.5 3.0 %shard_map.77.w_ref = bf16[8,512,768]{2,1,0:T(8,128)(2,1)S(1)} custom-call(bf16[512,6144]{1,0:T(8,128)(2,1)} %w_hbm), custom_call_target="tpu_custom_call" | custom-call | bytes 12600000 | tf_op jit(solution)/shard_map/pallas_call | solution.py:49
  74.6 0.7 shard_map.76
  75.3 1.1 collective-permute-done.other_ref
  76.3 0.6 shard_map.78
  76.9 2.4 %all-gather.1 = f32[256,768]{1,0:T(8,128)S(1)} all-gather(f32[128,768]{1,0:T(8,128)S(1)} %get-tuple-element.37), channel_id=3, replica_groups={{0,1},{2,3},{4,5},{6,7},{8,9},{10,11},{12,13},{14,15},{16,17},{18,19},{..., dimensions={0}, use_global_device_ids=true | all-gather | bytes 1179648 | tf_op jit(solution)/shard_map/all_gather | solution.py:352
  79.3 5.7 %collective-permute-start.2 = (f32[128,768]{1,0:T(8,128)S(1)}, f32[128,768]{1,0:T(8,128)S(1)}, u32[]{:S(2)}, u32[]{:S(2)}) collective-permute-start(f32[128,768]{1,0:T(8,128)S(1)} %shard_map.79), channel_id=1, source_target_pairs={{0,2},{1,7},{2,4},{3,1},{4,6},{5,3},{6,0},{7,5},{8,10},{9,15},{10,... | collective-permute-start | bytes 1179656 | tf_op jit(solution)/shard_map/ppermute | solution.py:355
  85.1 0.4 shard_map.80
  85.4 2.4 %all-gather.2 = f32[256,768]{1,0:T(8,128)S(1)} all-gather(f32[128,768]{1,0:T(8,128)S(1)} %get-tuple-element.40), channel_id=4, replica_groups={{0,1},{2,3},{4,5},{6,7},{8,9},{10,11},{12,13},{14,15},{16,17},{18,19},{..., dimensions={0}, use_global_device_ids=true | all-gather | bytes 1179648 | tf_op jit(solution)/shard_map/all_gather | solution.py:359
  87.9 2.2 %collective-permute-start.1 = (f32[128,768]{1,0:T(8,128)S(1)}, f32[128,768]{1,0:T(8,128)S(1)}, u32[]{:S(2)}, u32[]{:S(2)}) collective-permute-start(f32[128,768]{1,0:T(8,128)S(1)} %shard_map.82), channel_id=1, source_target_pairs={{0,6},{1,3},{2,0},{3,5},{4,2},{5,7},{6,4},{7,1},{8,14},{9,11},{10,... | collective-permute-start | bytes 1179656 | tf_op jit(solution)/shard_map/ppermute | solution.py:362
  90.0 0.6 shard_map.81
  90.6 2.4 %all-gather.4 = f32[256,768]{1,0:T(8,128)S(1)} all-gather(f32[128,768]{1,0:T(8,128)S(1)} %get-tuple-element.47), channel_id=6, replica_groups={{0,1},{2,3},{4,5},{6,7},{8,9},{10,11},{12,13},{14,15},{16,17},{18,19},{..., dimensions={0}, use_global_device_ids=true | all-gather | bytes 1179648 | tf_op jit(solution)/shard_map/all_gather | solution.py:366
  93.0 6.9 %collective-permute-done.2.more_ref = f32[128,768]{1,0:T(8,128)S(1)} collective-permute-done((f32[128,768]{1,0:T(8,128)S(1)}, f32[128,768]{1,0:T(8,128)S(1)}, u32[]{:S(2)}, u32[]{:S(2)}) %collective-permute-start.2) | collective-permute-done | bytes 393248 | tf_op jit(solution)/shard_map/ppermute | solution.py:355
  99.9 0.1 shard_map.84
  100.0 6.5 %collective-permute-start.3 = (f32[128,768]{1,0:T(8,128)S(1)}, f32[128,768]{1,0:T(8,128)S(1)}, u32[]{:S(2)}, u32[]{:S(2)}) collective-permute-start(f32[128,768]{1,0:T(8,128)S(1)} %shard_map.84), channel_id=1, source_target_pairs={{0,2},{1,7},{2,4},{3,1},{4,6},{5,3},{6,0},{7,5},{8,10},{9,15},{10,... | collective-permute-start | bytes 1179656 | tf_op jit(solution)/shard_map/ppermute | solution.py:369
  106.5 2.4 %all-gather.3 = f32[256,768]{1,0:T(8,128)S(1)} all-gather(f32[128,768]{1,0:T(8,128)S(1)} %get-tuple-element.43), channel_id=5, replica_groups={{0,1},{2,3},{4,5},{6,7},{8,9},{10,11},{12,13},{14,15},{16,17},{18,19},{..., dimensions={0}, use_global_device_ids=true | all-gather | bytes 1179648 | tf_op jit(solution)/shard_map/all_gather | solution.py:367
  108.8 0.1 shard_map.83.one_ref
  108.9 5.8 %collective-permute-done.3.two_ref = f32[128,768]{1,0:T(8,128)S(1)} collective-permute-done((f32[128,768]{1,0:T(8,128)S(1)}, f32[128,768]{1,0:T(8,128)S(1)}, u32[]{:S(2)}, u32[]{:S(2)}) %collective-permute-start.3) | collective-permute-done | bytes 393248 | tf_op jit(solution)/shard_map/ppermute | solution.py:369
  114.7 0.7 shard_map.85
  (16 shorter events, 0.2 us)
Async XLA Ops:
  68.0 8.3 %collective-permute-start = (f32[528,128]{1,0:T(8,128)S(1)}, f32[528,128]{1,0:T(8,128)S(1)}, u32[]{:S(2)}, u32[]{:S(2)}) collective-permute-start(f32[528,128]{1,0:T(8,128)S(1)} %bitcast.22), channel_id=1, source_target_pairs={{0,8},{8,0},{16,24},{24,16},{32,40},{40,32},{48,56},{56,48},{64,72... | collective-permute-start | bytes 811016 | tf_op jit(solution)/shard_map/ppermute | solution.py:318
  71.5 3.1 %copy-start = (bf16[128,512]{1,0:T(8,128)(2,1)S(1)}, bf16[128,512]{1,0:T(8,128)(2,1)}, u32[]{:S(2)}) copy-start(bf16[128,512]{1,0:T(8,128)(2,1)} %query_ref.3) | copy-start | bytes 393220
  71.5 3.1 %copy-start.1 = (bf16[128,512]{1,0:T(8,128)(2,1)S(1)}, bf16[128,512]{1,0:T(8,128)(2,1)}, u32[]{:S(2)}) copy-start(bf16[128,512]{1,0:T(8,128)(2,1)} %key_ref.1) | copy-start | bytes 393220
  71.5 3.1 %copy-start.2 = (bf16[128,512]{1,0:T(8,128)(2,1)S(1)}, bf16[128,512]{1,0:T(8,128)(2,1)}, u32[]{:S(2)}) copy-start(bf16[128,512]{1,0:T(8,128)(2,1)} %value_ref.1) | copy-start | bytes 393220
  71.5 3.1 %copy-start.3 = (f32[4,128]{1,0:T(4,128)S(1)}, f32[4,128]{1,0:T(4,128)}, u32[]{:S(2)}) copy-start(f32[4,128]{1,0:T(4,128)} %log_ref.1) | copy-start | bytes 6148
  71.5 3.1 %copy-start.5 = (s32[128]{0:T(128)S(1)}, s32[128]{0:T(128)}, u32[]{:S(2)}) copy-start(s32[128]{0:T(128)} %param.11) | copy-start | bytes 1540
  71.5 4.8 %copy-start.4 = (f32[512]{0:T(512)S(1)}, f32[512]{0:T(512)}, u32[]{:S(2)}) copy-start(f32[512]{0:T(512)} %param.12) | copy-start | bytes 6148
  79.3 20.6 %collective-permute-start.2 = (f32[128,768]{1,0:T(8,128)S(1)}, f32[128,768]{1,0:T(8,128)S(1)}, u32[]{:S(2)}, u32[]{:S(2)}) collective-permute-start(f32[128,768]{1,0:T(8,128)S(1)} %shard_map.79), channel_id=1, source_target_pairs={{0,2},{1,7},{2,4},{3,1},{4,6},{5,3},{6,0},{7,5},{8,10},{9,15},{10,... | collective-permute-start | bytes 1179656 | tf_op jit(solution)/shard_map/ppermute | solution.py:355
  87.9 21.0 %collective-permute-start.1 = (f32[128,768]{1,0:T(8,128)S(1)}, f32[128,768]{1,0:T(8,128)S(1)}, u32[]{:S(2)}, u32[]{:S(2)}) collective-permute-start(f32[128,768]{1,0:T(8,128)S(1)} %shard_map.82), channel_id=1, source_target_pairs={{0,6},{1,3},{2,0},{3,5},{4,2},{5,7},{6,4},{7,1},{8,14},{9,11},{10,... | collective-permute-start | bytes 1179656 | tf_op jit(solution)/shard_map/ppermute | solution.py:362
  100.0 14.7 %collective-permute-start.3 = (f32[128,768]{1,0:T(8,128)S(1)}, f32[128,768]{1,0:T(8,128)S(1)}, u32[]{:S(2)}, u32[]{:S(2)}) collective-permute-start(f32[128,768]{1,0:T(8,128)S(1)} %shard_map.84), channel_id=1, source_target_pairs={{0,2},{1,7},{2,4},{3,1},{4,6},{5,3},{6,0},{7,5},{8,10},{9,15},{10,... | collective-permute-start | bytes 1179656 | tf_op jit(solution)/shard_map/ppermute | solution.py:369

commit v13 on v12

--- a/solution.py
+++ b/solution.py
@@ -310,7 +310,7 @@
     (pair_terms,) = call(
         combine_kernel, [packed], (side, kept, both, decay), scalars=1, flops=200_000, moved=1_100_000
     )
-    slices = exchange_pieces(pair_terms, (3, 4))
+    slices = exchange_pieces(pair_terms, (CHUNK, 1))
     returned = ((PAIRS * ROWS, HEAD_DIM), F32)
     (states,) = call(scan_kernel, [returned], (side, slices), scalars=1, flops=200_000, moved=600_000)
     own = exchange_pieces(states, (ROWS, 1))

time: 116 us -> 116 us (level)
  no operation moved by 1% of the time
where the time goes in v13:
time: 116 us; the launch traced here: 115 us
  blocking collectives  75.8 us (65%)
  starting transfers between devices  17.9 us (15%)
  waiting for transfers between devices  13.7 us (12%)
  Pallas kernels  7.76 us (7%)
    all_to_all x2, blocking collectives, exchange_pieces(): pieces = lax.all_to_all(pieces, 'ctx', 0, 0, axis_index_groups=SIDE_GROUPS)  57.5 us
    all_gather x1, blocking collectives, body(): both = lax.all_gather(sent, 'ctx', axis_index_groups=SIDE_PAIRS)  8.81 us
    pallas_call x13, Pallas kernels, call(): pl.pallas_call(kernel, out_shape=shapes, in_specs=specs, out_specs=[pl.Bl...  7.76 us
    ppermute x1, waiting for transfers between devices, body(): ahead_got = lax.ppermute(opposite, 'tp', ONWARD)  6.89 us
    ppermute x1, starting transfers between devices, body(): two = lax.ppermute(passed, 'tp', ONWARD)  6.5 us
    ppermute x1, waiting for transfers between devices, body(): two = lax.ppermute(passed, 'tp', ONWARD)  5.76 us
    ppermute x1, starting transfers between devices, body(): ahead_got = lax.ppermute(opposite, 'tp', ONWARD)  5.71 us
    ppermute x1, starting transfers between devices, body(): other = lax.ppermute(own, 'ctx', SIDE_SWAP)  3.49 us
  transfers between devices with their start and end apart: 4, of which 3 were waited for; matrix products, arithmetic and copies ran while one was open for 0% of the time, Pallas kernels for 4%

profile of v13, /device:TPU:16, one launch (start us, length us, event | category | flops | bytes accessed | tf_op | source)
XLA Modules:
  0.0 115.4 jit_solution(10445719682327016908)
XLA Ops:
  0.0 1.5 %shard_map.73 = (f32[520,128]{1,0:T(8,128)S(1)}, f32[512,128]{1,0:T(8,128)S(1)}, f32[4,128]{1,0:T(4,128)S(1)}) custom-call(s32[1]{0:T(128)} %bitcast.1.side_ref, bf16[128,512]{1,0:T(8,128)(2,1)} %key_ref.1, bf16[128,512]{1,0:T(8,128)(2,1)} %value_ref.1, f32[4,128]{1,0:T(4,128)} %log_ref.1, s32[1,128]{1,0:T(1,128)} %bitcast.25), custom_call_target="tpu_custom_call" | custom-call | flops 70000000 | bytes 900000 | tf_op jit(solution)/shard_map/pallas_call | solution.py:49
  1.5 8.8 %all-gather = f32[1040,128]{1,0:T(8,128)S(1)} all-gather(f32[520,128]{1,0:T(8,128)S(1)} %get-tuple-element.27), channel_id=2, replica_groups={{0,8},{16,24},{32,40},{48,56},{64,72},{80,88},{96,104},{112,120},{128,1..., dimensions={0}, use_global_device_ids=true | all-gather | bytes 798720 | tf_op jit(solution)/shard_map/all_gather | solution.py:309
  10.4 35.9 %all_to_all.10 = f32[48,12,1,128]{3,2,1,0:T(1,128)S(1)} all-to-all(f32[48,12,1,128]{3,2,1,0:T(1,128)S(1)} %bitcast.20), channel_id=1, replica_groups={{0,192,384,576,16,208,400,592,32,224,416,608,48,240,432,624,64,256,448,..., dimensions={0} | all-to-all | bytes 589824 | tf_op jit(solution)/shard_map/all_to_all | solution.py:280
  46.2 0.1 shard_map.75
  46.3 21.6 %all_to_all.11 = f32[48,11,1,128]{3,2,1,0:T(1,128)S(1)} all-to-all(f32[48,11,1,128]{3,2,1,0:T(1,128)S(1)} %bitcast.21), channel_id=1, replica_groups={{0,192,384,576,16,208,400,592,32,224,416,608,48,240,432,624,64,256,448,..., dimensions={0} | all-to-all | bytes 540672 | tf_op jit(solution)/shard_map/all_to_all | solution.py:280
  68.0 3.5 %collective-permute-start = (f32[528,128]{1,0:T(8,128)S(1)}, f32[528,128]{1,0:T(8,128)S(1)}, u32[]{:S(2)}, u32[]{:S(2)}) collective-permute-start(f32[528,128]{1,0:T(8,128)S(1)} %bitcast.22), channel_id=1, source_target_pairs={{0,8},{8,0},{16,24},{24,16},{32,40},{40,32},{48,56},{56,48},{64,72... | collective-permute-start | bytes 811016 | tf_op jit(solution)/shard_map/ppermute | solution.py:318
  71.5 3.0 %shard_map.77.w_ref = bf16[8,512,768]{2,1,0:T(8,128)(2,1)S(1)} custom-call(bf16[512,6144]{1,0:T(8,128)(2,1)} %w_hbm), custom_call_target="tpu_custom_call" | custom-call | bytes 12600000 | tf_op jit(solution)/shard_map/pallas_call | solution.py:49
  74.6 0.7 shard_map.76
  75.3 1.1 collective-permute-done.other_ref
  76.3 0.6 shard_map.78
  76.9 2.4 %all-gather.1 = f32[256,768]{1,0:T(8,128)S(1)} all-gather(f32[128,768]{1,0:T(8,128)S(1)} %get-tuple-element.37), channel_id=3, replica_groups={{0,1},{2,3},{4,5},{6,7},{8,9},{10,11},{12,13},{14,15},{16,17},{18,19},{..., dimensions={0}, use_global_device_ids=true | all-gather | bytes 1179648 | tf_op jit(solution)/shard_map/all_gather | solution.py:352
  79.3 5.7 %collective-permute-start.2 = (f32[128,768]{1,0:T(8,128)S(1)}, f32[128,768]{1,0:T(8,128)S(1)}, u32[]{:S(2)}, u32[]{:S(2)}) collective-permute-start(f32[128,768]{1,0:T(8,128)S(1)} %shard_map.79), channel_id=1, source_target_pairs={{0,2},{1,7},{2,4},{3,1},{4,6},{5,3},{6,0},{7,5},{8,10},{9,15},{10,... | collective-permute-start | bytes 1179656 | tf_op jit(solution)/shard_map/ppermute | solution.py:355
  85.1 0.4 shard_map.80
  85.4 2.4 %all-gather.2 = f32[256,768]{1,0:T(8,128)S(1)} all-gather(f32[128,768]{1,0:T(8,128)S(1)} %get-tuple-element.40), channel_id=4, replica_groups={{0,1},{2,3},{4,5},{6,7},{8,9},{10,11},{12,13},{14,15},{16,17},{18,19},{..., dimensions={0}, use_global_device_ids=true | all-gather | bytes 1179648 | tf_op jit(solution)/shard_map/all_gather | solution.py:359
  87.9 2.2 %collective-permute-start.1 = (f32[128,768]{1,0:T(8,128)S(1)}, f32[128,768]{1,0:T(8,128)S(1)}, u32[]{:S(2)}, u32[]{:S(2)}) collective-permute-start(f32[128,768]{1,0:T(8,128)S(1)} %shard_map.82), channel_id=1, source_target_pairs={{0,6},{1,3},{2,0},{3,5},{4,2},{5,7},{6,4},{7,1},{8,14},{9,11},{10,... | collective-permute-start | bytes 1179656 | tf_op jit(solution)/shard_map/ppermute | solution.py:362
  90.0 0.6 shard_map.81
  90.6 2.4 %all-gather.4 = f32[256,768]{1,0:T(8,128)S(1)} all-gather(f32[128,768]{1,0:T(8,128)S(1)} %get-tuple-element.47), channel_id=6, replica_groups={{0,1},{2,3},{4,5},{6,7},{8,9},{10,11},{12,13},{14,15},{16,17},{18,19},{..., dimensions={0}, use_global_device_ids=true | all-gather | bytes 1179648 | tf_op jit(solution)/shard_map/all_gather | solution.py:366
  93.0 6.9 %collective-permute-done.2.more_ref = f32[128,768]{1,0:T(8,128)S(1)} collective-permute-done((f32[128,768]{1,0:T(8,128)S(1)}, f32[128,768]{1,0:T(8,128)S(1)}, u32[]{:S(2)}, u32[]{:S(2)}) %collective-permute-start.2) | collective-permute-done | bytes 393248 | tf_op jit(solution)/shard_map/ppermute | solution.py:355
  99.9 0.1 shard_map.84
  100.0 6.5 %collective-permute-start.3 = (f32[128,768]{1,0:T(8,128)S(1)}, f32[128,768]{1,0:T(8,128)S(1)}, u32[]{:S(2)}, u32[]{:S(2)}) collective-permute-start(f32[128,768]{1,0:T(8,128)S(1)} %shard_map.84), channel_id=1, source_target_pairs={{0,2},{1,7},{2,4},{3,1},{4,6},{5,3},{6,0},{7,5},{8,10},{9,15},{10,... | collective-permute-start | bytes 1179656 | tf_op jit(solution)/shard_map/ppermute | solution.py:369
  106.5 2.4 %all-gather.3 = f32[256,768]{1,0:T(8,128)S(1)} all-gather(f32[128,768]{1,0:T(8,128)S(1)} %get-tuple-element.43), channel_id=5, replica_groups={{0,1},{2,3},{4,5},{6,7},{8,9},{10,11},{12,13},{14,15},{16,17},{18,19},{..., dimensions={0}, use_global_device_ids=true | all-gather | bytes 1179648 | tf_op jit(solution)/shard_map/all_gather | solution.py:367
  108.8 0.1 shard_map.83.one_ref
  108.9 5.8 %collective-permute-done.3.two_ref = f32[128,768]{1,0:T(8,128)S(1)} collective-permute-done((f32[128,768]{1,0:T(8,128)S(1)}, f32[128,768]{1,0:T(8,128)S(1)}, u32[]{:S(2)}, u32[]{:S(2)}) %collective-permute-start.3) | collective-permute-done | bytes 393248 | tf_op jit(solution)/shard_map/ppermute | solution.py:369
  114.7 0.7 shard_map.85
  (16 shorter events, 0.2 us)
Async XLA Ops:
  68.0 8.3 %collective-permute-start = (f32[528,128]{1,0:T(8,128)S(1)}, f32[528,128]{1,0:T(8,128)S(1)}, u32[]{:S(2)}, u32[]{:S(2)}) collective-permute-start(f32[528,128]{1,0:T(8,128)S(1)} %bitcast.22), channel_id=1, source_target_pairs={{0,8},{8,0},{16,24},{24,16},{32,40},{40,32},{48,56},{56,48},{64,72... | collective-permute-start | bytes 811016 | tf_op jit(solution)/shard_map/ppermute | solution.py:318
  71.5 3.1 %copy-start = (bf16[128,512]{1,0:T(8,128)(2,1)S(1)}, bf16[128,512]{1,0:T(8,128)(2,1)}, u32[]{:S(2)}) copy-start(bf16[128,512]{1,0:T(8,128)(2,1)} %query_ref.3) | copy-start | bytes 393220
  71.5 3.1 %copy-start.1 = (bf16[128,512]{1,0:T(8,128)(2,1)S(1)}, bf16[128,512]{1,0:T(8,128)(2,1)}, u32[]{:S(2)}) copy-start(bf16[128,512]{1,0:T(8,128)(2,1)} %key_ref.1) | copy-start | bytes 393220
  71.5 3.1 %copy-start.2 = (bf16[128,512]{1,0:T(8,128)(2,1)S(1)}, bf16[128,512]{1,0:T(8,128)(2,1)}, u32[]{:S(2)}) copy-start(bf16[128,512]{1,0:T(8,128)(2,1)} %value_ref.1) | copy-start | bytes 393220
  71.5 3.1 %copy-start.3 = (f32[4,128]{1,0:T(4,128)S(1)}, f32[4,128]{1,0:T(4,128)}, u32[]{:S(2)}) copy-start(f32[4,128]{1,0:T(4,128)} %log_ref.1) | copy-start | bytes 6148
  71.5 3.1 %copy-start.5 = (s32[128]{0:T(128)S(1)}, s32[128]{0:T(128)}, u32[]{:S(2)}) copy-start(s32[128]{0:T(128)} %param.11) | copy-start | bytes 1540
  71.5 4.8 %copy-start.4 = (f32[512]{0:T(512)S(1)}, f32[512]{0:T(512)}, u32[]{:S(2)}) copy-start(f32[512]{0:T(512)} %param.12) | copy-start | bytes 6148
  79.3 20.6 %collective-permute-start.2 = (f32[128,768]{1,0:T(8,128)S(1)}, f32[128,768]{1,0:T(8,128)S(1)}, u32[]{:S(2)}, u32[]{:S(2)}) collective-permute-start(f32[128,768]{1,0:T(8,128)S(1)} %shard_map.79), channel_id=1, source_target_pairs={{0,2},{1,7},{2,4},{3,1},{4,6},{5,3},{6,0},{7,5},{8,10},{9,15},{10,... | collective-permute-start | bytes 1179656 | tf_op jit(solution)/shard_map/ppermute | solution.py:355
  87.9 21.0 %collective-permute-start.1 = (f32[128,768]{1,0:T(8,128)S(1)}, f32[128,768]{1,0:T(8,128)S(1)}, u32[]{:S(2)}, u32[]{:S(2)}) collective-permute-start(f32[128,768]{1,0:T(8,128)S(1)} %shard_map.82), channel_id=1, source_target_pairs={{0,6},{1,3},{2,0},{3,5},{4,2},{5,7},{6,4},{7,1},{8,14},{9,11},{10,... | collective-permute-start | bytes 1179656 | tf_op jit(solution)/shard_map/ppermute | solution.py:362
  100.0 14.7 %collective-permute-start.3 = (f32[128,768]{1,0:T(8,128)S(1)}, f32[128,768]{1,0:T(8,128)S(1)}, u32[]{:S(2)}, u32[]{:S(2)}) collective-permute-start(f32[128,768]{1,0:T(8,128)S(1)} %shard_map.84), channel_id=1, source_target_pairs={{0,2},{1,7},{2,4},{3,1},{4,6},{5,3},{6,0},{7,5},{8,10},{9,15},{10,... | collective-permute-start | bytes 1179656 | tf_op jit(solution)/shard_map/ppermute | solution.py:369

commit v14 on v12

--- a/solution.py
+++ b/solution.py
@@ -250,25 +250,25 @@
         out_ref[...] = jnp.dot(normed, w_ref[block_of(place, 3 - 2 * whose, whose)], preferred_element_type=F32)
 
 
-def rest_kernel(place_ref, normed_ref, w_ref, ahead_send_ref, ahead_ref, own_send_ref, own_ref):
+def rest_kernel(place_ref, normed_ref, w_ref, send_ref, mine_ref):
     place = place_ref[0]
     core = place & 1
     normed = normed_ref[...]
-    for out_ref, far, whose in (
-        (ahead_send_ref, 3 - 2 * core, 1 - core),
-        (ahead_ref, 1 + 2 * core, core),
-        (own_send_ref, 0, 1 - core),
-        (own_ref, 0, core),
-    ):
-        out_ref[...] = jnp.dot(normed, w_ref[block_of(place, far, whose)], preferred_element_type=F32)
+    for out_ref, whose in ((send_ref, 1 - core), (mine_ref, core)):
+        for slot, far in enumerate((1 + 2 * whose, 0)):
+            out_ref[slot] = jnp.dot(normed, w_ref[block_of(place, far, whose)], preferred_element_type=F32)
 
 
 def core_sum_kernel(place_ref, mine_ref, both_ref, out_ref):
     out_ref[...] = mine_ref[...] + both_ref[1 - (place_ref[0] & 1)]
 
 
-def three_kernel(place_ref, mine_ref, both_ref, more_ref, out_ref):
-    out_ref[...] = mine_ref[...] + both_ref[1 - (place_ref[0] & 1)] + more_ref[...]
+def ahead_kernel(mine_ref, got_ref, more_ref, out_ref):
+    out_ref[...] = mine_ref[0] + got_ref[0] + more_ref[...]
+
+
+def own_kernel(mine_ref, got_ref, more_ref, out_ref):
+    out_ref[...] = mine_ref[1] + got_ref[1] + more_ref[...]
 
 
 def final_kernel(one_ref, two_ref, out_ref):
@@ -357,17 +357,14 @@
         behind_kernel, [block, block], (place, normed, staged), scalars=1, flops=200_000_000, moved=2_500_000
     )
     behind_both = lax.all_gather(behind_send, "tp", axis_index_groups=CORE_PAIRS)
-    behind_both, normed = lax.optimization_barrier((behind_both, normed))
     behind = core_sum(behind_mine, behind_both)
     one = lax.ppermute(behind, "tp", BACK)
-    ahead_send, ahead_mine, own_send, own_mine = call(
-        rest_kernel, [block] * 4, (place, normed, staged), scalars=1, flops=400_000_000, moved=5_000_000
-    )
-    ahead_both = lax.all_gather(ahead_send, "tp", axis_index_groups=CORE_PAIRS)
-    own_both = lax.all_gather(own_send, "tp", axis_index_groups=CORE_PAIRS)
-    (passed,) = call(three_kernel, [block], (place, ahead_mine, ahead_both, ahead_got), scalars=1)
+    two_blocks = ((2, EVENTS, COLS), F32)
+    rest_send, rest_mine = call(rest_kernel, [two_blocks, two_blocks], (place, normed, staged), scalars=1)
+    rest_got = lax.ppermute(rest_send, "tp", CORE_SWAP)
+    (passed,) = call(ahead_kernel, [block], (rest_mine, rest_got, ahead_got))
     two = lax.ppermute(passed, "tp", ONWARD)
-    (own_and_one,) = call(three_kernel, [block], (place, own_mine, own_both, one), scalars=1, moved=1_600_000)
+    (own_and_one,) = call(own_kernel, [block], (rest_mine, rest_got, one), moved=1_600_000)
     (out,) = call(final_kernel, [((EVENTS, COLS), BF16)], (own_and_one, two), moved=1_000_000)
     return out
 

time: 116 us -> 118 us (1.017)
  the two profiles are of different devices: /device:TPU:16 before, /device:TPU:1 now
where the time goes in v14:
time: 118 us; the launch traced here: 117 us
  blocking collectives  73.3 us (62%)
  starting transfers between devices  22.2 us (19%)
  waiting for transfers between devices  13.2 us (11%)
  Pallas kernels  7.8 us (7%)
    all_to_all x2, blocking collectives, exchange_pieces(): pieces = lax.all_to_all(pieces, 'ctx', 0, 0, axis_index_groups=SIDE_GROUPS)  56.7 us
    ppermute x1, waiting for transfers between devices, body(): one = lax.ppermute(behind, 'tp', BACK)  9.15 us
    pallas_call x13, Pallas kernels, call(): pl.pallas_call(kernel, out_shape=shapes, in_specs=specs, out_specs=[pl.Bl...  7.8 us
    all_gather x1, blocking collectives, body(): lax.all_gather(opposite_send, 'tp', axis_index_groups=CORE_PAIRS)  7.68 us
    ppermute x1, starting transfers between devices, body(): two = lax.ppermute(passed, 'tp', ONWARD)  7.04 us
    all_gather x1, blocking collectives, body(): both = lax.all_gather(sent, 'ctx', axis_index_groups=SIDE_PAIRS)  6.6 us
    ppermute x1, starting transfers between devices, body(): ahead_got = lax.ppermute(opposite, 'tp', ONWARD)  5.88 us
    ppermute x1, starting transfers between devices, body(): one = lax.ppermute(behind, 'tp', BACK)  3.81 us
  transfers between devices with their start and end apart: 5, of which 4 were waited for; matrix products, arithmetic and copies ran while one was open for 0% of the time, Pallas kernels for 4%

profile of v14, /device:TPU:1, one launch (start us, length us, event | category | flops | bytes accessed | tf_op | source)
XLA Modules:
  0.0 116.8 jit_solution(3451159062717705911)
XLA Ops:
  0.0 1.5 %shard_map.73 = (f32[520,128]{1,0:T(8,128)S(1)}, f32[512,128]{1,0:T(8,128)S(1)}, f32[4,128]{1,0:T(4,128)S(1)}) custom-call(s32[1]{0:T(128)} %bitcast.1.side_ref, bf16[128,512]{1,0:T(8,128)(2,1)} %key_ref.1, bf16[128,512]{1,0:T(8,128)(2,1)} %value_ref.1, f32[4,128]{1,0:T(4,128)} %log_ref.1, s32[1,128]{1,0:T(1,128)} %bitcast.21), custom_call_target="tpu_custom_call" | custom-call | flops 70000000 | bytes 900000 | tf_op jit(solution)/shard_map/pallas_call | solution.py:49
  1.5 6.6 %all-gather = f32[1040,128]{1,0:T(8,128)S(1)} all-gather(f32[520,128]{1,0:T(8,128)S(1)} %get-tuple-element.23), channel_id=2, replica_groups={{0,8},{16,24},{32,40},{48,56},{64,72},{80,88},{96,104},{112,120},{128,1..., dimensions={0}, use_global_device_ids=true | all-gather | bytes 798720 | tf_op jit(solution)/shard_map/all_gather | solution.py:309
  8.1 35.7 %all_to_all.10 = f32[48,3,4,128]{3,2,1,0:T(4,128)S(1)} all-to-all(f32[48,3,4,128]{3,2,1,0:T(4,128)S(1)} %bitcast.16), channel_id=1, replica_groups={{0,192,384,576,16,208,400,592,32,224,416,608,48,240,432,624,64,256,448,..., dimensions={0} | all-to-all | bytes 589824 | tf_op jit(solution)/shard_map/all_to_all | solution.py:280
  43.8 0.1 shard_map.75
  43.9 21.0 %all_to_all.11 = f32[48,11,1,128]{3,2,1,0:T(1,128)S(1)} all-to-all(f32[48,11,1,128]{3,2,1,0:T(1,128)S(1)} %bitcast.17), channel_id=1, replica_groups={{0,192,384,576,16,208,400,592,32,224,416,608,48,240,432,624,64,256,448,..., dimensions={0} | all-to-all | bytes 540672 | tf_op jit(solution)/shard_map/all_to_all | solution.py:280
  64.9 3.2 %collective-permute-start = (f32[528,128]{1,0:T(8,128)S(1)}, f32[528,128]{1,0:T(8,128)S(1)}, u32[]{:S(2)}, u32[]{:S(2)}) collective-permute-start(f32[528,128]{1,0:T(8,128)S(1)} %bitcast.18), channel_id=1, source_target_pairs={{0,8},{8,0},{16,24},{24,16},{32,40},{40,32},{48,56},{56,48},{64,72... | collective-permute-start | bytes 811016 | tf_op jit(solution)/shard_map/ppermute | solution.py:318
  68.2 3.0 %shard_map.77.w_ref = bf16[8,512,768]{2,1,0:T(8,128)(2,1)S(1)} custom-call(bf16[512,6144]{1,0:T(8,128)(2,1)} %w_hbm), custom_call_target="tpu_custom_call" | custom-call | bytes 12600000 | tf_op jit(solution)/shard_map/pallas_call | solution.py:49
  71.3 0.7 shard_map.76
  71.9 0.2 collective-permute-done.other_ref
  72.1 0.6 shard_map.78
  72.7 7.7 %all-gather.1 = f32[256,768]{1,0:T(8,128)S(1)} all-gather(f32[128,768]{1,0:T(8,128)S(1)} %get-tuple-element.33), channel_id=3, replica_groups={{0,1},{2,3},{4,5},{6,7},{8,9},{10,11},{12,13},{14,15},{16,17},{18,19},{..., dimensions={0}, use_global_device_ids=true | all-gather | bytes 1179648 | tf_op jit(solution)/shard_map/all_gather | solution.py:352
  80.5 0.6 shard_map.80
  81.1 2.3 %collective-permute-start.1 = (f32[2,128,768]{2,1,0:T(8,128)S(1)}, f32[2,128,768]{2,1,0:T(8,128)S(1)}, u32[]{:S(2)}, u32[]{:S(2)}) collective-permute-start(f32[2,128,768]{2,1,0:T(8,128)S(1)} %get-tuple-element.37), channel_id=1, source_target_pairs={{0,1},{1,0},{2,3},{3,2},{4,5},{5,4},{6,7},{7,6},{8,9},{9,8},{10,11... | collective-permute-start | bytes 2359304 | tf_op jit(solution)/shard_map/ppermute | solution.py:364
  83.4 5.9 %collective-permute-start.3 = (f32[128,768]{1,0:T(8,128)S(1)}, f32[128,768]{1,0:T(8,128)S(1)}, u32[]{:S(2)}, u32[]{:S(2)}) collective-permute-start(f32[128,768]{1,0:T(8,128)S(1)} %shard_map.79), channel_id=1, source_target_pairs={{0,2},{1,7},{2,4},{3,1},{4,6},{5,3},{6,0},{7,5},{8,10},{9,15},{10,... | collective-permute-start | bytes 1179656 | tf_op jit(solution)/shard_map/ppermute | solution.py:355
  89.2 0.4 shard_map.81
  89.6 2.4 %all-gather.2 = f32[256,768]{1,0:T(8,128)S(1)} all-gather(f32[128,768]{1,0:T(8,128)S(1)} %get-tuple-element.39), channel_id=4, replica_groups={{0,1},{2,3},{4,5},{6,7},{8,9},{10,11},{12,13},{14,15},{16,17},{18,19},{..., dimensions={0}, use_global_device_ids=true | all-gather | bytes 1179648 | tf_op jit(solution)/shard_map/all_gather | solution.py:359
  92.0 3.8 %collective-permute-start.2 = (f32[128,768]{1,0:T(8,128)S(1)}, f32[128,768]{1,0:T(8,128)S(1)}, u32[]{:S(2)}, u32[]{:S(2)}) collective-permute-start(f32[128,768]{1,0:T(8,128)S(1)} %shard_map.82), channel_id=1, source_target_pairs={{0,6},{1,3},{2,0},{3,5},{4,2},{5,7},{6,4},{7,1},{8,14},{9,11},{10,... | collective-permute-start | bytes 1179656 | tf_op jit(solution)/shard_map/ppermute | solution.py:361
  95.9 3.2 %collective-permute-done.3.more_ref = f32[128,768]{1,0:T(8,128)S(1)} collective-permute-done((f32[128,768]{1,0:T(8,128)S(1)}, f32[128,768]{1,0:T(8,128)S(1)}, u32[]{:S(2)}, u32[]{:S(2)}) %collective-permute-start.3) | collective-permute-done | bytes 393248 | tf_op jit(solution)/shard_map/ppermute | solution.py:355
  99.1 0.1 shard_map.84
  99.2 7.0 %collective-permute-start.4 = (f32[128,768]{1,0:T(8,128)S(1)}, f32[128,768]{1,0:T(8,128)S(1)}, u32[]{:S(2)}, u32[]{:S(2)}) collective-permute-start(f32[128,768]{1,0:T(8,128)S(1)} %shard_map.84), channel_id=1, source_target_pairs={{0,2},{1,7},{2,4},{3,1},{4,6},{5,3},{6,0},{7,5},{8,10},{9,15},{10,... | collective-permute-start | bytes 1179656 | tf_op jit(solution)/shard_map/ppermute | solution.py:366
  106.2 9.2 %collective-permute-done.2.more_ref = f32[128,768]{1,0:T(8,128)S(1)} collective-permute-done((f32[128,768]{1,0:T(8,128)S(1)}, f32[128,768]{1,0:T(8,128)S(1)}, u32[]{:S(2)}, u32[]{:S(2)}) %collective-permute-start.2) | collective-permute-done | bytes 393248 | tf_op jit(solution)/shard_map/ppermute | solution.py:361
  115.4 0.1 shard_map.83.one_ref
  115.4 0.7 collective-permute-done.4.two_ref
  116.1 0.7 shard_map.85
  (16 shorter events, 0.2 us)
Async XLA Ops:
  64.9 7.2 %collective-permute-start = (f32[528,128]{1,0:T(8,128)S(1)}, f32[528,128]{1,0:T(8,128)S(1)}, u32[]{:S(2)}, u32[]{:S(2)}) collective-permute-start(f32[528,128]{1,0:T(8,128)S(1)} %bitcast.18), channel_id=1, source_target_pairs={{0,8},{8,0},{16,24},{24,16},{32,40},{40,32},{48,56},{56,48},{64,72... | collective-permute-start | bytes 811016 | tf_op jit(solution)/shard_map/ppermute | solution.py:318
  68.1 3.1 %copy-start = (bf16[128,512]{1,0:T(8,128)(2,1)S(1)}, bf16[128,512]{1,0:T(8,128)(2,1)}, u32[]{:S(2)}) copy-start(bf16[128,512]{1,0:T(8,128)(2,1)} %query_ref.3) | copy-start | bytes 393220
  68.2 3.1 %copy-start.1 = (bf16[128,512]{1,0:T(8,128)(2,1)S(1)}, bf16[128,512]{1,0:T(8,128)(2,1)}, u32[]{:S(2)}) copy-start(bf16[128,512]{1,0:T(8,128)(2,1)} %key_ref.1) | copy-start | bytes 393220
  68.2 3.1 %copy-start.2 = (bf16[128,512]{1,0:T(8,128)(2,1)S(1)}, bf16[128,512]{1,0:T(8,128)(2,1)}, u32[]{:S(2)}) copy-start(bf16[128,512]{1,0:T(8,128)(2,1)} %value_ref.1) | copy-start | bytes 393220
  68.2 3.1 %copy-start.3 = (f32[4,128]{1,0:T(4,128)S(1)}, f32[4,128]{1,0:T(4,128)}, u32[]{:S(2)}) copy-start(f32[4,128]{1,0:T(4,128)} %log_ref.1) | copy-start | bytes 6148
  68.2 3.1 %copy-start.5 = (s32[128]{0:T(128)S(1)}, s32[128]{0:T(128)}, u32[]{:S(2)}) copy-start(s32[128]{0:T(128)} %param.11) | copy-start | bytes 1540
  68.2 3.9 %copy-start.4 = (f32[512]{0:T(512)S(1)}, f32[512]{0:T(512)}, u32[]{:S(2)}) copy-start(f32[512]{0:T(512)} %param.12) | copy-start | bytes 6148
  81.1 18.0 %collective-permute-start.1 = (f32[2,128,768]{2,1,0:T(8,128)S(1)}, f32[2,128,768]{2,1,0:T(8,128)S(1)}, u32[]{:S(2)}, u32[]{:S(2)}) collective-permute-start(f32[2,128,768]{2,1,0:T(8,128)S(1)} %get-tuple-element.37), channel_id=1, source_target_pairs={{0,1},{1,0},{2,3},{3,2},{4,5},{5,4},{6,7},{7,6},{8,9},{9,8},{10,11... | collective-permute-start | bytes 2359304 | tf_op jit(solution)/shard_map/ppermute | solution.py:364
  83.4 15.7 %collective-permute-start.3 = (f32[128,768]{1,0:T(8,128)S(1)}, f32[128,768]{1,0:T(8,128)S(1)}, u32[]{:S(2)}, u32[]{:S(2)}) collective-permute-start(f32[128,768]{1,0:T(8,128)S(1)} %shard_map.79), channel_id=1, source_target_pairs={{0,2},{1,7},{2,4},{3,1},{4,6},{5,3},{6,0},{7,5},{8,10},{9,15},{10,... | collective-permute-start | bytes 1179656 | tf_op jit(solution)/shard_map/ppermute | solution.py:355
  92.0 23.3 %collective-permute-start.2 = (f32[128,768]{1,0:T(8,128)S(1)}, f32[128,768]{1,0:T(8,128)S(1)}, u32[]{:S(2)}, u32[]{:S(2)}) collective-permute-start(f32[128,768]{1,0:T(8,128)S(1)} %shard_map.82), channel_id=1, source_target_pairs={{0,6},{1,3},{2,0},{3,5},{4,2},{5,7},{6,4},{7,1},{8,14},{9,11},{10,... | collective-permute-start | bytes 1179656 | tf_op jit(solution)/shard_map/ppermute | solution.py:361
  99.2 16.9 %collective-permute-start.4 = (f32[128,768]{1,0:T(8,128)S(1)}, f32[128,768]{1,0:T(8,128)S(1)}, u32[]{:S(2)}, u32[]{:S(2)}) collective-permute-start(f32[128,768]{1,0:T(8,128)S(1)} %shard_map.84), channel_id=1, source_target_pairs={{0,2},{1,7},{2,4},{3,1},{4,6},{5,3},{6,0},{7,5},{8,10},{9,15},{10,... | collective-permute-start | bytes 1179656 | tf_op jit(solution)/shard_map/ppermute | solution.py:366

commit v15 on v12

--- a/solution.py
+++ b/solution.py
@@ -359,12 +359,13 @@
     behind_both = lax.all_gather(behind_send, "tp", axis_index_groups=CORE_PAIRS)
     behind_both, normed = lax.optimization_barrier((behind_both, normed))
     behind = core_sum(behind_mine, behind_both)
-    one = lax.ppermute(behind, "tp", BACK)
     ahead_send, ahead_mine, own_send, own_mine = call(
         rest_kernel, [block] * 4, (place, normed, staged), scalars=1, flops=400_000_000, moved=5_000_000
     )
     ahead_both = lax.all_gather(ahead_send, "tp", axis_index_groups=CORE_PAIRS)
     own_both = lax.all_gather(own_send, "tp", axis_index_groups=CORE_PAIRS)
+    behind, ahead_both = lax.optimization_barrier((behind, ahead_both))
+    one = lax.ppermute(behind, "tp", BACK)
     (passed,) = call(three_kernel, [block], (place, ahead_mine, ahead_both, ahead_got), scalars=1)
     two = lax.ppermute(passed, "tp", ONWARD)
     (own_and_one,) = call(three_kernel, [block], (place, own_mine, own_both, one), scalars=1, moved=1_600_000)

time: 116 us -> 116 us (level)
  the two profiles are of different devices: /device:TPU:16 before, /device:TPU:1 now
where the time goes in v15:
time: 116 us
  blocking collectives  81.2 us (70%)
  starting transfers between devices  18.6 us (16%)
  waiting for transfers between devices  8.02 us (7%)
  Pallas kernels  7.77 us (7%)
    all_to_all x2, blocking collectives, exchange_pieces(): pieces = lax.all_to_all(pieces, 'ctx', 0, 0, axis_index_groups=SIDE_GROUPS)  56.7 us
    pallas_call x13, Pallas kernels, call(): pl.pallas_call(kernel, out_shape=shapes, in_specs=specs, out_specs=[pl.Bl...  7.77 us
    all_gather x1, blocking collectives, body(): lax.all_gather(opposite_send, 'tp', axis_index_groups=CORE_PAIRS)  7.68 us
    all_gather x1, blocking collectives, body(): both = lax.all_gather(sent, 'ctx', axis_index_groups=SIDE_PAIRS)  6.6 us
    ppermute x1, waiting for transfers between devices, body(): one = lax.ppermute(behind, 'tp', BACK)  6.43 us
    ppermute x1, starting transfers between devices, body(): ahead_got = lax.ppermute(opposite, 'tp', ONWARD)  5.89 us
    ppermute x1, starting transfers between devices, body(): two = lax.ppermute(passed, 'tp', ONWARD)  5.5 us
    all_gather x1, blocking collectives, body(): own_both = lax.all_gather(own_send, 'tp', axis_index_groups=CORE_PAIRS)  5.43 us
  transfers between devices with their start and end apart: 4, of which 3 were waited for; matrix products, arithmetic and copies ran while one was open for 0% of the time, Pallas kernels for 4%

profile of v15, /device:TPU:1, one launch (start us, length us, event | category | flops | bytes accessed | tf_op | source)
XLA Modules:
  0.0 115.8 jit_solution(15632221149916107798)
XLA Ops:
  0.0 1.5 %shard_map.73 = (f32[520,128]{1,0:T(8,128)S(1)}, f32[512,128]{1,0:T(8,128)S(1)}, f32[4,128]{1,0:T(4,128)S(1)}) custom-call(s32[1]{0:T(128)} %bitcast.1.side_ref, bf16[128,512]{1,0:T(8,128)(2,1)} %key_ref.1, bf16[128,512]{1,0:T(8,128)(2,1)} %value_ref.1, f32[4,128]{1,0:T(4,128)} %log_ref.1, s32[1,128]{1,0:T(1,128)} %bitcast.25), custom_call_target="tpu_custom_call" | custom-call | flops 70000000 | bytes 900000 | tf_op jit(solution)/shard_map/pallas_call | solution.py:49
  1.5 6.6 %all-gather = f32[1040,128]{1,0:T(8,128)S(1)} all-gather(f32[520,128]{1,0:T(8,128)S(1)} %get-tuple-element.29), channel_id=2, replica_groups={{0,8},{16,24},{32,40},{48,56},{64,72},{80,88},{96,104},{112,120},{128,1..., dimensions={0}, use_global_device_ids=true | all-gather | bytes 798720 | tf_op jit(solution)/shard_map/all_gather | solution.py:309
  8.1 35.7 %all_to_all.10 = f32[48,3,4,128]{3,2,1,0:T(4,128)S(1)} all-to-all(f32[48,3,4,128]{3,2,1,0:T(4,128)S(1)} %bitcast.20), channel_id=1, replica_groups={{0,192,384,576,16,208,400,592,32,224,416,608,48,240,432,624,64,256,448,..., dimensions={0} | all-to-all | bytes 589824 | tf_op jit(solution)/shard_map/all_to_all | solution.py:280
  43.8 0.1 shard_map.75
  43.9 21.0 %all_to_all.11 = f32[48,11,1,128]{3,2,1,0:T(1,128)S(1)} all-to-all(f32[48,11,1,128]{3,2,1,0:T(1,128)S(1)} %bitcast.21), channel_id=1, replica_groups={{0,192,384,576,16,208,400,592,32,224,416,608,48,240,432,624,64,256,448,..., dimensions={0} | all-to-all | bytes 540672 | tf_op jit(solution)/shard_map/all_to_all | solution.py:280
  64.9 3.2 %collective-permute-start = (f32[528,128]{1,0:T(8,128)S(1)}, f32[528,128]{1,0:T(8,128)S(1)}, u32[]{:S(2)}, u32[]{:S(2)}) collective-permute-start(f32[528,128]{1,0:T(8,128)S(1)} %bitcast.22), channel_id=1, source_target_pairs={{0,8},{8,0},{16,24},{24,16},{32,40},{40,32},{48,56},{56,48},{64,72... | collective-permute-start | bytes 811016 | tf_op jit(solution)/shard_map/ppermute | solution.py:318
  68.2 3.0 %shard_map.77.w_ref = bf16[8,512,768]{2,1,0:T(8,128)(2,1)S(1)} custom-call(bf16[512,6144]{1,0:T(8,128)(2,1)} %w_hbm), custom_call_target="tpu_custom_call" | custom-call | bytes 12600000 | tf_op jit(solution)/shard_map/pallas_call | solution.py:49
  71.3 0.7 shard_map.76
  71.9 0.2 collective-permute-done.other_ref
  72.1 0.6 shard_map.78
  72.7 7.7 %all-gather.1 = f32[256,768]{1,0:T(8,128)S(1)} all-gather(f32[128,768]{1,0:T(8,128)S(1)} %get-tuple-element.39), channel_id=3, replica_groups={{0,1},{2,3},{4,5},{6,7},{8,9},{10,11},{12,13},{14,15},{16,17},{18,19},{..., dimensions={0}, use_global_device_ids=true | all-gather | bytes 1179648 | tf_op jit(solution)/shard_map/all_gather | solution.py:352
  80.5 0.4 shard_map.80
  80.9 5.9 %collective-permute-start.2 = (f32[128,768]{1,0:T(8,128)S(1)}, f32[128,768]{1,0:T(8,128)S(1)}, u32[]{:S(2)}, u32[]{:S(2)}) collective-permute-start(f32[128,768]{1,0:T(8,128)S(1)} %shard_map.79), channel_id=1, source_target_pairs={{0,2},{1,7},{2,4},{3,1},{4,6},{5,3},{6,0},{7,5},{8,10},{9,15},{10,... | collective-permute-start | bytes 1179656 | tf_op jit(solution)/shard_map/ppermute | solution.py:355
  86.8 2.4 %all-gather.2 = f32[256,768]{1,0:T(8,128)S(1)} all-gather(f32[128,768]{1,0:T(8,128)S(1)} %get-tuple-element.42), channel_id=4, replica_groups={{0,1},{2,3},{4,5},{6,7},{8,9},{10,11},{12,13},{14,15},{16,17},{18,19},{..., dimensions={0}, use_global_device_ids=true | all-gather | bytes 1179648 | tf_op jit(solution)/shard_map/all_gather | solution.py:359
  89.2 0.6 shard_map.81
  89.8 2.4 %all-gather.4 = f32[256,768]{1,0:T(8,128)S(1)} all-gather(f32[128,768]{1,0:T(8,128)S(1)} %get-tuple-element.48), channel_id=6, replica_groups={{0,1},{2,3},{4,5},{6,7},{8,9},{10,11},{12,13},{14,15},{16,17},{18,19},{..., dimensions={0}, use_global_device_ids=true | all-gather | bytes 1179648 | tf_op jit(solution)/shard_map/all_gather | solution.py:365
  92.1 4.0 %collective-permute-start.1 = (f32[128,768]{1,0:T(8,128)S(1)}, f32[128,768]{1,0:T(8,128)S(1)}, u32[]{:S(2)}, u32[]{:S(2)}) collective-permute-start(f32[128,768]{1,0:T(8,128)S(1)} %shard_map.82), channel_id=1, source_target_pairs={{0,6},{1,3},{2,0},{3,5},{4,2},{5,7},{6,4},{7,1},{8,14},{9,11},{10,... | collective-permute-start | bytes 1179656 | tf_op jit(solution)/shard_map/ppermute | solution.py:368
  96.2 0.1 shard_map.84
  96.3 5.5 %collective-permute-start.3 = (f32[128,768]{1,0:T(8,128)S(1)}, f32[128,768]{1,0:T(8,128)S(1)}, u32[]{:S(2)}, u32[]{:S(2)}) collective-permute-start(f32[128,768]{1,0:T(8,128)S(1)} %shard_map.84), channel_id=1, source_target_pairs={{0,2},{1,7},{2,4},{3,1},{4,6},{5,3},{6,0},{7,5},{8,10},{9,15},{10,... | collective-permute-start | bytes 1179656 | tf_op jit(solution)/shard_map/ppermute | solution.py:370
  101.8 5.4 %all-gather.3 = f32[256,768]{1,0:T(8,128)S(1)} all-gather(f32[128,768]{1,0:T(8,128)S(1)} %get-tuple-element.45), channel_id=5, replica_groups={{0,1},{2,3},{4,5},{6,7},{8,9},{10,11},{12,13},{14,15},{16,17},{18,19},{..., dimensions={0}, use_global_device_ids=true | all-gather | bytes 1179648 | tf_op jit(solution)/shard_map/all_gather | solution.py:366
  107.2 6.4 %collective-permute-done.1.more_ref = f32[128,768]{1,0:T(8,128)S(1)} collective-permute-done((f32[128,768]{1,0:T(8,128)S(1)}, f32[128,768]{1,0:T(8,128)S(1)}, u32[]{:S(2)}, u32[]{:S(2)}) %collective-permute-start.1) | collective-permute-done | bytes 393248 | tf_op jit(solution)/shard_map/ppermute | solution.py:368
  113.6 0.1 shard_map.83.one_ref
  113.7 1.4 %collective-permute-done.3.two_ref = f32[128,768]{1,0:T(8,128)S(1)} collective-permute-done((f32[128,768]{1,0:T(8,128)S(1)}, f32[128,768]{1,0:T(8,128)S(1)}, u32[]{:S(2)}, u32[]{:S(2)}) %collective-permute-start.3) | collective-permute-done | bytes 393248 | tf_op jit(solution)/shard_map/ppermute | solution.py:370
  115.1 0.7 shard_map.85
  (16 shorter events, 0.2 us)
Async XLA Ops:
  64.9 7.2 %collective-permute-start = (f32[528,128]{1,0:T(8,128)S(1)}, f32[528,128]{1,0:T(8,128)S(1)}, u32[]{:S(2)}, u32[]{:S(2)}) collective-permute-start(f32[528,128]{1,0:T(8,128)S(1)} %bitcast.22), channel_id=1, source_target_pairs={{0,8},{8,0},{16,24},{24,16},{32,40},{40,32},{48,56},{56,48},{64,72... | collective-permute-start | bytes 811016 | tf_op jit(solution)/shard_map/ppermute | solution.py:318
  68.1 3.1 %copy-start = (bf16[128,512]{1,0:T(8,128)(2,1)S(1)}, bf16[128,512]{1,0:T(8,128)(2,1)}, u32[]{:S(2)}) copy-start(bf16[128,512]{1,0:T(8,128)(2,1)} %query_ref.3) | copy-start | bytes 393220
  68.2 3.1 %copy-start.1 = (bf16[128,512]{1,0:T(8,128)(2,1)S(1)}, bf16[128,512]{1,0:T(8,128)(2,1)}, u32[]{:S(2)}) copy-start(bf16[128,512]{1,0:T(8,128)(2,1)} %key_ref.1) | copy-start | bytes 393220
  68.2 3.1 %copy-start.2 = (bf16[128,512]{1,0:T(8,128)(2,1)S(1)}, bf16[128,512]{1,0:T(8,128)(2,1)}, u32[]{:S(2)}) copy-start(bf16[128,512]{1,0:T(8,128)(2,1)} %value_ref.1) | copy-start | bytes 393220
  68.2 3.1 %copy-start.3 = (f32[4,128]{1,0:T(4,128)S(1)}, f32[4,128]{1,0:T(4,128)}, u32[]{:S(2)}) copy-start(f32[4,128]{1,0:T(4,128)} %log_ref.1) | copy-start | bytes 6148
  68.2 3.1 %copy-start.5 = (s32[128]{0:T(128)S(1)}, s32[128]{0:T(128)}, u32[]{:S(2)}) copy-start(s32[128]{0:T(128)} %param.11) | copy-start | bytes 1540
  68.2 3.9 %copy-start.4 = (f32[512]{0:T(512)S(1)}, f32[512]{0:T(512)}, u32[]{:S(2)}) copy-start(f32[512]{0:T(512)} %param.12) | copy-start | bytes 6148
  80.9 15.3 %collective-permute-start.2 = (f32[128,768]{1,0:T(8,128)S(1)}, f32[128,768]{1,0:T(8,128)S(1)}, u32[]{:S(2)}, u32[]{:S(2)}) collective-permute-start(f32[128,768]{1,0:T(8,128)S(1)} %shard_map.79), channel_id=1, source_target_pairs={{0,2},{1,7},{2,4},{3,1},{4,6},{5,3},{6,0},{7,5},{8,10},{9,15},{10,... | collective-permute-start | bytes 1179656 | tf_op jit(solution)/shard_map/ppermute | solution.py:355
  92.1 21.5 %collective-permute-start.1 = (f32[128,768]{1,0:T(8,128)S(1)}, f32[128,768]{1,0:T(8,128)S(1)}, u32[]{:S(2)}, u32[]{:S(2)}) collective-permute-start(f32[128,768]{1,0:T(8,128)S(1)} %shard_map.82), channel_id=1, source_target_pairs={{0,6},{1,3},{2,0},{3,5},{4,2},{5,7},{6,4},{7,1},{8,14},{9,11},{10,... | collective-permute-start | bytes 1179656 | tf_op jit(solution)/shard_map/ppermute | solution.py:368
  96.3 18.8 %collective-permute-start.3 = (f32[128,768]{1,0:T(8,128)S(1)}, f32[128,768]{1,0:T(8,128)S(1)}, u32[]{:S(2)}, u32[]{:S(2)}) collective-permute-start(f32[128,768]{1,0:T(8,128)S(1)} %shard_map.84), channel_id=1, source_target_pairs={{0,2},{1,7},{2,4},{3,1},{4,6},{5,3},{6,0},{7,5},{8,10},{9,15},{10,... | collective-permute-start | bytes 1179656 | tf_op jit(solution)/shard_map/ppermute | solution.py:370
